TPU v7x, 32 devices: a whole 2x2x4 slice. The times are simulated.
32 devices in a mesh: fsdp: 8 (over y, x, core), tp: 4 (over z).
Axes of the slice: x: 2, y: 2, z: 4, core: 2. Of those that a mesh axis runs over, the one named last changes fastest.
Arguments:
- tokens: bfloat16 [8192, 2048], P(('fsdp', 'tp')), may hold values from -6 to 6
- lengths: int32 [8, 4], P('fsdp'), may hold values from 1 to 512, 1024 in all within a row
- ln_gains: float32 [2, 2048], P(None, ('fsdp', 'tp')), may hold values from 0.1 to 1.9
- ln_shifts: float32 [2, 2048], P(None, ('fsdp', 'tp')), may hold values from -1.5 to 1.5
- w_qkv: bfloat16 [2048, 3, 2048], P('fsdp', None, 'tp'), may hold values from -0.125 to 0.125
- b_qkv: bfloat16 [3, 2048], P(None, ('tp', 'fsdp')), may hold values from -3 to 3
- w_out: bfloat16 [2048, 2048], P('tp', 'fsdp'), may hold values from -0.5 to 0.5
- w_gate_up: bfloat16 [2048, 2, 5632], P('fsdp', None, 'tp'), may hold values from -0.125 to 0.125
- w_down: bfloat16 [5632, 2048], P('tp', 'fsdp'), may hold values from -0.078125 to 0.078125
- cotangent: bfloat16 [8192, 2048], P(('fsdp', 'tp')), may hold values from -6 to 6
Outputs:
- out_tokens: bfloat16 [8192, 2048], P(('fsdp', 'tp'))
- grad_tokens: float32 [8192, 2048], P(('fsdp', 'tp'))
- grad_ln_gains: float32 [2, 2048], P(None, ('fsdp', 'tp'))
- grad_ln_shifts: float32 [2, 2048], P(None, ('fsdp', 'tp'))
- grad_w_qkv: float32 [2048, 3, 2048], P('fsdp', None, 'tp')
- grad_b_qkv: float32 [3, 2048], P(None, ('tp', 'fsdp'))
- grad_w_out: float32 [2048, 2048], P('tp', 'fsdp')
- grad_w_gate_up: float32 [2048, 2, 5632], P('fsdp', None, 'tp')
- grad_w_down: float32 [5632, 2048], P('tp', 'fsdp')
Inputs may be any that keep to these rules, and one draw needn't show every extreme that they name: In each row the lengths sum to 1024 and the largest is exactly 512.
All inputs are finite; a program needn't handle non-finite values.
Results may differ from a plain program's by a relative error of at most 0.03.
Values may be sent and summed in bfloat16 or wider, within the bound.
A program may use at most 192 MiB of HBM per device.

v0:
```python
import jax
import jax.numpy as jnp
from jax import lax
from jax.sharding import PartitionSpec as P

HEAD = 64
ROT = 16


NORM_EPS = 1e-05


def layer_norm(values, gain_row, shift_row):
    average = jnp.mean(values, axis=-1, keepdims=True)
    centred = values - average
    variance = jnp.mean(centred * centred, axis=-1, keepdims=True)
    return centred * lax.rsqrt(variance + NORM_EPS) * gain_row + shift_row


def swiglu(gate_vals, up_vals):
    return jax.nn.silu(gate_vals) * up_vals


def doc_layout(length_row, seq_len):
    doc_ends = jnp.cumsum(length_row)
    columns = jnp.arange(seq_len, dtype=jnp.int32)
    passed = (doc_ends[None, :] <= columns[:, None]).astype(jnp.int32)
    seg_ids = jnp.sum(passed, axis=1)
    starts = jnp.sum(passed * length_row[None, :], axis=1)
    return (seg_ids, columns - starts)


def rotate(values, places):
    half_rot = ROT // 2
    frequency = 10000.0 ** (-2.0 * jnp.arange(half_rot, dtype=jnp.float32) / ROT)
    angles = places.astype(jnp.float32)[:, None] * frequency[None, :]
    cosine = jnp.cos(angles)[:, None, :]
    sine_vals = jnp.sin(angles)[:, None, :]
    lower_half = values[..., :half_rot]
    upper_half = values[..., half_rot:ROT]
    return jnp.concatenate(
        [
            lower_half * cosine - upper_half * sine_vals,
            upper_half * cosine + lower_half * sine_vals,
            values[..., ROT:],
        ],
        axis=-1,
    )


def visible(seg_ids, first_row, block_rows):
    row_segs = lax.dynamic_slice_in_dim(seg_ids, first_row, block_rows, 0)
    row_places = first_row + jnp.arange(block_rows, dtype=jnp.int32)
    columns = jnp.arange(seg_ids.shape[0], dtype=jnp.int32)
    return (row_segs[:, None] == seg_ids[None, :]) & (columns[None, :] <= row_places[:, None])


def contract_rows(left_vals, right_vals):
    return lax.dot_general(
        left_vals, right_vals, (((0,), (0,)), ((), ())), preferred_element_type=jnp.float32
    )


def times_transposed(left_vals, right_vals):
    return lax.dot_general(
        left_vals, right_vals, (((1,), (1,)), ((), ())), preferred_element_type=jnp.float32
    )


def gather_rows(values):
    return lax.all_gather(values, "tp", axis=0, tiled=True)


def reduce_forward(values):
    return lax.psum_scatter(
        values.astype(jnp.bfloat16), "tp", scatter_dimension=0, tiled=True
    ).astype(jnp.float32)


def reduce_back(values):
    return lax.psum_scatter(
        values.astype(jnp.bfloat16), "tp", scatter_dimension=0, tiled=True
    ).astype(jnp.float32)


def attend_forward(queries, key_vals, value_rows, seg_ids, scale):
    seq_len = queries.shape[0]
    block_rows = min(512, seq_len)

    def one_block(carried, block_index):
        first_row = block_index * block_rows
        rows_q = lax.dynamic_slice_in_dim(queries, first_row, block_rows, 0)
        scores = (
            jnp.einsum("qhe,khe->hqk", rows_q, key_vals, preferred_element_type=jnp.float32) * scale
        )
        scores = jnp.where(visible(seg_ids, first_row, block_rows)[None], scores, -1e30)
        row_max = jnp.max(scores, axis=-1, keepdims=True)
        weights = jnp.exp(scores - row_max)
        row_sum = jnp.sum(weights, axis=-1, keepdims=True)
        weights_low = (weights / row_sum).astype(jnp.bfloat16)
        block_out = jnp.einsum(
            "hqk,khe->qhe", weights_low, value_rows, preferred_element_type=jnp.float32
        )
        return (carried, (block_out, (row_max + jnp.log(row_sum))[..., 0]))

    _, (outputs, logsum) = lax.scan(
        one_block, None, jnp.arange(seq_len // block_rows, dtype=jnp.int32)
    )
    return (outputs.reshape(queries.shape), logsum)


def attend_backward(queries, key_vals, value_rows, grad_outs, logsum, seg_ids, scale):
    seq_len = queries.shape[0]
    block_rows = min(512, seq_len)

    def one_block(carried, inputs):
        grad_key_sum, grad_value_sum = carried
        block_index, block_logsum = inputs
        first_row = block_index * block_rows
        rows_q = lax.dynamic_slice_in_dim(queries, first_row, block_rows, 0)
        grad_rows = lax.dynamic_slice_in_dim(grad_outs, first_row, block_rows, 0)
        scores = (
            jnp.einsum("qhe,khe->hqk", rows_q, key_vals, preferred_element_type=jnp.float32) * scale
        )
        scores = jnp.where(visible(seg_ids, first_row, block_rows)[None], scores, -1e30)
        weights = jnp.exp(scores - block_logsum[..., None])
        weights_low = weights.astype(jnp.bfloat16)
        grad_weights = jnp.einsum(
            "qhe,khe->hqk", grad_rows, value_rows, preferred_element_type=jnp.float32
        )
        inner = jnp.sum(weights * grad_weights, axis=-1, keepdims=True)
        grad_scores = (weights * (grad_weights - inner)).astype(jnp.bfloat16)
        grad_query_rows = (
            jnp.einsum("hqk,khe->qhe", grad_scores, key_vals, preferred_element_type=jnp.float32)
            * scale
        )
        grad_key_sum = (
            grad_key_sum
            + jnp.einsum("hqk,qhe->khe", grad_scores, rows_q, preferred_element_type=jnp.float32)
            * scale
        )
        grad_value_sum = grad_value_sum + jnp.einsum(
            "hqk,qhe->khe", weights_low, grad_rows, preferred_element_type=jnp.float32
        )
        return ((grad_key_sum, grad_value_sum), grad_query_rows)

    zeros_init = jnp.zeros(queries.shape, jnp.float32)
    block_ids = jnp.arange(seq_len // block_rows, dtype=jnp.int32)
    (grad_keys, grad_values), grad_queries = lax.scan(
        one_block, (zeros_init, zeros_init), (block_ids, logsum)
    )
    return (grad_queries.reshape(queries.shape), grad_keys, grad_values)


def local(tokens, lengths, ln_gains, ln_shifts, w_qkv, b_qkv, w_out, w_gate_up, w_down, cotangent):
    slab_rows, model_width = tokens.shape
    seq_len = slab_rows * lax.axis_size("tp")
    seg_ids, places = doc_layout(lengths[0], seq_len)
    gains_all, shifts_all = (
        lax.all_gather(ln_gains, ("fsdp", "tp"), axis=1, tiled=True),
        lax.all_gather(ln_shifts, ("fsdp", "tp"), axis=1, tiled=True),
    )
    q_weight, q_bias, o_weight = (
        lax.all_gather(w_qkv, "fsdp", axis=0, tiled=True),
        lax.all_gather(b_qkv, "fsdp", axis=1, tiled=True),
        lax.all_gather(w_out, "fsdp", axis=1, tiled=True),
    )
    gu_weight, down_weight = (
        lax.all_gather(w_gate_up, "fsdp", axis=0, tiled=True),
        lax.all_gather(w_down, "fsdp", axis=1, tiled=True),
    )
    local_width = q_weight.shape[2]
    head_count = local_width // HEAD
    hidden_width = gu_weight.shape[2]
    scale = HEAD ** (-0.5)
    token_rows = tokens.astype(jnp.float32)
    normed_one = layer_norm(token_rows, gains_all[0], shifts_all[0])
    full_one = gather_rows(normed_one.astype(jnp.bfloat16))
    projected = jnp.dot(
        full_one, q_weight.reshape(model_width, 3 * local_width), preferred_element_type=jnp.float32
    )
    projected = projected.reshape(seq_len, 3, local_width) + q_bias.astype(jnp.float32)[None]
    query_raw = projected[:, 0].reshape(seq_len, head_count, HEAD)
    key_raw = projected[:, 1].reshape(seq_len, head_count, HEAD)
    queries = rotate(query_raw, places).astype(jnp.bfloat16)
    key_vals = rotate(key_raw, places).astype(jnp.bfloat16)
    value_rows = projected[:, 2].reshape(seq_len, head_count, HEAD).astype(jnp.bfloat16)
    attended, logsum = attend_forward(queries, key_vals, value_rows, seg_ids, scale)
    attended_low = attended.reshape(seq_len, local_width).astype(jnp.bfloat16)
    attn_rows = reduce_forward(jnp.dot(attended_low, o_weight, preferred_element_type=jnp.float32))
    residual = token_rows + attn_rows
    normed_two = layer_norm(residual, gains_all[1], shifts_all[1])
    full_two = gather_rows(normed_two.astype(jnp.bfloat16))
    gate_up = jnp.dot(
        full_two,
        gu_weight.reshape(model_width, 2 * hidden_width),
        preferred_element_type=jnp.float32,
    )
    gate_up = gate_up.reshape(seq_len, 2, hidden_width)
    hidden_low = swiglu(gate_up[:, 0], gate_up[:, 1]).astype(jnp.bfloat16)
    branch = reduce_forward(jnp.dot(hidden_low, down_weight, preferred_element_type=jnp.float32))
    result = (residual + branch).astype(jnp.bfloat16)
    grad_out = cotangent.astype(jnp.float32)
    grad_branch = gather_rows(cotangent)
    grad_down = contract_rows(hidden_low, grad_branch)
    grad_hidden = times_transposed(grad_branch, down_weight)
    _, swiglu_pull = jax.vjp(swiglu, gate_up[:, 0], gate_up[:, 1])
    grad_gate, grad_up = swiglu_pull(grad_hidden)
    grad_gate_up = (
        jnp.stack([grad_gate, grad_up], axis=1)
        .astype(jnp.bfloat16)
        .reshape(seq_len, 2 * hidden_width)
    )
    grad_gu = contract_rows(full_two, grad_gate_up).reshape(model_width, 2, hidden_width)
    grad_normed_two = reduce_back(
        times_transposed(grad_gate_up, gu_weight.reshape(model_width, 2 * hidden_width))
    )
    _, second_pull = jax.vjp(layer_norm, residual, gains_all[1], shifts_all[1])
    grad_resid_norm, grad_gain_two, grad_shift_two = second_pull(grad_normed_two)
    grad_residual = grad_out + grad_resid_norm
    grad_attn = gather_rows(grad_residual.astype(jnp.bfloat16))
    grad_o = contract_rows(attended_low, grad_attn)
    grad_attended = (
        times_transposed(grad_attn, o_weight)
        .astype(jnp.bfloat16)
        .reshape(seq_len, head_count, HEAD)
    )
    grad_queries, grad_keys, grad_values = attend_backward(
        queries, key_vals, value_rows, grad_attended, logsum, seg_ids, scale
    )
    _, rotate_pull = jax.vjp(lambda values: rotate(values, places), query_raw)
    grad_query_raw = rotate_pull(grad_queries)[0]
    grad_key_raw = rotate_pull(grad_keys)[0]
    grad_projected = jnp.stack(
        [
            grad_query_raw.reshape(seq_len, local_width),
            grad_key_raw.reshape(seq_len, local_width),
            grad_values.reshape(seq_len, local_width),
        ],
        axis=1,
    ).astype(jnp.bfloat16)
    grad_bias = jnp.sum(grad_projected, axis=0, dtype=jnp.float32)
    grad_projected = grad_projected.reshape(seq_len, 3 * local_width)
    grad_qkv = contract_rows(full_one, grad_projected).reshape(model_width, 3, local_width)
    grad_normed_one = reduce_back(
        times_transposed(grad_projected, q_weight.reshape(model_width, 3 * local_width))
    )
    _, first_pull = jax.vjp(layer_norm, token_rows, gains_all[0], shifts_all[0])
    grad_token_norm, grad_gain_one, grad_shift_one = first_pull(grad_normed_one)
    grad_tokens = grad_residual + grad_token_norm
    gain_share, shift_share = (
        lax.psum_scatter(
            jnp.stack([grad_gain_one, grad_gain_two]),
            ("fsdp", "tp"),
            scatter_dimension=1,
            tiled=True,
        ),
        lax.psum_scatter(
            jnp.stack([grad_shift_one, grad_shift_two]),
            ("fsdp", "tp"),
            scatter_dimension=1,
            tiled=True,
        ),
    )
    qkv_share, bias_share, out_share, gu_share, down_share = (
        lax.psum_scatter(
            grad_qkv.astype(jnp.bfloat16), "fsdp", scatter_dimension=0, tiled=True
        ).astype(jnp.float32),
        lax.psum_scatter(
            grad_bias.astype(jnp.bfloat16), "fsdp", scatter_dimension=1, tiled=True
        ).astype(jnp.float32),
        lax.psum_scatter(
            grad_o.astype(jnp.bfloat16), "fsdp", scatter_dimension=1, tiled=True
        ).astype(jnp.float32),
        lax.psum_scatter(
            grad_gu.astype(jnp.bfloat16), "fsdp", scatter_dimension=0, tiled=True
        ).astype(jnp.float32),
        lax.psum_scatter(
            grad_down.astype(jnp.bfloat16), "fsdp", scatter_dimension=1, tiled=True
        ).astype(jnp.float32),
    )
    return (
        result,
        grad_tokens,
        gain_share,
        shift_share,
        qkv_share,
        bias_share,
        out_share,
        gu_share,
        down_share,
    )


def solution(mesh):
    placed = (
        P(("fsdp", "tp"), None),
        P("fsdp", None),
        P(None, ("fsdp", "tp")),
        P(None, ("fsdp", "tp")),
        P("fsdp", None, "tp"),
        P(None, ("tp", "fsdp")),
        P("tp", "fsdp"),
        P("fsdp", None, "tp"),
        P("tp", "fsdp"),
        P(("fsdp", "tp"), None),
    )
    return jax.shard_map(
        local,
        mesh=mesh,
        in_specs=placed,
        out_specs=(
            P(("fsdp", "tp"), None),
            P(("fsdp", "tp"), None),
            P(None, ("fsdp", "tp")),
            P(None, ("fsdp", "tp")),
            P("fsdp", None, "tp"),
            P(None, ("tp", "fsdp")),
            P("tp", "fsdp"),
            P("fsdp", None, "tp"),
            P("tp", "fsdp"),
        ),
        check_vma=False,
    )
```

profile of v0, /device:TPU:0, one launch (start us, length us, event | category | flops | bytes accessed | tf_op | source)
XLA Modules:
  0.0 1755.6 jit_solution(5223027610106076300)
XLA Ops:
  8.0 70.1 %all-gather = f32[32,64,2]{1,2,0:T(2,128)S(1)} all-gather(f32[1,64,2]{1,2,0:T(2,128)} %bitcast.222), channel_id=1, replica_groups=mesh['fsdp'=8,'tp'=4] {'fsdp','tp'}, dimensions={0}, use_global_device_ids=true | all-gather | bytes 16896 | tf_op jit(solution)/shard_map/all_gather | solution.py:160
  78.2 63.8 %all-gather.1 = f32[32,64,2]{1,2,0:T(2,128)S(1)} all-gather(f32[1,64,2]{1,2,0:T(2,128)} %bitcast.223), channel_id=1, replica_groups=mesh['fsdp'=8,'tp'=4] {'fsdp','tp'}, dimensions={0}, use_global_device_ids=true | all-gather | bytes 16896 | tf_op jit(solution)/shard_map/all_gather | solution.py:161
  148.7 7.9 all-gather.2
  157.2 8.8 copy.76
  166.0 60.7 %all-gather.12.cloned.1.call-done = bf16[1024,2048]{1,0:T(8,128)(2,1)} async-done(((bf16[256,2048]{1,0:T(8,128)(2,1)}), bf16[1024,2048]{1,0:T(8,128)(2,1)}) %all-gather.12.cloned.1.call-update) | async-done | bytes 4194320 | tf_op jit(solution)/shard_map/all_gather | solution.py:71
  226.8 10.1 broadcast_add_fusion
  239.2 45.2 %while.27 = (s32[]{:T(128)}, bf16[2,512,8,64]{1,3,2,0:T(8,128)(2,1)}, f32[2,8,512]{2,1,0:T(8,128)S(1)}, s32[2]{0:T(128)S(1)}, s32[1024]{0:T(1024)S(1)}, /*index=...) while((s32[]{:T(128)}, ...), condition=%wide.region_8.9_spmd, body=%wide.region_5.8_spmd.sunk | while | flops 1125642752 | bytes 64633084 | solution.py:106
  288.3 6.2 convolution_convert_fusion.4
  297.3 72.8 %reduce-scatter.18.cloned.1.call-done = bf16[256,2048]{1,0:T(8,128)(2,1)} async-done(((bf16[1024,2048]{1,0:T(8,128)(2,1)}), bf16[256,2048]{1,0:T(8,128)(2,1)}) %reduce-scatter.18.cloned.1.call-update) | async-done | bytes 1048592 | tf_op jit(solution)/shard_map/reduce_scatter | solution.py:75
  376.6 64.2 %all-gather.20.cloned.1.call-done = bf16[2048,2,1408]{2,0,1:T(8,128)(2,1)} async-done(((bf16[256,2,1408]{2,0,1:T(8,128)(2,1)}), bf16[2048,2,1408]{2,0,1:T(8,128)(2,1)}) %all-gather.20.cloned.1.call-update) | async-done | bytes 11534352 | tf_op jit(solution)/shard_map/all_gather | solution.py:169
  440.8 15.5 copy.80
  456.2 67.4 %all-gather.18.cloned.1.call-done = bf16[1024,2048]{1,0:T(8,128)(2,1)} async-done(((bf16[256,2048]{1,0:T(8,128)(2,1)}), bf16[1024,2048]{1,0:T(8,128)(2,1)}) %all-gather.18.cloned.1.call-update) | async-done | bytes 4194320 | tf_op jit(solution)/shard_map/all_gather | solution.py:71
  523.6 18.9 %fusion.26 = f32[1024,2,1408]{2,0,1:T(8,128)} fusion(bf16[2048,2,1408]{0,2,1:T(8,128)(2,1)} %copy.80, bf16[1024,2048]{1,0:T(8,128)(2,1)} %all-gather.18.cloned.1.call-done), kind=kOutput, calls=%fused_computation.40 | convolution fusion | flops 11811160064 | bytes 27262976 | tf_op jit(solution)/shard_map/dot_general | solution.py:194
  542.5 62.1 %all-gather.24.cloned.1.call-done = bf16[1024,2048]{1,0:T(8,128)(2,1)} async-done(((bf16[256,2048]{1,0:T(8,128)(2,1)}), bf16[1024,2048]{1,0:T(8,128)(2,1)}) %all-gather.24.cloned.1.call-update) | async-done | bytes 4194320 | tf_op jit(solution)/shard_map/all_gather | solution.py:71
  604.6 44.9 %all-gather.22.cloned.1.call-done = bf16[1408,2048]{1,0:T(8,128)(2,1)} async-done(((bf16[1408,256]{1,0:T(8,128)(2,1)}), bf16[1408,2048]{1,0:T(8,128)(2,1)}) %all-gather.22.cloned.1.call-update) | async-done | bytes 5767184 | tf_op jit(solution)/shard_map/all_gather | solution.py:170
  649.6 14.3 fusion.32
  666.4 16.3 bitcast_convert_fusion.1
  682.7 5.6 multiply_convert_fusion.1
  689.9 10.8 convolution_convert_fusion.3
  700.8 58.8 %reduce-scatter.22.cloned.1.call-done = bf16[256,2048]{1,0:T(8,128)(2,1)} async-done(((bf16[1024,2048]{1,0:T(8,128)(2,1)}), bf16[256,2048]{1,0:T(8,128)(2,1)}) %reduce-scatter.22.cloned.1.call-update) | async-done | bytes 1048592 | tf_op jit(solution)/shard_map/reduce_scatter | solution.py:81
  762.4 76.7 %reduce-scatter.20.cloned.1.call-done = bf16[256,2048]{1,0:T(8,128)(2,1)} async-done(((bf16[1024,2048]{1,0:T(8,128)(2,1)}), bf16[256,2048]{1,0:T(8,128)(2,1)}) %reduce-scatter.20.cloned.1.call-update) | async-done | bytes 1048592 | tf_op jit(solution)/shard_map/reduce_scatter | solution.py:75
  845.3 81.4 %all-gather.26.cloned.1.call-done = bf16[1024,2048]{1,0:T(8,128)(2,1)} async-done(((bf16[256,2048]{1,0:T(8,128)(2,1)}), bf16[1024,2048]{1,0:T(8,128)(2,1)}) %all-gather.26.cloned.1.call-update) | async-done | bytes 4194320 | tf_op jit(solution)/shard_map/all_gather | solution.py:71
  926.7 5.5 convolution_convert_fusion.6
  932.2 142.0 %while.28 = (s32[]{:T(128)}, f32[1024,8,64]{0,2,1:T(8,128)}, f32[1024,8,64]{0,2,1:T(8,128)}, f32[2,512,8,64]{1,0,3,2:T(2,128)}, s32[2]{0:T(128)S(1)}, /*index=5*...) while((s32[]{:T(128)}, f32[1024,8,64]{0,2,1:T(8,128)}, ...), condition=%wide.region_18.19_spmd.clone, body=%wide.region_16.18_spmd.clone.sunk | while | flops 2726556160 | bytes 166951280 | solution.py:149
  939.4 11.5 multiply_reduce_fusion.3
  950.9 9.3 multiply_convert_fusion.3
  960.2 6.1 fusion.127
  968.4 19.7 %dynamic_update_slice.19 = f32[2,512,8,64]{1,0,3,2:T(2,128)} dynamic-update-slice(f32[2,512,8,64]{1,0,3,2:T(2,128)} %get-tuple-element.455, f32[1,512,8,64]{1,0,3,2:T(1,128)} %copy.123, s32[]{:T(128)} %get-tuple-element.452, s32[]{:T(128)} %constant.75.clone.1..sunk.1, s32[]{:T(128)} %constant.75.clone.1..sunk.1, s32[]{:T(128)} %constant.75.clone.1..sunk.1) | dynamic-update-slice | bytes 2097156 | tf_op jit(solution)/shard_map/while/body/jit(dynamic_update_index_in_dim)/dynamic_update_slice | solution.py:106
  993.5 9.5 bitcast_add_fusion.5
  1010.0 11.5 multiply_reduce_fusion.3
  1021.5 9.3 multiply_convert_fusion.3
  1030.8 6.1 fusion.127
  1039.0 19.7 %dynamic_update_slice.19 = f32[2,512,8,64]{1,0,3,2:T(2,128)} dynamic-update-slice(f32[2,512,8,64]{1,0,3,2:T(2,128)} %get-tuple-element.455, f32[1,512,8,64]{1,0,3,2:T(1,128)} %copy.123, s32[]{:T(128)} %get-tuple-element.452, s32[]{:T(128)} %constant.75.clone.1..sunk.1, s32[]{:T(128)} %constant.75.clone.1..sunk.1, s32[]{:T(128)} %constant.75.clone.1..sunk.1) | dynamic-update-slice | bytes 2097156 | tf_op jit(solution)/shard_map/while/body/jit(dynamic_update_index_in_dim)/dynamic_update_slice | solution.py:106
  1064.1 10.1 bitcast_add_fusion.5
  1090.3 11.0 bitcast_convert_fusion
  1103.1 10.7 convolution_convert_fusion.1
  1120.6 8.3 copy.87
  1129.8 19.6 %convolution_convert_fusion = bf16[2048,2,1408]{2,0,1:T(8,128)(2,1)} fusion(bf16[1024,2,1408]{0,2,1:T(8,128)(2,1)} %copy.87, bf16[1024,2048]{1,0:T(8,128)(2,1)} %all-gather.18.cloned.1.call-done), kind=kOutput, calls=%fused_computation.42 | convolution fusion | flops 11816927232 | bytes 21495808 | tf_op jit(solution)/shard_map/dot_general | solution.py:59
  1150.6 5.9 convolution_convert_fusion.5
  1161.4 15.4 reduce-scatter.24.cloned.1.call-done
  1182.8 11.7 convolution_convert_fusion.2
  1194.5 45.3 %reduce-scatter.32.cloned.1.call-done = bf16[1408,256]{1,0:T(8,128)(2,1)} async-done(((bf16[1408,2048]{1,0:T(8,128)(2,1)}), bf16[1408,256]{1,0:T(8,128)(2,1)}) %reduce-scatter.32.cloned.1.call-update) | async-done | bytes 720912 | tf_op jit(solution)/shard_map/reduce_scatter | solution.py:278
  1242.1 34.8 %reduce-scatter.38.cloned.1.call-done = bf16[64,3]{1,0:T(8,128)(2,1)} async-done(((bf16[512,3]{1,0:T(8,128)(2,1)}), bf16[64,3]{1,0:T(8,128)(2,1)}) %reduce-scatter.38.cloned.1.call-update) | async-done | bytes 400
  1278.3 88.8 %reduce-scatter.30.cloned.1.call-done = bf16[256,2,1408]{2,0,1:T(8,128)(2,1)} async-done(((bf16[2048,2,1408]{2,0,1:T(8,128)(2,1)}), bf16[256,2,1408]{2,0,1:T(8,128)(2,1)}) %reduce-scatter.30.cloned.1.call-update) | async-done | bytes 1441808 | tf_op jit(solution)/shard_map/reduce_scatter | solution.py:275
  1371.5 40.5 %reduce-scatter.28.cloned.1.call-done = bf16[512,256]{1,0:T(8,128)(2,1)} async-done(((bf16[512,2048]{1,0:T(8,128)(2,1)}), bf16[512,256]{1,0:T(8,128)(2,1)}) %reduce-scatter.28.cloned.1.call-update) | async-done | bytes 262160 | tf_op jit(solution)/shard_map/reduce_scatter | solution.py:272
  1417.6 132.4 %reduce-scatter.36.cloned.1.call-done = f32[64,2]{1,0:T(8,128)} async-done(((f32[2048,2]{1,0:T(8,128)}), f32[64,2]{1,0:T(8,128)}) %reduce-scatter.36.cloned.1.call-update) | async-done | bytes 528
  1551.4 133.2 %reduce-scatter.34.cloned.1.call-done = f32[64,2]{1,0:T(8,128)} async-done(((f32[2048,2]{1,0:T(8,128)}), f32[64,2]{1,0:T(8,128)}) %reduce-scatter.34.cloned.1.call-update) | async-done | bytes 528
  1686.0 60.4 %reduce-scatter.26.cloned.1.call-done = bf16[256,3,512]{2,0,1:T(8,128)(2,1)} async-done(((bf16[2048,3,512]{2,0,1:T(8,128)(2,1)}), bf16[256,3,512]{2,0,1:T(8,128)(2,1)}) %reduce-scatter.26.cloned.1.call-update) | async-done | bytes 786448 | tf_op jit(solution)/shard_map/reduce_scatter | solution.py:266
  (257 shorter events, 152.7 us)
Async XLA Ops:
  7.2 139.2 %copy-start.3 = (bf16[256,2048]{1,0:T(8,128)(2,1)S(1)}, bf16[256,2048]{1,0:T(8,128)(2,1)}, u32[]{:S(2)}) copy-start(bf16[256,2048]{1,0:T(8,128)(2,1)} %param.14) | copy-start | bytes 3145732
  7.2 150.0 %all-gather.14.cloned.1.call-start = ((), (), s32[]{:S(2)}) async-start(), calls=%async_computation.12 | async-start | bytes 7077888 | tf_op jit(solution)/shard_map/all_gather | solution.py:164
  7.9 218.8 %all-gather.12.cloned.1.call-start = ((), (), s32[]{:S(2)}) async-start(), calls=%async_computation.11 | async-start | bytes 5242880 | tf_op jit(solution)/shard_map/all_gather | solution.py:71
  78.2 70.5 %copy-start.46 = (bf16[3,64]{1,0:T(4,128)(2,1)S(1)}, bf16[3,64]{1,0:T(4,128)(2,1)}, u32[]{:S(2)}) copy-start(bf16[3,64]{1,0:T(4,128)(2,1)} %param.19) | copy-start | bytes 1156
  141.9 14.7 copy-start.47
  143.5 22.5 %copy-start.35 = (f32[256]{0:T(256)}, f32[256]{0:T(256)S(1)}, u32[]{:S(2)}) copy-start(f32[256]{0:T(256)S(1)} %broadcast_multiply_fusion.1) | copy-start | bytes 3076
  145.2 20.9 %copy-start.40 = (f32[256]{0:T(256)}, f32[256]{0:T(256)S(1)}, u32[]{:S(2)}) copy-start(f32[256]{0:T(256)S(1)} %fusion.63) | copy-start | bytes 3076
  147.9 140.5 %all-gather.16.cloned.1.call-start = ((), (), s32[]{:S(2)}) async-start(), calls=%async_computation.13 | async-start | bytes 2359296 | tf_op jit(solution)/shard_map/all_gather | solution.py:166
  148.6 221.4 %reduce-scatter.18.cloned.1.call-start = ((), (), s32[]{:S(2)}) async-start(), calls=%async_computation.14 | async-start | bytes 5242880 | tf_op jit(solution)/shard_map/reduce_scatter | solution.py:75
  157.1 80.7 %copy-start.26 = (f32[1024,8]{0,1:T(8,128)}, f32[1024,8]{0,1:T(8,128)S(1)}, u32[]{:S(2)}) copy-start(f32[1024,8]{0,1:T(8,128)S(1)} %get-tuple-element.273) | copy-start | bytes 98308
  157.2 80.7 %copy-start.28 = (f32[1024,8]{0,1:T(8,128)}, f32[1024,8]{0,1:T(8,128)S(1)}, u32[]{:S(2)}) copy-start(f32[1024,8]{0,1:T(8,128)S(1)} %get-tuple-element.274) | copy-start | bytes 98308
  284.4 10.2 copy-start.6
  294.6 75.4 %copy-start.4 = (bf16[256,2048]{1,0:T(8,128)(2,1)S(1)}, bf16[256,2048]{1,0:T(8,128)(2,1)}, u32[]{:S(2)}) copy-start(bf16[256,2048]{1,0:T(8,128)(2,1)} %param.14) | copy-start | bytes 3145732
  294.6 146.2 %all-gather.20.cloned.1.call-start = ((), (), s32[]{:S(2)}) async-start(), calls=%async_computation.16 | async-start | bytes 12976128 | tf_op jit(solution)/shard_map/all_gather | solution.py:169
  297.2 76.3 %copy-start.34 = (f32[1,2048]{1,0:T(1,128)S(1)}, f32[1,2048]{1,0:T(1,128)}, u32[]{:S(2)}) copy-start(f32[1,2048]{1,0:T(1,128)} %get-tuple-element.269) | copy-start | bytes 24580
  297.2 76.3 %copy-start.39 = (f32[1,2048]{1,0:T(1,128)S(1)}, f32[1,2048]{1,0:T(1,128)}, u32[]{:S(2)}) copy-start(f32[1,2048]{1,0:T(1,128)} %get-tuple-element.271) | copy-start | bytes 24580
  297.2 226.4 %all-gather.18.cloned.1.call-start = ((), (), s32[]{:S(2)}) async-start(), calls=%async_computation.15 | async-start | bytes 5242880 | tf_op jit(solution)/shard_map/all_gather | solution.py:71
  375.0 229.6 %all-gather.24.cloned.1.call-start = ((), (), s32[]{:S(2)}) async-start(), calls=%async_computation.19 | async-start | bytes 5242880 | tf_op jit(solution)/shard_map/all_gather | solution.py:71
  375.8 273.8 %all-gather.22.cloned.1.call-start = ((), (), s32[]{:S(2)}) async-start(), calls=%async_computation.17 | async-start | bytes 6488064 | tf_op jit(solution)/shard_map/all_gather | solution.py:170
  376.5 383.1 %reduce-scatter.22.cloned.1.call-start = ((), (), s32[]{:S(2)}) async-start(), calls=%async_computation.20 | async-start | bytes 5242880 | tf_op jit(solution)/shard_map/reduce_scatter | solution.py:81
  682.7 156.3 %reduce-scatter.20.cloned.1.call-start = ((), (), s32[]{:S(2)}) async-start(), calls=%async_computation.18 | async-start | bytes 5242880 | tf_op jit(solution)/shard_map/reduce_scatter | solution.py:75
  700.7 225.9 %all-gather.26.cloned.1.call-start = ((), (), s32[]{:S(2)}) async-start(), calls=%async_computation.21 | async-start | bytes 5242880 | tf_op jit(solution)/shard_map/all_gather | solution.py:71
  839.0 4.9 copy-start.12
  842.6 84.1 %copy-start.48 = (bf16[512,2048]{1,0:T(8,128)(2,1)S(1)}, bf16[512,2048]{1,0:T(8,128)(2,1)}, u32[]{:S(2)}) copy-start(bf16[512,2048]{1,0:T(8,128)(2,1)} %all-gather.16.cloned.1.call-done) | copy-start | bytes 6291460
  845.2 331.5 %reduce-scatter.24.cloned.1.call-start = ((), (), s32[]{:S(2)}) async-start(), calls=%async_computation.22 | async-start | bytes 5242880 | tf_op jit(solution)/shard_map/reduce_scatter | solution.py:81
  966.3 21.7 %copy-start = (f32[1024,8,64]{0,2,1:T(8,128)S(1)}, f32[1024,8,64]{0,2,1:T(8,128)}, u32[]{:S(2)}) copy-start(f32[1024,8,64]{0,2,1:T(8,128)} %get-tuple-element.453) | copy-start | bytes 6291460 | tf_op jit(solution)/shard_map/while
  988.0 5.4 copy-start.7
  993.4 9.5 copy-start.1
  1036.9 21.7 %copy-start = (f32[1024,8,64]{0,2,1:T(8,128)S(1)}, f32[1024,8,64]{0,2,1:T(8,128)}, u32[]{:S(2)}) copy-start(f32[1024,8,64]{0,2,1:T(8,128)} %get-tuple-element.453) | copy-start | bytes 6291460 | tf_op jit(solution)/shard_map/while
  1058.6 5.4 copy-start.7
  1064.0 10.2 copy-start.1
  1074.2 4.4 copy-start.29
  1101.3 138.5 %reduce-scatter.32.cloned.1.call-start = ((), (), s32[]{:S(2)}) async-start(), calls=%async_computation.26 | async-start | bytes 6488064 | tf_op jit(solution)/shard_map/reduce_scatter | solution.py:278
  1113.8 163.0 %reduce-scatter.38.cloned.1.call-start = ((), (), s32[]{:S(2)}) async-start(), calls=%async_computation.29 | async-start | bytes 147456
  1129.7 237.4 %reduce-scatter.30.cloned.1.call-start = ((), (), s32[]{:S(2)}) async-start(), calls=%async_computation.25 | async-start | bytes 12976128 | tf_op jit(solution)/shard_map/reduce_scatter | solution.py:275
  1149.4 262.6 %reduce-scatter.28.cloned.1.call-start = ((), (), s32[]{:S(2)}) async-start(), calls=%async_computation.24 | async-start | bytes 2359296 | tf_op jit(solution)/shard_map/reduce_scatter | solution.py:272
  1156.5 20.2 %copy-start.5 = (bf16[256,2048]{1,0:T(8,128)(2,1)S(1)}, bf16[256,2048]{1,0:T(8,128)(2,1)}, u32[]{:S(2)}) copy-start(bf16[256,2048]{1,0:T(8,128)(2,1)} %param.14) | copy-start | bytes 3145732
  1156.5 20.2 %copy-start.33 = (f32[1,2048]{1,0:T(1,128)S(1)}, f32[1,2048]{1,0:T(1,128)}, u32[]{:S(2)}) copy-start(f32[1,2048]{1,0:T(1,128)} %copy-done.32) | copy-start | bytes 24580
  1156.5 20.2 %copy-start.36 = (f32[256]{0:T(256)S(1)}, f32[256]{0:T(256)}, u32[]{:S(2)}) copy-start(f32[256]{0:T(256)} %copy-done.35) | copy-start | bytes 3076
  1156.6 22.2 %copy-start.38 = (f32[2048]{0:T(1024)S(1)}, f32[2048]{0:T(1024)}, u32[]{:S(2)}) copy-start(f32[2048]{0:T(1024)} %get-tuple-element.203) | copy-start | bytes 24580
  1156.6 393.4 %reduce-scatter.36.cloned.1.call-start = ((), (), s32[]{:S(2)}) async-start(), calls=%async_computation.28 | async-start | bytes 1081344
  1161.4 18.8 %copy-start.45 = (f32[256]{0:T(256)S(1)}, f32[256]{0:T(256)}, u32[]{:S(2)}) copy-start(f32[256]{0:T(256)} %copy-done.44) | copy-start | bytes 3076
  1161.4 18.9 %copy-start.41 = (f32[256]{0:T(256)S(1)}, f32[256]{0:T(256)}, u32[]{:S(2)}) copy-start(f32[256]{0:T(256)} %copy-done.40) | copy-start | bytes 3076
  1161.4 19.9 %copy-start.37 = (f32[2048]{0:T(1024)S(1)}, f32[2048]{0:T(1024)}, u32[]{:S(2)}) copy-start(f32[2048]{0:T(1024)} %get-tuple-element.197) | copy-start | bytes 24580
  1180.2 504.4 %reduce-scatter.34.cloned.1.call-start = ((), (), s32[]{:S(2)}) async-start(), calls=%async_computation.27 | async-start | bytes 1081344
  1182.7 563.7 %reduce-scatter.26.cloned.1.call-start = ((), (), s32[]{:S(2)}) async-start(), calls=%async_computation.23 | async-start | bytes 7077888 | tf_op jit(solution)/shard_map/reduce_scatter | solution.py:266
  1242.1 171.7 %copy-start.10 = (f32[256,2048]{1,0:T(8,128)S(1)}, f32[256,2048]{1,0:T(8,128)}, u32[]{:S(2)}) copy-start(f32[256,2048]{1,0:T(8,128)} %copy-done.9) | copy-start | bytes 6291460
  1242.1 171.7 %copy-start.43 = (f32[256]{0:T(256)S(1)}, f32[256]{0:T(256)}, u32[]{:S(2)}) copy-start(f32[256]{0:T(256)} %copy-done.42) | copy-start | bytes 3076
  (27 other events, 63.2 us)
Sparse Core Ops, SparseCore 0:
  9.9 48.2 all-gather.13
  148.0 78.7 all-gather.11
  228.6 26.7 all-gather.15
  294.7 75.2 reduce-scatter.17
  372.5 68.2 all-gather.19
  442.8 80.7 all-gather.17
  525.3 79.2 all-gather.23
  606.6 42.8 all-gather.21
  682.8 76.7 reduce-scatter.21
  761.7 77.2 reduce-scatter.19
  845.3 81.2 all-gather.25
  1101.5 75.2 reduce-scatter.23
  1180.2 59.5 reduce-scatter.31
  1243.5 33.3 reduce-scatter.37
  1280.2 86.8 reduce-scatter.29
  1370.8 41.1 reduce-scatter.27
  1414.2 135.7 reduce-scatter.35
  1552.7 131.9 reduce-scatter.33
  1688.4 57.9 reduce-scatter.25
where the time goes:
time: 1760 us
  waiting for transfers between devices  1140 us (65%)
  matrix products  233 us (13%)
  blocking collectives  142 us (8%)
  local copies, waits for them, and re-layouts  131 us (7%)
  other arithmetic  77 us (4%)
    unnamed x22, waiting for transfers between devices  303 us
    all_gather x4, waiting for transfers between devices, gather_rows(): return lax.all_gather(values, 'tp', axis=0, tiled=True)  272 us
    reduce_scatter x2, waiting for transfers between devices, reduce_forward(): lax.psum_scatter(values.astype(jnp.bfloat16), 'tp', scatter_dimension=0,...  149 us
    reduce_scatter x1, waiting for transfers between devices, local(): lax.psum_scatter(grad_gu.astype(jnp.bfloat16), 'fsdp', scatter_dimension=...  88.8 us
    reduce_scatter x2, waiting for transfers between devices, reduce_back(): lax.psum_scatter(values.astype(jnp.bfloat16), 'tp', scatter_dimension=0,...  74.2 us
    all_gather x1, blocking collectives, local(): lax.all_gather(ln_gains, ('fsdp', 'tp'), axis=1, tiled=True)  70.1 us
    all_gather x1, waiting for transfers between devices, local(): lax.all_gather(w_gate_up, 'fsdp', axis=0, tiled=True)  64.2 us
    all_gather x1, blocking collectives, local(): lax.all_gather(ln_shifts, ('fsdp', 'tp'), axis=1, tiled=True)  63.8 us
  transfers between devices with their start and end apart: 19, of which 17 were waited for; matrix products, arithmetic and copies ran while one was open for 12% of the time, Pallas kernels for 0%

commit v1 on v0

v1 whole, which is shorter than its diff:
```python
import functools

import jax
import jax.numpy as jnp
from jax import lax
from jax.experimental import pallas as pl
from jax.experimental.pallas import tpu as pltpu
from jax.sharding import PartitionSpec as P

HEAD = 64
ROT = 16
NORM_EPS = 1e-05
LANES = 128
MESH = pl.DeviceIdType.MESH
NN = (((1,), (0,)), ((), ()))
NT = (((1,), (1,)), ((), ()))
TN = (((0,), (0,)), ((), ()))
F32 = jnp.float32
BF16 = jnp.bfloat16


def dot(left, right, dims):
    return lax.dot_general(left, right, dims, preferred_element_type=F32)


def layer_norm(values, gain_row, shift_row):
    average = jnp.mean(values, axis=-1, keepdims=True)
    centred = values - average
    variance = jnp.mean(centred * centred, axis=-1, keepdims=True)
    return centred * lax.rsqrt(variance + NORM_EPS) * gain_row + shift_row


def swiglu(gate_vals, up_vals):
    return jax.nn.silu(gate_vals) * up_vals


def exchange_kernel(sizes, scatter, send_ref, got_ref, send_sems, recv_sems):
    outer, inner = sizes
    count = outer * inner
    me = lax.axis_index("fsdp") * inner + lax.axis_index("tp")
    barrier = pltpu.get_barrier_semaphore()

    def greet(step, carry):
        other = lax.rem(me + step, count)
        pl.semaphore_signal(
            barrier, inc=1, device_id=(other // inner, lax.rem(other, inner)), device_id_type=MESH
        )
        return carry

    lax.fori_loop(1, count, greet, 0)
    pl.semaphore_wait(barrier, count - 1)

    def copy_to(step):
        other = lax.rem(me + step, count)
        return pltpu.make_async_remote_copy(
            src_ref=send_ref.at[other] if scatter else send_ref.at[0],
            dst_ref=got_ref.at[me],
            send_sem=send_sems.at[step],
            recv_sem=recv_sems.at[me],
            device_id=(other // inner, lax.rem(other, inner)),
            device_id_type=MESH,
        )

    def start(step, carry):
        copy_to(step).start()
        return carry

    lax.fori_loop(1, count, start, 0)
    got_ref[me] = send_ref[me] if scatter else send_ref[0]

    def finish(step, carry):
        source = lax.rem(me + step, count)
        copy_to(step).wait_send()
        pltpu.make_async_remote_copy(
            src_ref=send_ref.at[0],
            dst_ref=got_ref.at[source],
            send_sem=send_sems.at[step],
            recv_sem=recv_sems.at[source],
            device_id=(source // inner, lax.rem(source, inner)),
            device_id_type=MESH,
        ).wait_recv()
        return carry

    lax.fori_loop(1, count, finish, 0)


def exchange(tiles, sizes, scatter, collective_id):
    count = sizes[0] * sizes[1]
    return pl.pallas_call(
        functools.partial(exchange_kernel, sizes, scatter),
        out_shape=jax.ShapeDtypeStruct((count, 8, LANES), F32),
        in_specs=[pl.BlockSpec(memory_space=pltpu.VMEM)],
        out_specs=pl.BlockSpec(memory_space=pltpu.VMEM),
        scratch_shapes=[
            pltpu.SemaphoreType.DMA((count,)),
            pltpu.SemaphoreType.DMA((count,)),
        ],
        compiler_params=pltpu.CompilerParams(collective_id=collective_id, has_side_effects=True),
    )(tiles)


def turn(values, cosine, sine_low, sine_high):
    return (
        values * cosine
        + pltpu.roll(values, LANES - ROT // 2, 1) * sine_low
        + pltpu.roll(values, ROT // 2, 1) * sine_high
    )


def key_range(block, rows, widest):
    first = max(0, block * rows - widest)
    return first, (block + 1) * rows


def seen_weights(key_rows, query_cols, starts_row, first_key, first_query):
    scores = dot(key_rows, query_cols, NN)
    key_ids = first_key + lax.broadcasted_iota(jnp.int32, scores.shape, 0)
    query_ids = first_query + lax.broadcasted_iota(jnp.int32, scores.shape, 1)
    seen = (key_ids <= query_ids) & (key_ids >= starts_row)
    scores = jnp.where(seen, scores, -1e30)
    top = jnp.max(scores, axis=0, keepdims=True)
    weights = jnp.exp(scores - top)
    return weights, jnp.sum(weights, axis=0, keepdims=True)


def attend_kernel(rows, widest, q_in, k_in, v_in, cos, s_low, s_high, starts, q_out, k_out, v_out, o_out, vt):
    seq_len = q_in.shape[0]
    cosine, sine_low, sine_high = cos[...], s_low[...], s_high[...]
    q_out[...] = turn(q_in[...], cosine, sine_low, sine_high).astype(BF16)
    k_out[...] = turn(k_in[...], cosine, sine_low, sine_high).astype(BF16)
    v_low = v_in[...].astype(BF16)
    v_out[...] = v_low
    vt[...] = v_low.astype(F32).T.astype(BF16)
    for block in range(seq_len // rows):
        here = slice(block * rows, (block + 1) * rows)
        first, last = key_range(block, rows, widest)
        query_cols = (q_out[here, :].astype(F32) * HEAD**-0.5).T.astype(BF16)
        head_of = lax.broadcasted_iota(jnp.int32, query_cols.shape, 0) // HEAD
        parts = []
        for head in range(LANES // HEAD):
            own_cols = jnp.where(head_of == head, query_cols, jnp.zeros_like(query_cols))
            weights, total = seen_weights(
                k_out[first:last, :], own_cols, starts[:, here], first, block * rows
            )
            part = dot(vt[head * HEAD : (head + 1) * HEAD, first:last], weights.astype(BF16), NN)
            parts.append(part / total)
        o_out[here, :] = jnp.concatenate(parts, axis=0).T.astype(BF16)


def attend_back_kernel(
    rows, widest, q_in, k_in, v_in, g_in, cos, s_low, s_high, starts, g_out, b_out, kt, dk, dv
):
    seq_len = q_in.shape[0]
    cosine, sine_low, sine_high = cos[...], s_low[...], s_high[...]
    kt[...] = k_in[...].astype(F32).T.astype(BF16)
    dk[...] = jnp.zeros_like(dk)
    dv[...] = jnp.zeros_like(dv)
    for block in range(seq_len // rows):
        here = slice(block * rows, (block + 1) * rows)
        first, last = key_range(block, rows, widest)
        query_rows = (q_in[here, :].astype(F32) * HEAD**-0.5).astype(BF16)
        grad_rows = g_in[here, :]
        query_cols = query_rows.astype(F32).T.astype(BF16)
        grad_cols = grad_rows.astype(F32).T.astype(BF16)
        head_down = lax.broadcasted_iota(jnp.int32, query_cols.shape, 0) // HEAD
        head_along = lax.broadcasted_iota(jnp.int32, query_rows.shape, 1) // HEAD
        none_down, none_along = jnp.zeros_like(query_cols), jnp.zeros_like(query_rows)
        parts = []
        for head in range(LANES // HEAD):
            weights, total = seen_weights(
                k_in[first:last, :],
                jnp.where(head_down == head, query_cols, none_down),
                starts[:, here],
                first,
                block * rows,
            )
            probs = weights * (1.0 / total)
            grad_probs = dot(
                v_in[first:last, :], jnp.where(head_down == head, grad_cols, none_down), NN
            )
            inner = jnp.sum(probs * grad_probs, axis=0, keepdims=True)
            grad_scores = (probs * (grad_probs - inner)).astype(BF16)
            dk[first:last, :] += dot(
                grad_scores, jnp.where(head_along == head, query_rows, none_along), NN
            )
            dv[first:last, :] += dot(
                probs.astype(BF16), jnp.where(head_along == head, grad_rows, none_along), NN
            )
            parts.append(dot(kt[head * HEAD : (head + 1) * HEAD, first:last], grad_scores, NN))
        grad_queries = jnp.concatenate(parts, axis=0).T * HEAD**-0.5
        g_out[0, here, :] = turn(
            grad_queries, cosine[here, :], -sine_low[here, :], -sine_high[here, :]
        ).astype(BF16)
    g_out[1] = turn(dk[...], cosine, -sine_low, -sine_high).astype(BF16)
    g_out[2] = dv[...].astype(BF16)
    b_out[...] = jnp.sum(g_out[...].astype(F32), axis=1, keepdims=True)


def attend_forward(projected, tables, starts, widest):
    seq_len, width = projected.shape[0], projected.shape[1] // 3
    pairs = width // LANES
    rows = min(256, seq_len)
    column = lambda part: pl.BlockSpec((seq_len, LANES), lambda i, part=part: (0, part * pairs + i))
    whole = lambda shape: pl.BlockSpec(shape, lambda i: (0, 0))
    out = jax.ShapeDtypeStruct((seq_len, width), BF16)
    return pl.pallas_call(
        functools.partial(attend_kernel, rows, widest),
        grid=(pairs,),
        in_specs=[column(0), column(1), column(2)]
        + [whole((seq_len, LANES))] * 3
        + [whole((1, seq_len))],
        out_specs=[column(0)] * 4,
        out_shape=[out] * 4,
        scratch_shapes=[pltpu.VMEM((LANES, seq_len), BF16)],
        compiler_params=pltpu.CompilerParams(vmem_limit_bytes=48 * 2**20),
        cost_estimate=pl.CostEstimate(
            flops=4 * seq_len * seq_len * width, bytes_accessed=20 * seq_len * width, transcendentals=0
        ),
    )(projected, projected, projected, *tables, starts)


def attend_backward(queries, key_vals, value_rows, grad_attended, tables, starts, widest):
    seq_len, width = queries.shape
    pairs = width // LANES
    rows = min(256, seq_len)
    column = pl.BlockSpec((seq_len, LANES), lambda i: (0, i))
    whole = lambda shape: pl.BlockSpec(shape, lambda i: (0, 0))
    return pl.pallas_call(
        functools.partial(attend_back_kernel, rows, widest),
        grid=(pairs,),
        in_specs=[column] * 4 + [whole((seq_len, LANES))] * 3 + [whole((1, seq_len))],
        out_specs=[
            pl.BlockSpec((3, seq_len, LANES), lambda i: (0, 0, i)),
            pl.BlockSpec((3, 1, LANES), lambda i: (0, 0, i)),
        ],
        out_shape=[
            jax.ShapeDtypeStruct((3, seq_len, width), BF16),
            jax.ShapeDtypeStruct((3, 1, width), F32),
        ],
        scratch_shapes=[
            pltpu.VMEM((LANES, seq_len), BF16),
            pltpu.VMEM((seq_len, LANES), F32),
            pltpu.VMEM((seq_len, LANES), F32),
        ],
        compiler_params=pltpu.CompilerParams(vmem_limit_bytes=48 * 2**20),
        cost_estimate=pl.CostEstimate(
            flops=10 * seq_len * seq_len * width, bytes_accessed=20 * seq_len * width, transcendentals=0
        ),
    )(queries, key_vals, value_rows, grad_attended, *tables, starts)


def hop(values, axis, size, partner):
    return lax.ppermute(values, axis, [(i, partner(i)) for i in range(size)])


def gather_fsdp(own, size):
    me = lax.axis_index("fsdp")
    near = [own] + [
        hop(own, "fsdp", size, lambda i, k=k: i ^ (2 * k)) for k in range(1, size // 2)
    ]
    far = [hop(block, "fsdp", size, lambda i: i ^ 1) for block in near]
    whole = jnp.zeros((size,) + own.shape, own.dtype)
    for k in range(size // 2):
        whole = lax.dynamic_update_index_in_dim(whole, near[k], me ^ (2 * k), 0)
        whole = lax.dynamic_update_index_in_dim(whole, far[k], me ^ (2 * k) ^ 1, 0)
    return whole


def scatter_fsdp(blocks, size):
    me = lax.axis_index("fsdp")
    core, chip = me % 2, me // 2
    pairs = blocks.reshape((size // 2, 2) + blocks.shape[1:])
    mine = lax.dynamic_index_in_dim(pairs, core, 1, keepdims=False)
    other = lax.dynamic_index_in_dim(pairs, 1 - core, 1, keepdims=False)
    got = hop(other, "fsdp", size, lambda i: i ^ 1)
    sums = (mine.astype(F32) + got.astype(F32)).astype(BF16)
    total = lax.dynamic_index_in_dim(sums, chip, 0, keepdims=False).astype(F32)
    for k in range(1, size // 2):
        block = lax.dynamic_index_in_dim(sums, chip ^ k, 0, keepdims=False)
        total = total + hop(block, "fsdp", size, lambda i, k=k: i ^ (2 * k)).astype(F32)
    return total


def swap_tp(blocks, size):
    me = lax.axis_index("tp")
    got = blocks
    for k in range(1, size):
        block = lax.dynamic_index_in_dim(blocks, (me + k) % size, 0, keepdims=False)
        came = hop(block, "tp", size, lambda i, k=k: (i + k) % size)
        got = lax.dynamic_update_index_in_dim(got, came, (me + size - k) % size, 0)
    return got


def gather_tp_small(own, size):
    me = lax.axis_index("tp")
    whole = jnp.zeros((size,) + own.shape, own.dtype)
    whole = lax.dynamic_update_index_in_dim(whole, own, me, 0)
    for k in range(1, size):
        came = hop(own, "tp", size, lambda i, k=k: (i + k) % size)
        whole = lax.dynamic_update_index_in_dim(whole, came, (me + size - k) % size, 0)
    return whole


def gather_rows(values):
    return lax.all_gather(values, "tp", axis=0, tiled=True)


def reduce_rows(values):
    return lax.psum_scatter(values.astype(BF16), "tp", scatter_dimension=0, tiled=True).astype(F32)


def local(tokens, lengths, ln_gains, ln_shifts, w_qkv, b_qkv, w_out, w_gate_up, w_down, cotangent):
    n_fsdp, n_tp = lax.axis_size("fsdp"), lax.axis_size("tp")
    sizes = (n_fsdp, n_tp)
    at_tp = lax.axis_index("tp")
    slab_rows, model_width = tokens.shape
    seq_len = slab_rows * n_tp
    small = ln_gains.shape[1]
    local_width = w_qkv.shape[2]
    hidden_width = w_gate_up.shape[2]
    part_rows = w_qkv.shape[0]

    tile = jnp.concatenate([ln_gains, ln_shifts, b_qkv.astype(F32), jnp.zeros((1, small), F32)], 0)
    tile = jnp.pad(tile, ((0, 0), (0, LANES - small)))
    got = exchange(tile[None], sizes, False, 1)
    rows_all = got[:, :, :small]
    norm_rows = rows_all[:, :4].transpose(1, 0, 2).reshape(4, model_width)
    gains_all, shifts_all = norm_rows[:2], norm_rows[2:]
    bias = lax.dynamic_index_in_dim(rows_all.reshape(n_fsdp, n_tp, 8, small), at_tp, 1, keepdims=False)
    bias = bias[:, 4:7].transpose(1, 0, 2).reshape(1, 3 * local_width)

    qkv_all = gather_fsdp(w_qkv.reshape(part_rows, 3 * local_width), n_fsdp).reshape(
        model_width, 3 * local_width
    )
    out_part = gather_tp_small(w_out.T, n_tp).transpose(1, 0, 2).reshape(part_rows, model_width)
    out_all = gather_fsdp(out_part, n_fsdp).reshape(model_width, model_width)
    gu_all = gather_fsdp(w_gate_up.reshape(part_rows, 2 * hidden_width), n_fsdp).reshape(
        model_width, 2 * hidden_width
    )
    down_all = gather_fsdp(w_down.T, n_fsdp).reshape(model_width, hidden_width)

    length_row = lengths[0]
    doc_ends = jnp.cumsum(length_row)
    ids = jnp.arange(seq_len, dtype=jnp.int32)
    passed = (doc_ends[None, :] <= ids[:, None]).astype(jnp.int32)
    starts = jnp.sum(passed * length_row[None, :], axis=1)
    places = (ids - starts).astype(F32)
    lane = jnp.arange(LANES, dtype=jnp.int32) % HEAD
    frequency = 10000.0 ** (-2.0 * (lane % (ROT // 2)).astype(F32) / ROT)
    angles = places[:, None] * frequency[None, :]
    cosine = jnp.where(lane[None] < ROT, jnp.cos(angles), 1.0)
    sine = jnp.sin(angles)
    sine_low = jnp.where(lane[None] < ROT // 2, -sine, 0.0)
    sine_high = jnp.where((lane[None] >= ROT // 2) & (lane[None] < ROT), sine, 0.0)
    tables = (cosine, sine_low, sine_high)
    starts_row = starts.reshape(1, seq_len).astype(jnp.int32)
    widest = seq_len // 2

    token_rows = tokens.astype(F32)
    normed_one = layer_norm(token_rows, gains_all[0], shifts_all[0])
    full_one = gather_rows(normed_one.astype(BF16))
    projected = dot(full_one, qkv_all, NN) + bias
    queries, key_vals, value_rows, attended = attend_forward(projected, tables, starts_row, widest)
    attended_own = (
        swap_tp(attended.reshape(n_tp, slab_rows, local_width), n_tp)
        .transpose(1, 0, 2)
        .reshape(slab_rows, model_width)
    )
    residual = token_rows + dot(attended_own, out_all, NT)

    normed_two = layer_norm(residual, gains_all[1], shifts_all[1])
    full_two = gather_rows(normed_two.astype(BF16))
    grad_branch = gather_rows(cotangent)
    gate_up = dot(full_two, gu_all, NN)
    gate, up = gate_up[:, :hidden_width], gate_up[:, hidden_width:]
    hidden_low = swiglu(gate, up).astype(BF16)
    branch = reduce_rows(dot(hidden_low, down_all, NT))
    result = (residual + branch).astype(BF16)
    grad_out = cotangent.astype(F32)
    grad_hidden = dot(grad_branch, down_all, NN)
    _, swiglu_pull = jax.vjp(swiglu, gate, up)
    grad_gate, grad_up = swiglu_pull(grad_hidden)
    grad_gate_up = jnp.concatenate([grad_gate, grad_up], axis=1).astype(BF16)
    grad_normed_two = reduce_rows(dot(grad_gate_up, gu_all, NT))
    grad_gu = dot(full_two, grad_gate_up, TN).astype(BF16)
    grad_down = dot(grad_branch, hidden_low, TN).astype(BF16)
    gu_share = scatter_fsdp(grad_gu.reshape(n_fsdp, part_rows, 2 * hidden_width), n_fsdp)
    down_share = scatter_fsdp(grad_down.reshape(n_fsdp, part_rows, hidden_width), n_fsdp)
    _, second_pull = jax.vjp(layer_norm, residual, gains_all[1], shifts_all[1])
    grad_resid_norm, grad_gain_two, grad_shift_two = second_pull(grad_normed_two)
    grad_residual = grad_out + grad_resid_norm

    grad_attn = grad_residual.astype(BF16)
    grad_o = dot(grad_attn, attended_own, TN).astype(BF16)
    grad_attended_own = dot(grad_attn, out_all, NN).astype(BF16)
    grad_attended = swap_tp(
        grad_attended_own.reshape(slab_rows, n_tp, local_width).transpose(1, 0, 2), n_tp
    ).reshape(seq_len, local_width)
    grad_projected, grad_bias = attend_backward(
        queries, key_vals, value_rows, grad_attended, tables, starts_row, widest
    )
    grad_projected = grad_projected.transpose(1, 0, 2).reshape(seq_len, 3 * local_width)
    grad_qkv = dot(full_one, grad_projected, TN).astype(BF16)
    grad_normed_one = reduce_rows(dot(grad_projected, qkv_all, NT))
    _, first_pull = jax.vjp(layer_norm, token_rows, gains_all[0], shifts_all[0])
    grad_token_norm, grad_gain_one, grad_shift_one = first_pull(grad_normed_one)
    grad_tokens = grad_residual + grad_token_norm

    out_share = scatter_fsdp(grad_o.reshape(n_fsdp, part_rows, model_width), n_fsdp).astype(BF16)
    out_share = jnp.sum(
        swap_tp(out_share.reshape(part_rows, n_tp, local_width).transpose(1, 0, 2), n_tp).astype(F32),
        axis=0,
    ).T
    qkv_share = scatter_fsdp(grad_qkv.reshape(n_fsdp, part_rows, 3 * local_width), n_fsdp)

    count = n_fsdp * n_tp
    norm_grads = jnp.stack([grad_gain_one, grad_gain_two, grad_shift_one, grad_shift_two])
    norm_grads = norm_grads.reshape(4, count, small).transpose(1, 0, 2)
    bias_grads = grad_bias.reshape(3, n_fsdp, small).transpose(1, 0, 2)
    bias_grads = jnp.where(
        (jnp.arange(n_tp) == at_tp)[None, :, None, None], bias_grads[:, None], 0.0
    ).reshape(count, 3, small)
    tiles = jnp.concatenate([norm_grads, bias_grads, jnp.zeros((count, 1, small), F32)], axis=1)
    tiles = jnp.pad(tiles, ((0, 0), (0, 0), (0, LANES - small)))
    shares = jnp.sum(exchange(tiles, sizes, True, 2), axis=0)[:, :small]

    return (
        result,
        grad_tokens,
        shares[0:2],
        shares[2:4],
        qkv_share.reshape(part_rows, 3, local_width),
        shares[4:7],
        out_share,
        gu_share.reshape(part_rows, 2, hidden_width),
        down_share.T,
    )


def solution(mesh):
    placed = (
        P(("fsdp", "tp"), None),
        P("fsdp", None),
        P(None, ("fsdp", "tp")),
        P(None, ("fsdp", "tp")),
        P("fsdp", None, "tp"),
        P(None, ("tp", "fsdp")),
        P("tp", "fsdp"),
        P("fsdp", None, "tp"),
        P("tp", "fsdp"),
        P(("fsdp", "tp"), None),
    )
    return jax.shard_map(
        local,
        mesh=mesh,
        in_specs=placed,
        out_specs=(
            P(("fsdp", "tp"), None),
            P(("fsdp", "tp"), None),
            P(None, ("fsdp", "tp")),
            P(None, ("fsdp", "tp")),
            P("fsdp", None, "tp"),
            P(None, ("tp", "fsdp")),
            P("tp", "fsdp"),
            P("fsdp", None, "tp"),
            P("tp", "fsdp"),
        ),
        check_vma=False,
    )
```

time: 1760 us -> 937 us (0.53)
  waiting for transfers between devices: 1140 us -> 327 us
  blocking collectives: 142 us -> 0 us
  local copies, waits for them, and re-layouts: 131 us -> 243 us
  matrix products: 233 us -> 139 us
  Pallas kernels: 0 us -> 79.8 us
  starting transfers between devices: 0.78 us -> 64.2 us
  other arithmetic: 77 us -> 58.8 us
    reduce_scatter x8 -> x3, waiting for transfers between devices: 459 us -> 68.3 us  [reduce_rows(): lax.psum_scatter(values.astype(BF16), 'tp', scatter_dimension=0, tiled=True)]
    unnamed x22 -> x6, waiting for transfers between devices: 303 us -> 0.1 us
    all_gather x4 -> x3, waiting for transfers between devices: 272 us -> 23.1 us  [gather_rows(): return lax.all_gather(values, 'tp', axis=0, tiled=True)]
    ppermute x0 -> x56, waiting for transfers between devices: none -> 236 us  [hop(): return lax.ppermute(values, axis, [(i, partner(i)) for i in range(size)])]
    all_gather x3 -> x0, blocking collectives: 142 us -> none  [the longest x1 70.1 us: local(): lax.all_gather(ln_gains, ('fsdp', 'tp'), axis=1, tiled=True)]
    all_gather x4 -> x0, waiting for transfers between devices: 109 us -> none  [the longest x1 64.2 us: local(): lax.all_gather(w_gate_up, 'fsdp', axis=0, tiled=True)]
    dot_general x26 -> x12, matrix products: 233 us -> 139 us  [dot(): return lax.dot_general(left, right, dims, preferred_element_type=F32)]
    pallas_call x0 -> x4, Pallas kernels: none -> 79.8 us  [the longest x2 36.3 us: exchange(): pl.pallas_call(functools.partial(exchange_kernel, sizes, scatter), out_sh...]
  transfers between devices with their start and end apart: 19 -> 62, of which waited for: 17 -> 18; matrix products, arithmetic and copies ran while one was open for 12% -> 40% of each run, Pallas kernels for 0% -> 7%
where the time goes in v1:
time: 937 us; the launch traced here: 928 us
  waiting for transfers between devices  327 us (35%)
  local copies, waits for them, and re-layouts  243 us (26%)
  matrix products  139 us (15%)
  Pallas kernels  79.8 us (9%)
  starting transfers between devices  64.2 us (7%)
  other arithmetic  58.8 us (6%)
  between operations  15.2 us (2%)
    ppermute x56, waiting for transfers between devices, hop(): return lax.ppermute(values, axis, [(i, partner(i)) for i in range(size)])  236 us
    dot_general x12, matrix products, dot(): return lax.dot_general(left, right, dims, preferred_element_type=F32)  139 us
    reduce_scatter x3, waiting for transfers between devices, reduce_rows(): lax.psum_scatter(values.astype(BF16), 'tp', scatter_dimension=0, tiled=True)  68.3 us
    ppermute x56, starting transfers between devices, hop(): return lax.ppermute(values, axis, [(i, partner(i)) for i in range(size)])  63.9 us
    pallas_call x2, Pallas kernels, exchange(): pl.pallas_call(functools.partial(exchange_kernel, sizes, scatter), out_sh...  36.3 us
    unnamed x93, local copies, waits for them, and re-layouts  34.5 us
    dynamic_update_slice x3, local copies, waits for them, and re-layouts, gather_tp_small(): lax.dynamic_update_index_in_dim(whole, came, (me + size - k) % size, 0)  25.4 us
    pallas_call x1, Pallas kernels, attend_backward(): pl.pallas_call(functools.partial(attend_back_kernel, rows, widest), grid=...  25.2 us
  transfers between devices with their start and end apart: 62, of which 18 were waited for; matrix products, arithmetic and copies ran while one was open for 40% of the time, Pallas kernels for 7%

profile of v1, /device:TPU:0, one launch (start us, length us, event | category | flops | bytes accessed | tf_op | source)
XLA Modules:
  0.0 927.7 jit_solution(5461989315010382096)
XLA Ops:
  19.5 24.1 %shard_map.169 = f32[32,8,128]{2,1,0:T(8,128)} custom-call(f32[1,8,128]{2,1,0:T(8,128)} %pad_bitcast_fusion.send_ref), custom_call_target="tpu_custom_call" | custom-call | tf_op jit(solution)/shard_map/pallas_call | solution.py:89
  54.8 8.5 dynamic_update_slice.151
  74.7 8.4 dynamic_update_slice.152
  83.2 8.5 dynamic_update_slice.153
  91.6 8.5 dynamic_update_slice.154
  106.1 4.4 broadcast_in_dim.265
  124.0 20.7 %collective-permute-done.5 = bf16[256,1536]{0,1:T(8,128)(2,1)} collective-permute-done((bf16[256,1536]{0,1:T(8,128)(2,1)S(1)}, bf16[256,1536]{0,1:T(8,128)(2,1)}, u32[]{:S(2)}, u32[]{:S(2)}) %collective-permute-start.5) | collective-permute-done | bytes 786464 | tf_op jit(solution)/shard_map/ppermute | solution.py:253
  151.6 26.4 %collective-permute-done.16 = bf16[256,2048]{1,0:T(8,128)(2,1)} collective-permute-done((bf16[256,2048]{1,0:T(8,128)(2,1)}, bf16[256,2048]{1,0:T(8,128)(2,1)}, u32[]{:S(2)}, u32[]{:S(2)}) %collective-permute-start.16) | collective-permute-done | bytes 1048608 | tf_op jit(solution)/shard_map/ppermute | solution.py:253
  201.7 11.7 %convolution_add_fusion.q_in.k_in.v_in = f32[1024,1536]{1,0:T(8,128)} fusion(bf16[1024,2048]{1,0:T(8,128)(2,1)} %all-gather.4.cloned.1.call-done, bf16[2048,1536]{1,0:T(8,128)(2,1)} %bitcast.11, f32[1536]{0:T(1024)S(1)} %add.374), kind=kOutput, calls=%fused_computation.25 | convolution fusion | flops 6444023808 | bytes 16783360 | tf_op jit(solution)/shard_map/dot_general | solution.py:23
  213.4 18.3 %shard_map.170 = (bf16[1024,512]{1,0:T(8,128)(2,1)S(1)}, bf16[1024,512]{1,0:T(8,128)(2,1)S(1)}, bf16[1024,512]{1,0:T(8,128)(2,1)S(1)}, bf16[1024,512]{1,0:T(8,128)(2,1)S(1)}) custom-call(f32[1024,1536]{1,0:T(8,128)} %convolution_add_fusion.q_in.k_in.v_in, f32[1024,1536]{1,0:T(8,128)} %convolution_add_fusion.q_in.k_in.v_in, ...), custom_call_target="tpu_custom_call" | custom-call | flops 2147483648 | bytes 10485760 | tf_op jit(solution)/shard_map/pallas_call | solution.py:206
  247.6 10.0 %collective-permute-done.8 = bf16[256,512]{0,1:T(8,128)(2,1)S(1)} collective-permute-done((bf16[256,512]{0,1:T(8,128)(2,1)}, bf16[256,512]{0,1:T(8,128)(2,1)S(1)}, u32[]{:S(2)}, u32[]{:S(2)}) %collective-permute-start.8) | collective-permute-done | bytes 262176 | tf_op jit(solution)/shard_map/ppermute | solution.py:253
  259.0 6.4 fusion.52
  279.0 5.0 broadcast_in_dim.279
  286.4 63.2 %collective-permute-done.28 = bf16[256,1408]{1,0:T(8,128)(2,1)} collective-permute-done((bf16[256,1408]{1,0:T(8,128)(2,1)}, bf16[256,1408]{1,0:T(8,128)(2,1)}, u32[]{:S(2)}, u32[]{:S(2)}) %collective-permute-start.28) | collective-permute-done | bytes 720928 | tf_op jit(solution)/shard_map/ppermute | solution.py:253
  354.3 17.3 %collective-permute-done.32 = bf16[256,1408]{1,0:T(8,128)(2,1)S(1)} collective-permute-done((bf16[256,1408]{1,0:T(8,128)(2,1)S(1)}, bf16[256,1408]{1,0:T(8,128)(2,1)S(1)}, u32[]{:S(2)}, u32[]{:S(2)}) %collective-permute-start.32) | collective-permute-done | bytes 720928 | tf_op jit(solution)/shard_map/ppermute | solution.py:253
  390.5 18.8 %fusion.53 = f32[1024,2816]{1,0:T(8,128)} fusion(bf16[1024,2048]{1,0:T(8,128)(2,1)} %all-gather.6.cloned.1.call-done, bf16[2048,2816]{1,0:T(8,128)(2,1)} %bitcast.49), kind=kOutput, calls=%fused_computation.199 | convolution fusion | flops 11811160064 | bytes 27262976 | tf_op jit(solution)/shard_map/dot_general | solution.py:23
  409.3 23.1 %all-gather.8.cloned.1.call-done = bf16[1024,2048]{1,0:T(8,128)(2,1)} async-done(((bf16[256,2048]{1,0:T(8,128)(2,1)}), bf16[1024,2048]{1,0:T(8,128)(2,1)}) %all-gather.8.cloned.1.call-update) | async-done | bytes 4194320 | tf_op jit(solution)/shard_map/all_gather | solution.py:305
  432.4 15.5 %fusion.6 = (bf16[1024,1408]{1,0:T(8,128)(2,1)S(1)}, bf16[1024,1408]{1,0:T(8,128)(2,1)S(1)}, bf16[1024,1408]{1,0:T(8,128)(2,1)}) fusion(f32[1024,2816]{1,0:T(8,128)} %fusion.53, bf16[1024,2048]{1,0:T(8,128)(2,1)} %all-gather.8.cloned.1.call-done, bf16[2048,1408]{1,0:T(8,128)(2,1)} %bitcast.252), kind=kOutput, calls=%fused_computation.14 | convolution fusion | flops 5928648704 | bytes 30146560 | tf_op jit(solution)/shard_map/dot_general | solution.py:23
  450.5 16.3 %convolution_convert_fusion.4 = bf16[1024,2048]{1,0:T(8,128)(2,1)} fusion(bf16[2048,2816]{1,0:T(8,128)(2,1)} %bitcast.49, bf16[1024,1408]{1,0:T(8,128)(2,1)S(1)} %get-tuple-element.61, bf16[1024,1408]{1,0:T(8,128)(2,1)S(1)} %get-tuple-element.60), kind=kOutput, calls=%fused_computation.26 | convolution fusion | flops 11824791552 | bytes 21495808 | tf_op jit(solution)/shard_map/dot_general | solution.py:23
  466.9 11.0 %convolution_convert_fusion.6 = bf16[1024,2048]{1,0:T(8,128)(2,1)} fusion(bf16[1024,1408]{1,0:T(8,128)(2,1)} %get-tuple-element.62, bf16[2048,1408]{1,0:T(8,128)(2,1)} %bitcast.253), kind=kOutput, calls=%fused_computation.28 | convolution fusion | flops 5907677184 | bytes 12845056 | tf_op jit(solution)/shard_map/dot_general | solution.py:23
  477.9 10.9 %fusion.2 = bf16[2048,1408]{0,1:T(8,128)(2,1)} fusion(bf16[1024,1408]{1,0:T(8,128)(2,1)} %get-tuple-element.62, bf16[1024,2048]{1,0:T(8,128)(2,1)} %all-gather.8.cloned.1.call-done), kind=kOutput, calls=%fused_computation.9 | convolution fusion | flops 5908463616 | bytes 12845056 | tf_op jit(solution)/shard_map/dot_general | solution.py:23
  488.8 10.4 %reshape_reshape.15 = bf16[4,2,256,1408]{2,1,0,3:T(2,128)(2,1)} reshape(bf16[2048,1408]{0,1:T(8,128)(2,1)} %fusion.2) | data formatting | bytes 11534336 | tf_op jit(solution)/shard_map/reshape;reshape | solution.py:272
  499.3 14.6 %constant_dynamic-slice_fusion.1 = (bf16[4,1,256,1408]{2,1,0,3:T(2,128)(2,1)}, bf16[4,1,256,1408]{2,1,0,3:T(2,128)(2,1)S(1)}) fusion(bf16[4,2,256,1408]{2,1,0,3:T(2,128)(2,1)} %reshape_reshape.15, s32[]{:T(128)S(6)} %select_n.268, s32[]{:T(128)S(6)} %select_n.269), kind=kLoop, calls=%fused_computation.136 | loop fusion | bytes 11534344 | tf_op jit(solution)/shard_map/jit(dynamic_index_in_dim)/dynamic_slice | solution.py:273
  516.4 18.6 %convolution_convert_fusion = bf16[2048,2816]{1,0:T(8,128)(2,1)} fusion(bf16[1024,2048]{1,0:T(8,128)(2,1)} %all-gather.6.cloned.1.call-done, bf16[1024,1408]{1,0:T(8,128)(2,1)} %copy-done.40, bf16[1024,1408]{1,0:T(8,128)(2,1)} %copy-done.39), kind=kOutput, calls=%fused_computation.2 | convolution fusion | flops 11828461568 | bytes 21495808 | tf_op jit(solution)/shard_map/dot_general | solution.py:23
  535.1 5.6 dynamic-slice_bitcast_fusion
  553.5 68.3 %reduce-scatter.4.cloned.1.call-done = bf16[256,2048]{1,0:T(8,128)(2,1)} async-done(((bf16[1024,2048]{1,0:T(8,128)(2,1)}), bf16[256,2048]{1,0:T(8,128)(2,1)}) %reduce-scatter.4.cloned.1.call-update) | async-done | bytes 1048592 | tf_op jit(solution)/shard_map/reduce_scatter | solution.py:309
  627.0 5.8 convolution_convert_fusion.7
  643.6 6.3 copy.118
  653.6 4.3 collective-permute-done.35
  667.1 25.2 %shard_map.171 = (bf16[3,1024,512]{2,1,0:T(8,128)(2,1)}, f32[3,1,512]{2,1,0:T(1,128)S(1)}) custom-call(bf16[1024,512]{1,0:T(8,128)(2,1)S(1)} %copy-done.1, bf16[1024,512]{1,0:T(8,128)(2,1)S(1)} %copy-done.3, bf16[1024,512]{1,0:T(8,128)(2,1)S(1)} %copy-done.5, bf16[1024,512]{1,0:T(8,128)(2,1)S(1)} %bitcast.238, f32[1024,128]{1,0:T(8,128)S(1)} %get-tuple-element.95.cos, ...), custom_call_target="tpu_custom_call" | custom-call | flops 5368709120 | bytes 10485760 | tf_op jit(solution)/shard_map/pallas_call | solution.py:228
  692.3 4.7 copy.113
  697.0 11.2 %convolution_convert_fusion.5 = bf16[1024,2048]{1,0:T(8,128)(2,1)} fusion(bf16[1024,1536]{0,1:T(8,128)(2,1)} %bitcast.259, bf16[2048,1536]{1,0:T(8,128)(2,1)} %bitcast.11), kind=kOutput, calls=%fused_computation.27 | convolution fusion | flops 6444548096 | bytes 13631488 | tf_op jit(solution)/shard_map/dot_general | solution.py:23
  708.2 10.2 %convolution_convert_fusion.3 = bf16[2048,1536]{1,0:T(8,128)(2,1)S(1)} fusion(bf16[1024,2048]{1,0:T(8,128)(2,1)} %all-gather.4.cloned.1.call-done, bf16[1024,1536]{0,1:T(8,128)(2,1)} %bitcast.260), kind=kOutput, calls=%fused_computation.8 | convolution fusion | flops 6445596672 | bytes 13631488 | tf_op jit(solution)/shard_map/dot_general | solution.py:23
  721.9 4.7 copy.116
  730.1 5.7 fusion
  742.2 6.3 copy.130
  748.5 4.6 copy.129
  753.1 4.5 fusion.1
  765.9 8.5 collective-permute-done.51
  777.4 28.0 %collective-permute-done.50 = bf16[256,2816]{1,0:T(8,128)(2,1)} collective-permute-done((bf16[256,2816]{1,0:T(8,128)(2,1)S(1)}, bf16[256,2816]{1,0:T(8,128)(2,1)}, u32[]{:S(2)}, u32[]{:S(2)}) %collective-permute-start.50) | collective-permute-done | bytes 1441824 | tf_op jit(solution)/shard_map/ppermute | solution.py:253
  808.3 19.5 %collective-permute-done.44 = bf16[256,2048]{0,1:T(8,128)(2,1)} collective-permute-done((bf16[256,2048]{0,1:T(8,128)(2,1)S(1)}, bf16[256,2048]{0,1:T(8,128)(2,1)}, u32[]{:S(2)}, u32[]{:S(2)}) %collective-permute-start.44) | collective-permute-done | bytes 1048608 | tf_op jit(solution)/shard_map/ppermute | solution.py:253
  829.3 4.9 fusion.15
  834.2 4.8 reshape.280
  839.4 10.9 %collective-permute-done.43 = bf16[256,2048]{0,1:T(8,128)(2,1)} collective-permute-done((bf16[256,2048]{0,1:T(8,128)(2,1)}, bf16[256,2048]{0,1:T(8,128)(2,1)}, u32[]{:S(2)}, u32[]{:S(2)}) %collective-permute-start.43) | collective-permute-done | bytes 1048608 | tf_op jit(solution)/shard_map/ppermute | solution.py:253
  861.0 6.1 collective-permute-done.40
  867.1 4.7 collective-permute-start.47
  871.8 11.2 %collective-permute-done.39 = bf16[256,1536]{0,1:T(8,128)(2,1)S(1)} collective-permute-done((bf16[256,1536]{0,1:T(8,128)(2,1)}, bf16[256,1536]{0,1:T(8,128)(2,1)S(1)}, u32[]{:S(2)}, u32[]{:S(2)}) %collective-permute-start.39) | collective-permute-done | bytes 786464 | tf_op jit(solution)/shard_map/ppermute | solution.py:253
  902.2 12.1 %shard_map.172 = f32[32,8,128]{2,1,0:T(8,128)} custom-call(f32[32,8,128]{2,1,0:T(8,128)} %pad.9.send_ref), custom_call_target="tpu_custom_call" | custom-call | tf_op jit(solution)/shard_map/pallas_call | solution.py:89
  (350 shorter events, 253.6 us)
Async XLA Ops:
  7.2 194.5 %all-gather.4.cloned.1.call-start = ((), (), s32[]{:S(2)}) async-start(), calls=%async_computation.3 | async-start | bytes 5242880 | tf_op jit(solution)/shard_map/all_gather | solution.py:305
  8.7 94.5 %collective-permute-start = (bf16[256,1536]{0,1:T(8,128)(2,1)S(1)}, bf16[256,1536]{0,1:T(8,128)(2,1)}, u32[]{:S(2)}, u32[]{:S(2)}) collective-permute-start(bf16[256,1536]{0,1:T(8,128)(2,1)S(1)} %bitcast.262), channel_id=1, source_target_pairs={{0,4},{4,0},{8,12},{12,8},{16,20},{20,16},{24,28},{28,24},{1,5},{5... | collective-permute-start | bytes 2359304 | tf_op jit(solution)/shard_map/ppermute | solution.py:253
  9.2 103.8 %collective-permute-start.1 = (bf16[256,1536]{0,1:T(8,128)(2,1)S(1)}, bf16[256,1536]{0,1:T(8,128)(2,1)}, u32[]{:S(2)}, u32[]{:S(2)}) collective-permute-start(bf16[256,1536]{0,1:T(8,128)(2,1)S(1)} %bitcast.263), channel_id=1, source_target_pairs={{0,8},{4,12},{8,0},{12,4},{16,24},{20,28},{24,16},{28,20},{1,9},{5... | collective-permute-start | bytes 2359304 | tf_op jit(solution)/shard_map/ppermute | solution.py:253
  11.8 55.7 %collective-permute-start.10 = (bf16[256,512]{0,1:T(8,128)(2,1)}, bf16[256,512]{0,1:T(8,128)(2,1)}, u32[]{:S(2)}, u32[]{:S(2)}) collective-permute-start(bf16[256,512]{0,1:T(8,128)(2,1)} %bitcast.274), channel_id=1, source_target_pairs={{0,1},{1,2},{2,3},{3,0},{4,5},{5,6},{6,7},{7,4},{8,9},{9,10},{10,1... | collective-permute-start | bytes 786440 | tf_op jit(solution)/shard_map/ppermute | solution.py:253
  13.4 57.4 %collective-permute-start.11 = (bf16[256,512]{0,1:T(8,128)(2,1)}, bf16[256,512]{0,1:T(8,128)(2,1)}, u32[]{:S(2)}, u32[]{:S(2)}) collective-permute-start(bf16[256,512]{0,1:T(8,128)(2,1)} %bitcast.275), channel_id=1, source_target_pairs={{0,2},{1,3},{2,0},{3,1},{4,6},{5,7},{6,4},{7,5},{8,10},{9,11},{10,... | collective-permute-start | bytes 786440 | tf_op jit(solution)/shard_map/ppermute | solution.py:253
  16.0 56.8 %collective-permute-start.12 = (bf16[256,512]{0,1:T(8,128)(2,1)}, bf16[256,512]{0,1:T(8,128)(2,1)}, u32[]{:S(2)}, u32[]{:S(2)}) collective-permute-start(bf16[256,512]{0,1:T(8,128)(2,1)} %bitcast.276), channel_id=1, source_target_pairs={{0,3},{1,0},{2,1},{3,2},{4,7},{5,4},{6,5},{7,6},{8,11},{9,8},{10,9... | collective-permute-start | bytes 786440 | tf_op jit(solution)/shard_map/ppermute | solution.py:253
  49.5 341.0 %all-gather.6.cloned.1.call-start = ((), (), s32[]{:S(2)}) async-start(), calls=%async_computation.4 | async-start | bytes 5242880 | tf_op jit(solution)/shard_map/all_gather | solution.py:305
  67.5 50.2 %collective-permute-start.3 = (bf16[256,1536]{0,1:T(8,128)(2,1)S(1)}, bf16[256,1536]{0,1:T(8,128)(2,1)}, u32[]{:S(2)}, u32[]{:S(2)}) collective-permute-start(bf16[256,1536]{0,1:T(8,128)(2,1)S(1)} %bitcast.265), channel_id=1, source_target_pairs={{0,16},{4,20},{8,24},{12,28},{16,0},{20,4},{24,8},{28,12},{1,17},{... | collective-permute-start | bytes 2359304 | tf_op jit(solution)/shard_map/ppermute | solution.py:253
  101.4 44.9 %collective-permute-start.13 = (bf16[256,2048]{1,0:T(8,128)(2,1)}, bf16[256,2048]{1,0:T(8,128)(2,1)}, u32[]{:S(2)}, u32[]{:S(2)}) collective-permute-start(bf16[256,2048]{1,0:T(8,128)(2,1)} %bitcast.130), channel_id=1, source_target_pairs={{0,4},{4,0},{8,12},{12,8},{16,20},{20,16},{24,28},{28,24},{1,5},{5... | collective-permute-start | bytes 3145736 | tf_op jit(solution)/shard_map/ppermute | solution.py:253
  101.4 45.4 %collective-permute-start.14 = (bf16[256,2048]{1,0:T(8,128)(2,1)}, bf16[256,2048]{1,0:T(8,128)(2,1)}, u32[]{:S(2)}, u32[]{:S(2)}) collective-permute-start(bf16[256,2048]{1,0:T(8,128)(2,1)} %bitcast.130), channel_id=1, source_target_pairs={{0,8},{4,12},{8,0},{12,4},{16,24},{20,28},{24,16},{28,20},{1,9},{5... | collective-permute-start | bytes 3145736 | tf_op jit(solution)/shard_map/ppermute | solution.py:253
  103.2 41.6 %collective-permute-start.5 = (bf16[256,1536]{0,1:T(8,128)(2,1)S(1)}, bf16[256,1536]{0,1:T(8,128)(2,1)}, u32[]{:S(2)}, u32[]{:S(2)}) collective-permute-start(bf16[256,1536]{0,1:T(8,128)(2,1)S(1)} %bitcast.266), channel_id=1, source_target_pairs={{0,24},{4,28},{8,16},{12,20},{16,8},{20,12},{24,0},{28,4},{1,25},{... | collective-permute-start | bytes 2359304 | tf_op jit(solution)/shard_map/ppermute | solution.py:253
  113.0 65.0 %collective-permute-start.16 = (bf16[256,2048]{1,0:T(8,128)(2,1)}, bf16[256,2048]{1,0:T(8,128)(2,1)}, u32[]{:S(2)}, u32[]{:S(2)}) collective-permute-start(bf16[256,2048]{1,0:T(8,128)(2,1)} %bitcast.130), channel_id=1, source_target_pairs={{0,16},{4,20},{8,24},{12,28},{16,0},{20,4},{24,8},{28,12},{1,17},{... | collective-permute-start | bytes 3145736 | tf_op jit(solution)/shard_map/ppermute | solution.py:253
  117.7 60.3 %collective-permute-start.18 = (bf16[256,2048]{1,0:T(8,128)(2,1)}, bf16[256,2048]{1,0:T(8,128)(2,1)}, u32[]{:S(2)}, u32[]{:S(2)}) collective-permute-start(bf16[256,2048]{1,0:T(8,128)(2,1)} %bitcast.130), channel_id=1, source_target_pairs={{0,24},{4,28},{8,16},{12,20},{16,8},{20,12},{24,0},{28,4},{1,25},{... | collective-permute-start | bytes 3145736 | tf_op jit(solution)/shard_map/ppermute | solution.py:253
  146.2 32.3 %collective-permute-start.2 = (bf16[256,1536]{0,1:T(8,128)(2,1)}, bf16[256,1536]{0,1:T(8,128)(2,1)}, u32[]{:S(2)}, u32[]{:S(2)}) collective-permute-start(bf16[256,1536]{0,1:T(8,128)(2,1)} %collective-permute-done.1), channel_id=1, source_target_pairs={{0,4},{4,0},{8,12},{12,8},{16,20},{20,16},{24,28},{28,24},{1,5},{5... | collective-permute-start | bytes 2359304 | tf_op jit(solution)/shard_map/ppermute | solution.py:253
  146.3 36.7 %collective-permute-start.4 = (bf16[256,1536]{0,1:T(8,128)(2,1)}, bf16[256,1536]{0,1:T(8,128)(2,1)}, u32[]{:S(2)}, u32[]{:S(2)}) collective-permute-start(bf16[256,1536]{0,1:T(8,128)(2,1)} %collective-permute-done.3), channel_id=1, source_target_pairs={{0,4},{4,0},{8,12},{12,8},{16,20},{20,16},{24,28},{28,24},{1,5},{5... | collective-permute-start | bytes 2359304 | tf_op jit(solution)/shard_map/ppermute | solution.py:253
  146.7 38.5 %collective-permute-start.6 = (bf16[256,1536]{0,1:T(8,128)(2,1)}, bf16[256,1536]{0,1:T(8,128)(2,1)}, u32[]{:S(2)}, u32[]{:S(2)}) collective-permute-start(bf16[256,1536]{0,1:T(8,128)(2,1)} %collective-permute-done.5), channel_id=1, source_target_pairs={{0,4},{4,0},{8,12},{12,8},{16,20},{20,16},{24,28},{28,24},{1,5},{5... | collective-permute-start | bytes 2359304 | tf_op jit(solution)/shard_map/ppermute | solution.py:253
  178.5 60.4 %collective-permute-start.19 = (bf16[256,2048]{1,0:T(8,128)(2,1)}, bf16[256,2048]{1,0:T(8,128)(2,1)}, u32[]{:S(2)}, u32[]{:S(2)}) collective-permute-start(bf16[256,2048]{1,0:T(8,128)(2,1)} %collective-permute-done.18), channel_id=1, source_target_pairs={{0,4},{4,0},{8,12},{12,8},{16,20},{20,16},{24,28},{28,24},{1,5},{5... | collective-permute-start | bytes 3145736 | tf_op jit(solution)/shard_map/ppermute | solution.py:253
  237.1 20.5 %collective-permute-start.8 = (bf16[256,512]{0,1:T(8,128)(2,1)}, bf16[256,512]{0,1:T(8,128)(2,1)S(1)}, u32[]{:S(2)}, u32[]{:S(2)}) collective-permute-start(bf16[256,512]{0,1:T(8,128)(2,1)} %bitcast.279), channel_id=1, source_target_pairs={{0,2},{1,3},{2,0},{3,1},{4,6},{5,7},{6,4},{7,5},{8,10},{9,11},{10,... | collective-permute-start | bytes 786440 | tf_op jit(solution)/shard_map/ppermute | solution.py:253
  268.2 164.2 %all-gather.8.cloned.1.call-start = ((), (), s32[]{:S(2)}) async-start(), calls=%async_computation.6 | async-start | bytes 5242880 | tf_op jit(solution)/shard_map/all_gather | solution.py:305
  269.5 102.1 %collective-permute-start.21 = (bf16[256,2816]{1,0:T(8,128)(2,1)}, bf16[256,2816]{1,0:T(8,128)(2,1)}, u32[]{:S(2)}, u32[]{:S(2)}) collective-permute-start(bf16[256,2816]{1,0:T(8,128)(2,1)} %bitcast.132), channel_id=1, source_target_pairs={{0,8},{4,12},{8,0},{12,4},{16,24},{20,28},{24,16},{28,20},{1,9},{5... | collective-permute-start | bytes 4325384 | tf_op jit(solution)/shard_map/ppermute | solution.py:253
  271.2 100.9 %collective-permute-start.23 = (bf16[256,2816]{1,0:T(8,128)(2,1)}, bf16[256,2816]{1,0:T(8,128)(2,1)}, u32[]{:S(2)}, u32[]{:S(2)}) collective-permute-start(bf16[256,2816]{1,0:T(8,128)(2,1)} %bitcast.132), channel_id=1, source_target_pairs={{0,16},{4,20},{8,24},{12,28},{16,0},{20,4},{24,8},{28,12},{1,17},{... | collective-permute-start | bytes 4325384 | tf_op jit(solution)/shard_map/ppermute | solution.py:253
  271.8 100.4 %collective-permute-start.25 = (bf16[256,2816]{1,0:T(8,128)(2,1)}, bf16[256,2816]{1,0:T(8,128)(2,1)}, u32[]{:S(2)}, u32[]{:S(2)}) collective-permute-start(bf16[256,2816]{1,0:T(8,128)(2,1)} %bitcast.132), channel_id=1, source_target_pairs={{0,24},{4,28},{8,16},{12,20},{16,8},{20,12},{24,0},{28,4},{1,25},{... | collective-permute-start | bytes 4325384 | tf_op jit(solution)/shard_map/ppermute | solution.py:253
  275.2 74.4 %collective-permute-start.28 = (bf16[256,1408]{1,0:T(8,128)(2,1)}, bf16[256,1408]{1,0:T(8,128)(2,1)}, u32[]{:S(2)}, u32[]{:S(2)}) collective-permute-start(bf16[256,1408]{1,0:T(8,128)(2,1)} %bitcast.268), channel_id=1, source_target_pairs={{0,8},{4,12},{8,0},{12,4},{16,24},{20,28},{24,16},{28,20},{1,9},{5... | collective-permute-start | bytes 2162696 | tf_op jit(solution)/shard_map/ppermute | solution.py:253
  276.9 273.2 %reduce-scatter.6.cloned.1.call-start = ((), (), s32[]{:S(2)}) async-start(), calls=%async_computation.7 | async-start | bytes 5242880 | tf_op jit(solution)/shard_map/reduce_scatter | solution.py:309
  285.8 66.3 %collective-permute-start.30 = (bf16[256,1408]{1,0:T(8,128)(2,1)S(1)}, bf16[256,1408]{1,0:T(8,128)(2,1)S(1)}, u32[]{:S(2)}, u32[]{:S(2)}) collective-permute-start(bf16[256,1408]{1,0:T(8,128)(2,1)S(1)} %bitcast.269), channel_id=1, source_target_pairs={{0,16},{4,20},{8,24},{12,28},{16,0},{20,4},{24,8},{28,12},{1,17},{... | collective-permute-start | bytes 2162696 | tf_op jit(solution)/shard_map/ppermute | solution.py:253
  352.1 19.5 %collective-permute-start.32 = (bf16[256,1408]{1,0:T(8,128)(2,1)S(1)}, bf16[256,1408]{1,0:T(8,128)(2,1)S(1)}, u32[]{:S(2)}, u32[]{:S(2)}) collective-permute-start(bf16[256,1408]{1,0:T(8,128)(2,1)S(1)} %bitcast.270), channel_id=1, source_target_pairs={{0,24},{4,28},{8,16},{12,20},{16,8},{20,12},{24,0},{28,4},{1,25},{... | collective-permute-start | bytes 2162696 | tf_op jit(solution)/shard_map/ppermute | solution.py:253
  466.8 155.0 %reduce-scatter.4.cloned.1.call-start = ((), (), s32[]{:S(2)}) async-start(), calls=%async_computation.5 | async-start | bytes 5242880 | tf_op jit(solution)/shard_map/reduce_scatter | solution.py:309
  477.9 419.1 %reduce-scatter.8.cloned.1.call-start = ((), (), s32[]{:S(2)}) async-start(), calls=%async_computation.8 | async-start | bytes 5242880 | tf_op jit(solution)/shard_map/reduce_scatter | solution.py:309
  516.4 24.7 %collective-permute-start.52 = (bf16[4,256,1408]{1,2,0:T(8,128)(2,1)}, bf16[4,256,1408]{1,2,0:T(8,128)(2,1)}, u32[]{:S(2)}, u32[]{:S(2)}) collective-permute-start(bf16[4,256,1408]{1,2,0:T(8,128)(2,1)} %bitcast.230), channel_id=1, source_target_pairs={{0,4},{4,0},{8,12},{12,8},{16,20},{20,16},{24,28},{28,24},{1,5},{5... | collective-permute-start | bytes 8650760 | tf_op jit(solution)/shard_map/ppermute | solution.py:253
  540.6 189.5 %collective-permute-start.48 = (bf16[4,256,2816]{2,1,0:T(8,128)(2,1)}, bf16[4,256,2816]{2,1,0:T(8,128)(2,1)}, u32[]{:S(2)}, u32[]{:S(2)}) collective-permute-start(bf16[4,256,2816]{2,1,0:T(8,128)(2,1)} %dynamic-slice_bitcast_fusion), channel_id=1, source_target_pairs={{0,4},{4,0},{8,12},{12,8},{16,20},{20,16},{24,28},{28,24},{1,5},{5... | collective-permute-start | bytes 17301512 | tf_op jit(solution)/shard_map/ppermute | solution.py:253
  547.2 179.5 %collective-permute-start.55 = (bf16[256,1408]{0,1:T(8,128)(2,1)}, bf16[256,1408]{0,1:T(8,128)(2,1)S(1)}, u32[]{:S(2)}, u32[]{:S(2)}) collective-permute-start(bf16[256,1408]{0,1:T(8,128)(2,1)} %get-tuple-element.79), channel_id=1, source_target_pairs={{0,24},{4,28},{8,16},{12,20},{16,8},{20,12},{24,0},{28,4},{1,25},{... | collective-permute-start | bytes 2162696 | tf_op jit(solution)/shard_map/ppermute | solution.py:253
  549.6 177.5 %collective-permute-start.54 = (bf16[256,1408]{0,1:T(8,128)(2,1)}, bf16[256,1408]{0,1:T(8,128)(2,1)}, u32[]{:S(2)}, u32[]{:S(2)}) collective-permute-start(bf16[256,1408]{0,1:T(8,128)(2,1)} %get-tuple-element.80), channel_id=1, source_target_pairs={{0,16},{4,20},{8,24},{12,28},{16,0},{20,4},{24,8},{28,12},{1,17},{... | collective-permute-start | bytes 2162696 | tf_op jit(solution)/shard_map/ppermute | solution.py:253
  637.8 20.1 %collective-permute-start.35 = (bf16[256,512]{1,0:T(8,128)(2,1)}, bf16[256,512]{1,0:T(8,128)(2,1)}, u32[]{:S(2)}, u32[]{:S(2)}) collective-permute-start(bf16[256,512]{1,0:T(8,128)(2,1)} %get-tuple-element.86), channel_id=1, source_target_pairs={{0,2},{1,3},{2,0},{3,1},{4,6},{5,7},{6,4},{7,5},{8,10},{9,11},{10,... | collective-permute-start | bytes 786440 | tf_op jit(solution)/shard_map/ppermute | solution.py:253
  657.9 69.2 %collective-permute-start.53 = (bf16[256,1408]{0,1:T(8,128)(2,1)}, bf16[256,1408]{0,1:T(8,128)(2,1)}, u32[]{:S(2)}, u32[]{:S(2)}) collective-permute-start(bf16[256,1408]{0,1:T(8,128)(2,1)} %get-tuple-element.78), channel_id=1, source_target_pairs={{0,8},{4,12},{8,0},{12,4},{16,24},{20,28},{24,16},{28,20},{1,9},{5... | collective-permute-start | bytes 2162696 | tf_op jit(solution)/shard_map/ppermute | solution.py:253
  663.3 89.9 %collective-permute-start.41 = (bf16[4,256,2048]{1,2,0:T(8,128)(2,1)}, bf16[4,256,2048]{1,2,0:T(8,128)(2,1)}, u32[]{:S(2)}, u32[]{:S(2)}) collective-permute-start(bf16[4,256,2048]{1,2,0:T(8,128)(2,1)} %bitcast.255), channel_id=1, source_target_pairs={{0,4},{4,0},{8,12},{12,8},{16,20},{20,16},{24,28},{28,24},{1,5},{5... | collective-permute-start | bytes 12582920 | tf_op jit(solution)/shard_map/ppermute | solution.py:253
  726.6 34.8 %collective-permute-start.37 = (bf16[4,256,1536]{1,2,0:T(8,128)(2,1)}, bf16[4,256,1536]{1,2,0:T(8,128)(2,1)}, u32[]{:S(2)}, u32[]{:S(2)}) collective-permute-start(bf16[4,256,1536]{1,2,0:T(8,128)(2,1)} %bitcast.258), channel_id=1, source_target_pairs={{0,4},{4,0},{8,12},{12,8},{16,20},{20,16},{24,28},{28,24},{1,5},{5... | collective-permute-start | bytes 9437192 | tf_op jit(solution)/shard_map/ppermute | solution.py:253
  738.7 35.7 %collective-permute-start.51 = (bf16[256,2816]{1,0:T(8,128)(2,1)}, bf16[256,2816]{1,0:T(8,128)(2,1)}, u32[]{:S(2)}, u32[]{:S(2)}) collective-permute-start(bf16[256,2816]{1,0:T(8,128)(2,1)} %get-tuple-element.70), channel_id=1, source_target_pairs={{0,24},{4,28},{8,16},{12,20},{16,8},{20,12},{24,0},{28,4},{1,25},{... | collective-permute-start | bytes 4325384 | tf_op jit(solution)/shard_map/ppermute | solution.py:253
  741.1 64.3 %collective-permute-start.50 = (bf16[256,2816]{1,0:T(8,128)(2,1)S(1)}, bf16[256,2816]{1,0:T(8,128)(2,1)}, u32[]{:S(2)}, u32[]{:S(2)}) collective-permute-start(bf16[256,2816]{1,0:T(8,128)(2,1)S(1)} %get-tuple-element.71), channel_id=1, source_target_pairs={{0,16},{4,20},{8,24},{12,28},{16,0},{20,4},{24,8},{28,12},{1,17},{... | collective-permute-start | bytes 4325384 | tf_op jit(solution)/shard_map/ppermute | solution.py:253
  741.7 66.1 %collective-permute-start.49 = (bf16[256,2816]{1,0:T(8,128)(2,1)S(1)}, bf16[256,2816]{1,0:T(8,128)(2,1)}, u32[]{:S(2)}, u32[]{:S(2)}) collective-permute-start(bf16[256,2816]{1,0:T(8,128)(2,1)S(1)} %get-tuple-element.69), channel_id=1, source_target_pairs={{0,8},{4,12},{8,0},{12,4},{16,24},{20,28},{24,16},{28,20},{1,9},{5... | collective-permute-start | bytes 4325384 | tf_op jit(solution)/shard_map/ppermute | solution.py:253
  759.1 68.7 %collective-permute-start.44 = (bf16[256,2048]{0,1:T(8,128)(2,1)S(1)}, bf16[256,2048]{0,1:T(8,128)(2,1)}, u32[]{:S(2)}, u32[]{:S(2)}) collective-permute-start(bf16[256,2048]{0,1:T(8,128)(2,1)S(1)} %get-tuple-element.73), channel_id=1, source_target_pairs={{0,24},{4,28},{8,16},{12,20},{16,8},{20,12},{24,0},{28,4},{1,25},{... | collective-permute-start | bytes 3145736 | tf_op jit(solution)/shard_map/ppermute | solution.py:253
  764.4 85.9 %collective-permute-start.43 = (bf16[256,2048]{0,1:T(8,128)(2,1)}, bf16[256,2048]{0,1:T(8,128)(2,1)}, u32[]{:S(2)}, u32[]{:S(2)}) collective-permute-start(bf16[256,2048]{0,1:T(8,128)(2,1)} %get-tuple-element.74), channel_id=1, source_target_pairs={{0,16},{4,20},{8,24},{12,28},{16,0},{20,4},{24,8},{28,12},{1,17},{... | collective-permute-start | bytes 3145736 | tf_op jit(solution)/shard_map/ppermute | solution.py:253
  774.4 75.9 %collective-permute-start.42 = (bf16[256,2048]{0,1:T(8,128)(2,1)}, bf16[256,2048]{0,1:T(8,128)(2,1)}, u32[]{:S(2)}, u32[]{:S(2)}) collective-permute-start(bf16[256,2048]{0,1:T(8,128)(2,1)} %get-tuple-element.72), channel_id=1, source_target_pairs={{0,8},{4,12},{8,0},{12,4},{16,24},{20,28},{24,16},{28,20},{1,9},{5... | collective-permute-start | bytes 3145736 | tf_op jit(solution)/shard_map/ppermute | solution.py:253
  805.4 61.7 %collective-permute-start.40 = (bf16[256,1536]{0,1:T(8,128)(2,1)}, bf16[256,1536]{0,1:T(8,128)(2,1)S(1)}, u32[]{:S(2)}, u32[]{:S(2)}) collective-permute-start(bf16[256,1536]{0,1:T(8,128)(2,1)} %get-tuple-element.76), channel_id=1, source_target_pairs={{0,24},{4,28},{8,16},{12,20},{16,8},{20,12},{24,0},{28,4},{1,25},{... | collective-permute-start | bytes 2359304 | tf_op jit(solution)/shard_map/ppermute | solution.py:253
  807.8 75.2 %collective-permute-start.39 = (bf16[256,1536]{0,1:T(8,128)(2,1)}, bf16[256,1536]{0,1:T(8,128)(2,1)S(1)}, u32[]{:S(2)}, u32[]{:S(2)}) collective-permute-start(bf16[256,1536]{0,1:T(8,128)(2,1)} %get-tuple-element.77), channel_id=1, source_target_pairs={{0,16},{4,20},{8,24},{12,28},{16,0},{20,4},{24,8},{28,12},{1,17},{... | collective-permute-start | bytes 2359304 | tf_op jit(solution)/shard_map/ppermute | solution.py:253
  827.9 55.4 %collective-permute-start.38 = (bf16[256,1536]{0,1:T(8,128)(2,1)}, bf16[256,1536]{0,1:T(8,128)(2,1)}, u32[]{:S(2)}, u32[]{:S(2)}) collective-permute-start(bf16[256,1536]{0,1:T(8,128)(2,1)} %get-tuple-element.75), channel_id=1, source_target_pairs={{0,8},{4,12},{8,0},{12,4},{16,24},{20,28},{24,16},{28,20},{1,9},{5... | collective-permute-start | bytes 2359304 | tf_op jit(solution)/shard_map/ppermute | solution.py:253
  854.1 35.2 %collective-permute-start.45 = (bf16[256,512]{1,0:T(8,128)(2,1)}, bf16[256,512]{1,0:T(8,128)(2,1)}, u32[]{:S(2)}, u32[]{:S(2)}) collective-permute-start(bf16[256,512]{1,0:T(8,128)(2,1)} %bitcast.278), channel_id=1, source_target_pairs={{0,1},{1,2},{2,3},{3,0},{4,5},{5,6},{6,7},{7,4},{8,9},{9,10},{10,1... | collective-permute-start | bytes 786440 | tf_op jit(solution)/shard_map/ppermute | solution.py:253
  856.7 33.7 %collective-permute-start.46 = (bf16[256,512]{1,0:T(8,128)(2,1)}, bf16[256,512]{1,0:T(8,128)(2,1)}, u32[]{:S(2)}, u32[]{:S(2)}) collective-permute-start(bf16[256,512]{1,0:T(8,128)(2,1)} %bitcast.94), channel_id=1, source_target_pairs={{0,2},{1,3},{2,0},{3,1},{4,6},{5,7},{6,4},{7,5},{8,10},{9,11},{10,... | collective-permute-start | bytes 786440 | tf_op jit(solution)/shard_map/ppermute | solution.py:253
  867.1 24.4 %collective-permute-start.47 = (bf16[256,512]{1,0:T(8,128)(2,1)}, bf16[256,512]{1,0:T(8,128)(2,1)}, u32[]{:S(2)}, u32[]{:S(2)}) collective-permute-start(bf16[256,512]{1,0:T(8,128)(2,1)} %bitcast.96), channel_id=1, source_target_pairs={{0,3},{1,0},{2,1},{3,2},{4,7},{5,4},{6,5},{7,6},{8,11},{9,8},{10,9... | collective-permute-start | bytes 786440 | tf_op jit(solution)/shard_map/ppermute | solution.py:253
  (57 other events, 652.3 us)
Sparse Core Ops, SparseCore 0:
  49.6 79.6 all-gather.3
  268.3 83.1 all-gather.5
  353.1 79.2 all-gather.7
  466.9 75.2 reduce-scatter.5
  544.5 77.2 reduce-scatter.3
  708.4 78.0 reduce-scatter.7

commit v2 on v1

--- a/solution.py
+++ b/solution.py
@@ -121,30 +121,6 @@
     top = jnp.max(scores, axis=0, keepdims=True)
     weights = jnp.exp(scores - top)
     return weights, jnp.sum(weights, axis=0, keepdims=True)
-
-
-def attend_kernel(rows, widest, q_in, k_in, v_in, cos, s_low, s_high, starts, q_out, k_out, v_out, o_out, vt):
-    seq_len = q_in.shape[0]
-    cosine, sine_low, sine_high = cos[...], s_low[...], s_high[...]
-    q_out[...] = turn(q_in[...], cosine, sine_low, sine_high).astype(BF16)
-    k_out[...] = turn(k_in[...], cosine, sine_low, sine_high).astype(BF16)
-    v_low = v_in[...].astype(BF16)
-    v_out[...] = v_low
-    vt[...] = v_low.astype(F32).T.astype(BF16)
-    for block in range(seq_len // rows):
-        here = slice(block * rows, (block + 1) * rows)
-        first, last = key_range(block, rows, widest)
-        query_cols = (q_out[here, :].astype(F32) * HEAD**-0.5).T.astype(BF16)
-        head_of = lax.broadcasted_iota(jnp.int32, query_cols.shape, 0) // HEAD
-        parts = []
-        for head in range(LANES // HEAD):
-            own_cols = jnp.where(head_of == head, query_cols, jnp.zeros_like(query_cols))
-            weights, total = seen_weights(
-                k_out[first:last, :], own_cols, starts[:, here], first, block * rows
-            )
-            part = dot(vt[head * HEAD : (head + 1) * HEAD, first:last], weights.astype(BF16), NN)
-            parts.append(part / total)
-        o_out[here, :] = jnp.concatenate(parts, axis=0).T.astype(BF16)
 
 
 def attend_back_kernel(
@@ -196,29 +172,6 @@
     b_out[...] = jnp.sum(g_out[...].astype(F32), axis=1, keepdims=True)
 
 
-def attend_forward(projected, tables, starts, widest):
-    seq_len, width = projected.shape[0], projected.shape[1] // 3
-    pairs = width // LANES
-    rows = min(256, seq_len)
-    column = lambda part: pl.BlockSpec((seq_len, LANES), lambda i, part=part: (0, part * pairs + i))
-    whole = lambda shape: pl.BlockSpec(shape, lambda i: (0, 0))
-    out = jax.ShapeDtypeStruct((seq_len, width), BF16)
-    return pl.pallas_call(
-        functools.partial(attend_kernel, rows, widest),
-        grid=(pairs,),
-        in_specs=[column(0), column(1), column(2)]
-        + [whole((seq_len, LANES))] * 3
-        + [whole((1, seq_len))],
-        out_specs=[column(0)] * 4,
-        out_shape=[out] * 4,
-        scratch_shapes=[pltpu.VMEM((LANES, seq_len), BF16)],
-        compiler_params=pltpu.CompilerParams(vmem_limit_bytes=48 * 2**20),
-        cost_estimate=pl.CostEstimate(
-            flops=4 * seq_len * seq_len * width, bytes_accessed=20 * seq_len * width, transcendentals=0
-        ),
-    )(projected, projected, projected, *tables, starts)
-
-
 def attend_backward(queries, key_vals, value_rows, grad_attended, tables, starts, widest):
     seq_len, width = queries.shape
     pairs = width // LANES
@@ -249,21 +202,529 @@
     )(queries, key_vals, value_rows, grad_attended, *tables, starts)
 
 
+def xor(value, mask):
+    bit = 1
+    while bit <= mask:
+        if mask & bit:
+            value = value + bit * (1 - 2 * lax.rem(value // bit, 2))
+        bit *= 2
+    return value
+
+
+class Places:
+    def __init__(self, n_fsdp, n_tp):
+        self.n_fsdp, self.n_tp = n_fsdp, n_tp
+        self.f, self.t = lax.axis_index("fsdp"), lax.axis_index("tp")
+        self.chip, self.core = self.f // 2, lax.rem(self.f, 2)
+
+    def near_f(self, k):
+        return xor(self.chip, k) * 2 + self.core
+
+    def near(self, k):
+        return (self.near_f(k), self.t)
+
+    def sibling(self):
+        return (self.chip * 2 + 1 - self.core, self.t)
+
+    def along(self, t):
+        return (self.f, t)
+
+    def greet(self):
+        barrier = pltpu.get_barrier_semaphore()
+        partners = [self.near(k) for k in range(1, self.n_fsdp // 2)] + [self.sibling()]
+        partners += [self.along(lax.rem(self.t + k, self.n_tp)) for k in range(1, self.n_tp)]
+        for partner in partners:
+            pl.semaphore_signal(barrier, inc=1, device_id=partner, device_id_type=MESH)
+        pl.semaphore_wait(barrier, len(partners))
+
+
+def send(src, dst, send_sem, recv_sem, device):
+    return pltpu.make_async_remote_copy(
+        src_ref=src,
+        dst_ref=dst,
+        send_sem=send_sem,
+        recv_sem=recv_sem,
+        device_id=device,
+        device_id_type=MESH,
+    )
+
+
+class Line:
+    def __init__(self, at, own, slots, send_sems, recv_sems):
+        self.at, self.own, self.slots = at, own, slots
+        self.send_sems, self.recv_sems = send_sems, recv_sems
+
+    def copy(self, slot, way, first):
+        at = self.at
+        return send(
+            self.own if first else self.slots.at[slot],
+            self.slots.at[slot],
+            self.send_sems.at[way, slot],
+            self.recv_sems.at[slot],
+            at.along(at.t + 1 - 2 * way),
+        )
+
+    def start(self):
+        at = self.at
+        pl.when(at.t < at.n_tp - 1)(lambda: self.copy(at.t, 0, True).start())
+        pl.when(at.t > 0)(lambda: self.copy(at.t, 1, True).start())
+
+    def step(self, s):
+        at = self.at
+
+        @pl.when(at.t >= s)
+        def _():
+            self.copy(at.t - s, 0, False).wait_recv()
+            pl.when(at.t < at.n_tp - 1)(lambda: self.copy(at.t - s, 0, False).start())
+
+        @pl.when(at.t + s < at.n_tp)
+        def _():
+            self.copy(at.t + s, 1, False).wait_recv()
+            pl.when(at.t > 0)(lambda: self.copy(at.t + s, 1, False).start())
+
+    def finish(self):
+        at = self.at
+        for s in range(at.n_tp):
+            pl.when((at.t >= s) & (at.t < at.n_tp - 1))(
+                lambda s=s: self.copy(at.t - s, 0, s == 0).wait_send()
+            )
+            pl.when((at.t + s < at.n_tp) & (at.t > 0))(
+                lambda s=s: self.copy(at.t + s, 1, s == 0).wait_send()
+            )
+
+
+class Shards:
+    def __init__(self, at, own, whole, by_rows, near_sems, sib_sems, index):
+        self.at, self.own, self.whole, self.by_rows = at, own, whole, by_rows
+        self.near_sems, self.sib_sems, self.index = near_sems, sib_sems, index
+        self.half = at.n_fsdp // 2
+        self.relay = at.n_fsdp == 8
+        self.direct = [1, 2] if self.relay else list(range(1, self.half))
+
+    def slot(self, f, part=None):
+        if self.by_rows:
+            rows = self.whole.shape[0] // self.at.n_fsdp
+            first = f * rows
+            if part is not None:
+                rows = rows // 2
+                first = first + part * rows
+            return self.whole.at[pl.ds(pl.multiple_of(first, rows), rows), :]
+        width = self.whole.shape[1] // self.at.n_fsdp
+        columns = pl.ds(pl.multiple_of(f * width, LANES), width)
+        if part is None:
+            return self.whole.at[:, columns]
+        rows = self.whole.shape[0] // 2
+        return self.whole.at[pl.ds(part * rows, rows), columns]
+
+    def near_copy(self, k):
+        return send(
+            self.own,
+            self.slot(self.at.f),
+            self.near_sems.at[self.index, 0, k],
+            self.near_sems.at[self.index, 1, k],
+            self.at.near(k),
+        )
+
+    def start(self):
+        for k in self.direct:
+            self.near_copy(k).start()
+        self.sib_copy(0).start()
+
+    def arrived(self, k):
+        slot = self.slot(self.at.near_f(k))
+        send(
+            slot,
+            slot,
+            self.near_sems.at[self.index, 0, k],
+            self.near_sems.at[self.index, 1, k],
+            self.at.near(k),
+        ).wait_recv()
+
+    def relay_copy(self, part):
+        source, target = (1, 2) if part == 0 else (2, 1)
+        slot = self.slot(self.at.near_f(source), part)
+        return send(
+            slot,
+            slot,
+            self.near_sems.at[self.index, 0, 3 + part],
+            self.near_sems.at[self.index, 1, 3 + part],
+            self.at.near(target),
+        )
+
+    def sib_copy(self, k):
+        f = self.at.near_f(k)
+        return send(
+            self.own if k == 0 else self.slot(f),
+            self.slot(f),
+            self.sib_sems.at[self.index, 0, k],
+            self.sib_sems.at[self.index, 1, k],
+            self.at.sibling(),
+        )
+
+    def pass_on(self):
+        for k in self.direct:
+            self.arrived(k)
+            if self.relay:
+                self.relay_copy(k - 1).start()
+        for k in self.direct:
+            self.sib_copy(k).start()
+
+    def pass_last(self):
+        if self.relay:
+            for part in range(2):
+                slot = self.slot(self.at.near_f(3), part)
+                send(
+                    slot,
+                    slot,
+                    self.near_sems.at[self.index, 0, 3 + part],
+                    self.near_sems.at[self.index, 1, 3 + part],
+                    self.at.near(2 - part),
+                ).wait_recv()
+            self.sib_copy(3).start()
+
+    def complete(self):
+        for k in range(self.half):
+            f = xor(self.at.chip, k) * 2 + 1 - self.at.core
+            slot = self.slot(f)
+            send(
+                slot,
+                slot,
+                self.sib_sems.at[self.index, 0, k],
+                self.sib_sems.at[self.index, 1, k],
+                self.at.sibling(),
+            ).wait_recv()
+
+    def finish(self):
+        for k in self.direct:
+            self.near_copy(k).wait_send()
+        if self.relay:
+            for part in range(2):
+                self.relay_copy(part).wait_send()
+        for k in range(self.half):
+            self.sib_copy(k).wait_send()
+
+
+def norm_rows(values, gain_row, shift_row):
+    average = jnp.mean(values, axis=-1, keepdims=True)
+    centred = values - average
+    variance = jnp.mean(centred * centred, axis=-1, keepdims=True)
+    return centred * lax.rsqrt(variance + NORM_EPS) * gain_row + shift_row
+
+
+def front_kernel(
+    sizes, widest,
+    tok, cot, wq, wo, wgu, wd, tile, cos, s_low, s_high, starts,
+    one, q_out, k_out, v_out, resid, two, rows_out, att_out, cot_all, wq_all, wo_all, wgu_all, wd_all,
+    toks, wq_v, wo_v, att, heads, vt, small, bias,
+    tok_send, tok_recv, cot_send, cot_recv, near_sems, sib_sems, wz_sems, small_sems,
+    swap_send, swap_recv, local_sems,
+):
+    n_fsdp, n_tp = sizes
+    half = n_fsdp // 2
+    at = Places(n_fsdp, n_tp)
+    slab, model = tok.shape
+    width = q_out.shape[1]
+    each = wo.shape[0]
+    at.greet()
+
+    line = Line(at, tok, toks, tok_send, tok_recv)
+    line.start()
+    grads = Line(at, cot, cot_all, cot_send, cot_recv)
+    weights = [
+        Shards(at, wq, wq_all, True, near_sems, sib_sems, 0),
+        None,
+        Shards(at, wgu, wgu_all, True, near_sems, sib_sems, 2),
+        Shards(at, wd, wd_all, False, near_sems, sib_sems, 3),
+    ]
+    weights[1] = Shards(at, None, wo_all, False, near_sems, sib_sems, 1)
+    weights[1].own = weights[1].slot(at.f)
+    weights[0].start()
+
+    own_columns = pl.ds(pl.multiple_of(at.f * (model // n_fsdp), LANES), model // n_fsdp)
+
+    def wo_rows(t):
+        return wo_all.at[pl.ds(pl.multiple_of(t * each, each), each), own_columns]
+
+    def wo_copy(k):
+        return send(wo, wo_rows(at.t), wz_sems.at[0, k], wz_sems.at[1, k], at.along(lax.rem(at.t + k, n_tp)))
+
+    for k in range(1, n_tp):
+        wo_copy(k).start()
+    own_copies = [
+        pltpu.make_async_copy(tok, toks.at[at.t], local_sems.at[0]),
+        pltpu.make_async_copy(wq, weights[0].slot(at.f), local_sems.at[1]),
+        pltpu.make_async_copy(wo, wo_rows(at.t), local_sems.at[2]),
+        pltpu.make_async_copy(wgu, weights[2].slot(at.f), local_sems.at[3]),
+        pltpu.make_async_copy(wd, weights[3].slot(at.f), local_sems.at[4]),
+        pltpu.make_async_copy(cot, cot_all.at[at.t], local_sems.at[5]),
+    ]
+    for copy in own_copies:
+        copy.start()
+
+    small[at.t, at.f] = tile[...]
+    mine = small.at[at.t, at.f]
+    to_sib = send(mine, mine, small_sems.at[0, 0], small_sems.at[1, 0], at.sibling())
+    to_sib.start()
+    to_sib.wait()
+    pair = small.at[at.t, pl.ds(at.chip * 2, 2)]
+    to_near = [
+        send(pair, pair, small_sems.at[0, k], small_sems.at[1, k], at.near(k)) for k in range(1, half)
+    ]
+    for copy in to_near:
+        copy.start()
+    for k in range(1, half):
+        to_near[k - 1].wait_send()
+        came = small.at[at.t, pl.ds(xor(at.chip, k) * 2, 2)]
+        send(came, came, small_sems.at[0, k], small_sems.at[1, k], at.near(k)).wait_recv()
+    plane = small.at[at.t]
+    to_line = [
+        send(
+            plane, plane, small_sems.at[0, half + k], small_sems.at[1, half + k],
+            at.along(lax.rem(at.t + k, n_tp)),
+        )
+        for k in range(1, n_tp)
+    ]
+    for copy in to_line:
+        copy.start()
+    for k in range(1, n_tp):
+        to_line[k - 1].wait_send()
+        came = small.at[lax.rem(at.t + n_tp - k, n_tp)]
+        send(
+            came, came, small_sems.at[0, half + k], small_sems.at[1, half + k],
+            at.along(lax.rem(at.t + k, n_tp)),
+        ).wait_recv()
+    lanes_each = model // (n_fsdp * n_tp)
+    group = LANES // lanes_each
+    for i in range(model // LANES):
+        total = jnp.zeros((8, LANES), F32)
+        for j in range(group):
+            linear = i * group + j
+            total = total + pltpu.roll(small[linear % n_tp, linear // n_tp], j * lanes_each, 1)
+        rows_out[:, i * LANES : (i + 1) * LANES] = total
+    for i in range(width // LANES):
+        total = jnp.zeros((8, LANES), F32)
+        for j in range(group):
+            total = total + pltpu.roll(small[at.t, i * group + j], j * lanes_each, 1)
+        bias[:, i * LANES : (i + 1) * LANES] = total
+    own_copies[0].wait()
+
+    def normalise(slot):
+        step = 32
+
+        def some(i, carry):
+            here = pl.ds(pl.multiple_of(i * step, step), step)
+            one[slot, here, :] = norm_rows(
+                toks[slot, here, :].astype(F32), rows_out[0:1, :], rows_out[2:3, :]
+            ).astype(BF16)
+            return carry
+
+        lax.fori_loop(0, slab // step, some, 0)
+
+    wide = 256
+
+    def project(slot):
+        here = pl.ds(pl.multiple_of(slot * slab, slab), slab)
+        for part, out in enumerate((q_out, k_out, v_out)):
+
+            def some(i, carry, part=part, out=out):
+                values = dot(
+                    one[slot], wq_v[:, pl.ds(pl.multiple_of(part * width + i * wide, wide), wide)], NN
+                )
+                for j in range(wide // LANES):
+                    lanes = pl.ds(pl.multiple_of(i * wide + j * LANES, LANES), LANES)
+                    piece = values[:, j * LANES : (j + 1) * LANES] + bias[4 + part : 5 + part, lanes]
+                    if part < 2:
+                        piece = turn(piece, cos[here, :], s_low[here, :], s_high[here, :])
+                    out[here, lanes] = piece.astype(BF16)
+                return carry
+
+            lax.fori_loop(0, width // wide, some, 0)
+
+    def each_from(first, last, work):
+        def some(i, carry):
+            s = (i + 1) // 2
+            slot = at.t + s * (2 * lax.rem(i, 2) - 1)
+            pl.when((slot >= 0) & (slot < n_tp))(lambda: work(slot))
+            return carry
+
+        lax.fori_loop(max(0, 2 * first - 1), 2 * last - 1, some, 0)
+
+    normalise(at.t)
+    for s in range(1, n_tp - 1):
+        line.step(s)
+        if s == 1:
+            weights[0].pass_on()
+            own_copies[2].wait()
+            for k in range(1, n_tp):
+                wo_copy(k).wait_send()
+                came = wo_rows(lax.rem(at.t + n_tp - k, n_tp))
+                send(came, came, wz_sems.at[0, k], wz_sems.at[1, k], at.along(at.t)).wait_recv()
+            weights[1].start()
+        each_from(s, s + 1, normalise)
+    weights[0].pass_last()
+    own_copies[1].wait()
+    weights[0].complete()
+    load = pltpu.make_async_copy(wq_all, wq_v, local_sems.at[6])
+    load.start()
+    load.wait()
+    each_from(0, n_tp - 1, project)
+    weights[1].pass_on()
+    weights[2].start()
+    weights[3].start()
+    line.step(n_tp - 1)
+    grads.start()
+    each_from(n_tp - 1, n_tp, normalise)
+    each_from(n_tp - 1, n_tp, project)
+
+    def swap_copy(i, k):
+        lanes = pl.ds(pl.multiple_of(i * LANES, LANES), LANES)
+        columns = pl.ds(pl.multiple_of(at.t * width + i * LANES, LANES), LANES)
+        other = lax.rem(at.t + k, n_tp)
+        return send(
+            heads.at[other, :, lanes], att.at[:, columns],
+            swap_send.at[i, k], swap_recv.at[i, k], at.along(other),
+        )
+
+    def some_heads(i, carry):
+        lanes = pl.ds(pl.multiple_of(i * LANES, LANES), LANES)
+        attend(widest, q_out, k_out, v_out, starts, heads, vt, lanes, slab)
+        for k in range(1, n_tp):
+            swap_copy(i, k).start()
+        columns = pl.ds(pl.multiple_of(at.t * width + i * LANES, LANES), LANES)
+        att[:, columns] = heads[at.t, :, lanes]
+        return carry
+
+    lax.fori_loop(0, width // LANES, some_heads, 0)
+    weights[1].pass_last()
+    weights[1].complete()
+    load = pltpu.make_async_copy(wo_all, wo_v, local_sems.at[7])
+    load.start()
+
+    def took_heads(i, carry):
+        for k in range(1, n_tp):
+            swap_copy(i, k).wait_send()
+            source = lax.rem(at.t + n_tp - k, n_tp)
+            came = att.at[:, pl.ds(pl.multiple_of(source * width + i * LANES, LANES), LANES)]
+            send(came, came, swap_send.at[i, k], swap_recv.at[i, k], at.along(source)).wait_recv()
+        return carry
+
+    lax.fori_loop(0, width // LANES, took_heads, 0)
+    grads.step(1)
+    keep = pltpu.make_async_copy(att, att_out, local_sems.at[8])
+    keep.start()
+    load.wait()
+
+    def out_columns(i, carry):
+        here = pl.ds(pl.multiple_of(i * wide, wide), wide)
+        resid[:, here] = toks[at.t, :, here].astype(F32) + dot(att[...], wo_v[:, here], NN)
+        return carry
+
+    lax.fori_loop(0, model // wide, out_columns, 0)
+
+    def second_norm(i, carry):
+        here = pl.ds(pl.multiple_of(i * 32, 32), 32)
+        two[here, :] = norm_rows(resid[here, :], rows_out[1:2, :], rows_out[3:4, :]).astype(BF16)
+        return carry
+
+    lax.fori_loop(0, slab // 32, second_norm, 0)
+
+    weights[2].pass_on()
+    weights[3].pass_on()
+    for s in range(2, n_tp):
+        grads.step(s)
+    weights[2].pass_last()
+    weights[3].pass_last()
+    for copy in own_copies[3:]:
+        copy.wait()
+    weights[2].complete()
+    weights[3].complete()
+    keep.wait()
+    line.finish()
+    grads.finish()
+    for weight in weights:
+        weight.finish()
+
+
+def attend(widest, q_in, k_in, v_in, starts, heads, vt, lanes, slab):
+    seq_len = q_in.shape[0]
+    rows = min(256, seq_len)
+    vt[...] = v_in[:, lanes].astype(F32).T.astype(BF16)
+    for block in range(seq_len // rows):
+        here = slice(block * rows, (block + 1) * rows)
+        first, last = key_range(block, rows, widest)
+        query_cols = (q_in[here, lanes].astype(F32) * HEAD**-0.5).T.astype(BF16)
+        head_of = lax.broadcasted_iota(jnp.int32, query_cols.shape, 0) // HEAD
+        parts = []
+        for head in range(LANES // HEAD):
+            own_cols = jnp.where(head_of == head, query_cols, jnp.zeros_like(query_cols))
+            weights, total = seen_weights(
+                k_in[first:last, lanes], own_cols, starts[:, here], first, block * rows
+            )
+            part = dot(vt[head * HEAD : (head + 1) * HEAD, first:last], weights.astype(BF16), NN)
+            parts.append(part / total)
+        found = jnp.concatenate(parts, axis=0).T.astype(BF16)
+        for j in range(max(1, rows // slab)):
+            count = min(slab, rows)
+            row = block * rows + j * count
+            heads[row // slab, row % slab : row % slab + count, lanes] = found[
+                j * count : (j + 1) * count, :
+            ]
+
+
+def front(sizes, widest, tok, cot, wq, wo, wgu, wd, tile, tables, starts):
+    n_fsdp, n_tp = sizes
+    half = n_fsdp // 2
+    slab, model = tok.shape
+    seq_len = slab * n_tp
+    width = wq.shape[1] // 3
+    hidden = wd.shape[0]
+    hbm = pl.BlockSpec(memory_space=pl.ANY)
+    vmem = pl.BlockSpec(memory_space=pltpu.VMEM)
+    shape = jax.ShapeDtypeStruct
+    outs = [
+        (shape((n_tp, slab, model), BF16), vmem),
+        (shape((seq_len, width), BF16), vmem),
+        (shape((seq_len, width), BF16), vmem),
+        (shape((seq_len, width), BF16), vmem),
+        (shape((slab, model), F32), vmem),
+        (shape((slab, model), BF16), vmem),
+        (shape((8, model), F32), vmem),
+        (shape((slab, model), BF16), hbm),
+        (shape((n_tp, slab, model), BF16), hbm),
+        (shape((model, 3 * width), BF16), hbm),
+        (shape((model, model), BF16), hbm),
+        (shape((model, 2 * hidden), BF16), hbm),
+        (shape((hidden, model), BF16), hbm),
+    ]
+    dma = pltpu.SemaphoreType.DMA
+    pairs = width // LANES
+    return pl.pallas_call(
+        functools.partial(front_kernel, sizes, widest),
+        in_specs=[hbm] * 6 + [vmem] * 5,
+        out_specs=[spec for _, spec in outs],
+        out_shape=[out for out, _ in outs],
+        scratch_shapes=[
+            pltpu.VMEM((n_tp, slab, model), BF16),
+            pltpu.VMEM((model, 3 * width), BF16),
+            pltpu.VMEM((model, model), BF16),
+            pltpu.VMEM((slab, model), BF16),
+            pltpu.VMEM((n_tp, slab, width), BF16),
+            pltpu.VMEM((LANES, seq_len), BF16),
+            pltpu.VMEM((n_tp, n_fsdp, 8, LANES), F32),
+            pltpu.VMEM((8, width), F32),
+            dma((2, n_tp)), dma((n_tp,)), dma((2, n_tp)), dma((n_tp,)),
+            dma((4, 2, half + 1)), dma((4, 2, half)), dma((2, n_tp)), dma((2, half + n_tp)),
+            dma((pairs, n_tp)), dma((pairs, n_tp)), dma((9,)),
+        ],
+        compiler_params=pltpu.CompilerParams(
+            collective_id=1, has_side_effects=True, vmem_limit_bytes=60 * 2**20
+        ),
+        cost_estimate=pl.CostEstimate(flops=10**11, bytes_accessed=10**8, transcendentals=0),
+    )(tok, cot, wq, wo, wgu, wd, tile, *tables, starts)
+
+
 def hop(values, axis, size, partner):
     return lax.ppermute(values, axis, [(i, partner(i)) for i in range(size)])
-
-
-def gather_fsdp(own, size):
-    me = lax.axis_index("fsdp")
-    near = [own] + [
-        hop(own, "fsdp", size, lambda i, k=k: i ^ (2 * k)) for k in range(1, size // 2)
-    ]
-    far = [hop(block, "fsdp", size, lambda i: i ^ 1) for block in near]
-    whole = jnp.zeros((size,) + own.shape, own.dtype)
-    for k in range(size // 2):
-        whole = lax.dynamic_update_index_in_dim(whole, near[k], me ^ (2 * k), 0)
-        whole = lax.dynamic_update_index_in_dim(whole, far[k], me ^ (2 * k) ^ 1, 0)
-    return whole
 
 
 def scatter_fsdp(blocks, size):
@@ -291,16 +752,6 @@
     return got
 
 
-def gather_tp_small(own, size):
-    me = lax.axis_index("tp")
-    whole = jnp.zeros((size,) + own.shape, own.dtype)
-    whole = lax.dynamic_update_index_in_dim(whole, own, me, 0)
-    for k in range(1, size):
-        came = hop(own, "tp", size, lambda i, k=k: (i + k) % size)
-        whole = lax.dynamic_update_index_in_dim(whole, came, (me + size - k) % size, 0)
-    return whole
-
-
 def gather_rows(values):
     return lax.all_gather(values, "tp", axis=0, tiled=True)
 
@@ -319,25 +770,6 @@
     local_width = w_qkv.shape[2]
     hidden_width = w_gate_up.shape[2]
     part_rows = w_qkv.shape[0]
-
-    tile = jnp.concatenate([ln_gains, ln_shifts, b_qkv.astype(F32), jnp.zeros((1, small), F32)], 0)
-    tile = jnp.pad(tile, ((0, 0), (0, LANES - small)))
-    got = exchange(tile[None], sizes, False, 1)
-    rows_all = got[:, :, :small]
-    norm_rows = rows_all[:, :4].transpose(1, 0, 2).reshape(4, model_width)
-    gains_all, shifts_all = norm_rows[:2], norm_rows[2:]
-    bias = lax.dynamic_index_in_dim(rows_all.reshape(n_fsdp, n_tp, 8, small), at_tp, 1, keepdims=False)
-    bias = bias[:, 4:7].transpose(1, 0, 2).reshape(1, 3 * local_width)
-
-    qkv_all = gather_fsdp(w_qkv.reshape(part_rows, 3 * local_width), n_fsdp).reshape(
-        model_width, 3 * local_width
-    )
-    out_part = gather_tp_small(w_out.T, n_tp).transpose(1, 0, 2).reshape(part_rows, model_width)
-    out_all = gather_fsdp(out_part, n_fsdp).reshape(model_width, model_width)
-    gu_all = gather_fsdp(w_gate_up.reshape(part_rows, 2 * hidden_width), n_fsdp).reshape(
-        model_width, 2 * hidden_width
-    )
-    down_all = gather_fsdp(w_down.T, n_fsdp).reshape(model_width, hidden_width)
 
     length_row = lengths[0]
     doc_ends = jnp.cumsum(length_row)
@@ -356,28 +788,28 @@
     starts_row = starts.reshape(1, seq_len).astype(jnp.int32)
     widest = seq_len // 2
 
+    tile = jnp.concatenate([ln_gains, ln_shifts, b_qkv.astype(F32), jnp.zeros((1, small), F32)], 0)
+    tile = jnp.pad(tile, ((0, 0), (0, LANES - small)))
     token_rows = tokens.astype(F32)
-    normed_one = layer_norm(token_rows, gains_all[0], shifts_all[0])
-    full_one = gather_rows(normed_one.astype(BF16))
-    projected = dot(full_one, qkv_all, NN) + bias
-    queries, key_vals, value_rows, attended = attend_forward(projected, tables, starts_row, widest)
-    attended_own = (
-        swap_tp(attended.reshape(n_tp, slab_rows, local_width), n_tp)
-        .transpose(1, 0, 2)
-        .reshape(slab_rows, model_width)
+    (
+        full_one, queries, key_vals, value_rows, residual, normed_two, norm_rows_all, attended_own,
+        grad_branch, qkv_all, out_all, gu_all, down_all,
+    ) = front(
+        sizes, widest, tokens, cotangent, w_qkv.reshape(part_rows, 3 * local_width), w_out,
+        w_gate_up.reshape(part_rows, 2 * hidden_width), w_down, tile, tables, starts_row,
     )
-    residual = token_rows + dot(attended_own, out_all, NT)
-
-    normed_two = layer_norm(residual, gains_all[1], shifts_all[1])
-    full_two = gather_rows(normed_two.astype(BF16))
-    grad_branch = gather_rows(cotangent)
+    full_one = full_one.reshape(seq_len, model_width)
+    grad_branch = grad_branch.reshape(seq_len, model_width)
+    gains_all, shifts_all = norm_rows_all[0:2], norm_rows_all[2:4]
+
+    full_two = gather_rows(normed_two)
     gate_up = dot(full_two, gu_all, NN)
     gate, up = gate_up[:, :hidden_width], gate_up[:, hidden_width:]
     hidden_low = swiglu(gate, up).astype(BF16)
-    branch = reduce_rows(dot(hidden_low, down_all, NT))
+    branch = reduce_rows(dot(hidden_low, down_all, NN))
     result = (residual + branch).astype(BF16)
     grad_out = cotangent.astype(F32)
-    grad_hidden = dot(grad_branch, down_all, NN)
+    grad_hidden = dot(grad_branch, down_all, NT)
     _, swiglu_pull = jax.vjp(swiglu, gate, up)
     grad_gate, grad_up = swiglu_pull(grad_hidden)
     grad_gate_up = jnp.concatenate([grad_gate, grad_up], axis=1).astype(BF16)
@@ -392,7 +824,7 @@
 
     grad_attn = grad_residual.astype(BF16)
     grad_o = dot(grad_attn, attended_own, TN).astype(BF16)
-    grad_attended_own = dot(grad_attn, out_all, NN).astype(BF16)
+    grad_attended_own = dot(grad_attn, out_all, NT).astype(BF16)
     grad_attended = swap_tp(
         grad_attended_own.reshape(slab_rows, n_tp, local_width).transpose(1, 0, 2), n_tp
     ).reshape(seq_len, local_width)

time: 937 us -> 814 us (0.87)
  Pallas kernels: 79.8 us -> 241 us
  local copies, waits for them, and re-layouts: 243 us -> 93.8 us
  waiting for transfers between devices: 327 us -> 252 us
  starting transfers between devices: 64.2 us -> 32 us
  matrix products: 139 us -> 119 us
    pallas_call x1, Pallas kernels: 18.3 us -> 204 us  [front(): pl.pallas_call(functools.partial(front_kernel, sizes, widest), in_specs=[...]
    ppermute x56 -> x22, waiting for transfers between devices: 236 us -> 89.7 us  [hop(): return lax.ppermute(values, axis, [(i, partner(i)) for i in range(size)])]
    dynamic_update_slice x36 -> x0, local copies, waits for them, and re-layouts: 80.3 us -> none  [the longest x3 25.4 us: gather_tp_small(): lax.dynamic_update_index_in_dim(whole, came, (me + size - k) % size, 0)]
    all_gather x3 -> x1, waiting for transfers between devices: 23.1 us -> 80.6 us  [gather_rows(): return lax.all_gather(values, 'tp', axis=0, tiled=True)]
    broadcast_in_dim x20 -> x0, local copies, waits for them, and re-layouts: 40.2 us -> none  [the longest x4 13 us: gather_fsdp(): whole = jnp.zeros((size,) + own.shape, own.dtype)]
    ppermute x56 -> x22, starting transfers between devices: 63.9 us -> 31.5 us  [hop(): return lax.ppermute(values, axis, [(i, partner(i)) for i in range(size)])]
    pallas_call x2 -> x1, Pallas kernels: 36.3 us -> 11.3 us  [exchange(): pl.pallas_call(functools.partial(exchange_kernel, sizes, scatter), out_sh...]
    dot_general x12 -> x10, matrix products: 139 us -> 119 us  [dot(): return lax.dot_general(left, right, dims, preferred_element_type=F32)]
  transfers between devices with their start and end apart: 62 -> 26, of which waited for: 18 -> 13; matrix products, arithmetic and copies ran while one was open for 40% -> 22% of each run, Pallas kernels for 7% -> 3%
where the time goes in v2:
time: 814 us; the launch traced here: 805 us
  waiting for transfers between devices  252 us (31%)
  Pallas kernels  241 us (30%)
  matrix products  119 us (15%)
  local copies, waits for them, and re-layouts  93.8 us (12%)
  other arithmetic  52.8 us (6%)
  starting transfers between devices  32 us (4%)
  between operations  14.6 us (2%)
    pallas_call x1, Pallas kernels, front(): pl.pallas_call(functools.partial(front_kernel, sizes, widest), in_specs=[...  204 us
    dot_general x10, matrix products, dot(): return lax.dot_general(left, right, dims, preferred_element_type=F32)  119 us
    ppermute x22, waiting for transfers between devices, hop(): return lax.ppermute(values, axis, [(i, partner(i)) for i in range(size)])  89.7 us
    reduce_scatter x3, waiting for transfers between devices, reduce_rows(): lax.psum_scatter(values.astype(BF16), 'tp', scatter_dimension=0, tiled=True)  81.8 us
    all_gather x1, waiting for transfers between devices, gather_rows(): return lax.all_gather(values, 'tp', axis=0, tiled=True)  80.6 us
    unnamed x64, local copies, waits for them, and re-layouts  33.3 us
    ppermute x22, starting transfers between devices, hop(): return lax.ppermute(values, axis, [(i, partner(i)) for i in range(size)])  31.5 us
    pallas_call x1, Pallas kernels, attend_backward(): pl.pallas_call(functools.partial(attend_back_kernel, rows, widest), grid=...  25.3 us
  transfers between devices with their start and end apart: 26, of which 13 were waited for; matrix products, arithmetic and copies ran while one was open for 22% of the time, Pallas kernels for 3%

profile of v2, /device:TPU:0, one launch (start us, length us, event | category | flops | bytes accessed | tf_op | source)
XLA Modules:
  0.0 805.0 jit_solution(10655362203117714061)
XLA Ops:
  14.9 3.2 fusion.32
  18.1 204.5 %shard_map.169 = (bf16[4,256,2048]{2,1,0:T(8,128)(2,1)}, bf16[1024,512]{1,0:T(8,128)(2,1)}, bf16[1024,512]{1,0:T(8,128)(2,1)}, bf16[1024,512]{1,0:T(8,128)(2,1)}...) custom-call(bf16[256,2048]{1,0:T(8,128)(2,1)} %tok.1, ...), custom_call_target="tpu_custom_call" | custom-call | flops 99999997952 | bytes 100000000 | tf_op jit(solution)/shard_map/pallas_call | solution.py:701
  222.8 80.6 %all-gather.2.cloned.1.call-done = bf16[1024,2048]{1,0:T(8,128)(2,1)} async-done(((bf16[256,2048]{1,0:T(8,128)(2,1)}), bf16[1024,2048]{1,0:T(8,128)(2,1)}) %all-gather.2.cloned.1.call-update) | async-done | bytes 4194320 | tf_op jit(solution)/shard_map/all_gather | solution.py:756
  303.4 18.9 %fusion.48 = f32[1024,2816]{1,0:T(8,128)} fusion(bf16[1024,2048]{1,0:T(8,128)(2,1)} %all-gather.2.cloned.1.call-done, bf16[2048,2816]{1,0:T(8,128)(2,1)} %get-tuple-element.26), kind=kOutput, calls=%fused_computation.141 | convolution fusion | flops 11811160064 | bytes 27262976 | tf_op jit(solution)/shard_map/dot_general | solution.py:23
  322.3 13.6 %fusion.5 = (bf16[1024,1408]{1,0:T(8,128)(2,1)}, bf16[1024,1408]{1,0:T(8,128)(2,1)}, bf16[1024,1408]{1,0:T(8,128)(2,1)}) fusion(f32[1024,2816]{1,0:T(8,128)} %fusion.48, bf16[1024,2048]{1,0:T(8,128)(2,1)S(1)} %bitcast.168, bf16[1408,2048]{1,0:T(8,128)(2,1)S(1)} %bitcast.170), kind=kOutput, calls=%fused_computation.13 | convolution fusion | flops 5928648704 | bytes 30146560 | tf_op jit(solution)/shard_map/dot_general | solution.py:23
  336.0 18.0 %convolution_convert_fusion.4 = bf16[1024,2048]{1,0:T(8,128)(2,1)} fusion(bf16[2048,2816]{1,0:T(8,128)(2,1)} %get-tuple-element.26, bf16[1024,1408]{1,0:T(8,128)(2,1)} %get-tuple-element.77, bf16[1024,1408]{1,0:T(8,128)(2,1)} %get-tuple-element.76), kind=kOutput, calls=%fused_computation.22 | convolution fusion | flops 11824791552 | bytes 21495808 | tf_op jit(solution)/shard_map/dot_general | solution.py:23
  355.8 10.8 %convolution_convert_fusion.6 = bf16[1024,2048]{1,0:T(8,128)(2,1)} fusion(bf16[1024,1408]{1,0:T(8,128)(2,1)S(1)} %copy-done.26, bf16[1408,2048]{1,0:T(8,128)(2,1)} %get-tuple-element.27), kind=kOutput, calls=%fused_computation.24 | convolution fusion | flops 5907677184 | bytes 12845056 | tf_op jit(solution)/shard_map/dot_general | solution.py:23
  370.0 9.4 %convolution_convert_fusion.1 = bf16[2048,1408]{1,0:T(8,128)(2,1)S(1)} fusion(bf16[1024,2048]{1,0:T(8,128)(2,1)} %bitcast.167, bf16[1024,1408]{1,0:T(8,128)(2,1)} %get-tuple-element.78), kind=kOutput, calls=%fused_computation.6 | convolution fusion | flops 5908463616 | bytes 12845056 | tf_op jit(solution)/shard_map/dot_general | solution.py:23
  379.5 3.0 constant_dynamic-slice_fusion.1
  382.5 4.6 copy.77
  387.1 4.6 copy.81
  391.7 18.8 %convolution_convert_fusion = bf16[2048,2816]{1,0:T(8,128)(2,1)} fusion(bf16[1024,2048]{1,0:T(8,128)(2,1)} %all-gather.2.cloned.1.call-done, bf16[1024,1408]{1,0:T(8,128)(2,1)} %get-tuple-element.77, bf16[1024,1408]{1,0:T(8,128)(2,1)} %get-tuple-element.76), kind=kOutput, calls=%fused_computation.2 | convolution fusion | flops 11828461568 | bytes 21495808 | tf_op jit(solution)/shard_map/dot_general | solution.py:23
  410.5 5.8 dynamic-slice_bitcast_fusion
  416.8 2.6 fusion.6
  425.4 4.1 reduce-scatter.6.cloned.1.call-done
  431.4 77.7 %reduce-scatter.4.cloned.1.call-done = bf16[256,2048]{1,0:T(8,128)(2,1)} async-done(((bf16[1024,2048]{1,0:T(8,128)(2,1)}), bf16[256,2048]{1,0:T(8,128)(2,1)}) %reduce-scatter.4.cloned.1.call-update) | async-done | bytes 1048592 | tf_op jit(solution)/shard_map/reduce_scatter | solution.py:760
  509.2 3.3 fusion.45
  514.1 5.7 convolution_convert_fusion.7
  520.0 3.0 collective-permute-start.1
  525.6 4.2 constant_dynamic-slice_fusion.6
  529.8 6.3 copy.69
  536.1 3.6 collective-permute-start.2
  543.2 3.0 collective-permute-done.2
  549.9 25.3 %shard_map.170 = (bf16[3,1024,512]{2,1,0:T(8,128)(2,1)}, f32[3,1,512]{2,1,0:T(1,128)S(1)}) custom-call(bf16[1024,512]{1,0:T(8,128)(2,1)S(1)} %copy-done.5, bf16[1024,512]{1,0:T(8,128)(2,1)S(1)} %copy-done.6, bf16[1024,512]{1,0:T(8,128)(2,1)S(1)} %copy-done.7, bf16[1024,512]{1,0:T(8,128)(2,1)S(1)} %bitcast.131, f32[1024,128]{1,0:T(8,128)S(1)} %copy-done.2, ...), custom_call_target="tpu_custom_call" | custom-call | flops 5368709120 | bytes 10485760 | tf_op jit(solution)/shard_map/pallas_call | solution.py:181
  575.2 3.2 copy.64
  578.4 11.2 %convolution_convert_fusion.5 = bf16[1024,2048]{1,0:T(8,128)(2,1)} fusion(bf16[1024,1536]{0,1:T(8,128)(2,1)S(1)} %bitcast.144, bf16[2048,1536]{1,0:T(8,128)(2,1)} %get-tuple-element.35), kind=kOutput, calls=%fused_computation.23 | convolution fusion | flops 6444548096 | bytes 13631488 | tf_op jit(solution)/shard_map/dot_general | solution.py:23
  589.6 9.7 %convolution_convert_fusion.3 = bf16[2048,1536]{1,0:T(8,128)(2,1)S(1)} fusion(bf16[1024,2048]{1,0:T(8,128)(2,1)} %bitcast.166, bf16[1024,1536]{0,1:T(8,128)(2,1)S(1)} %bitcast.145), kind=kOutput, calls=%fused_computation.8 | convolution fusion | flops 6445596672 | bytes 13631488 | tf_op jit(solution)/shard_map/dot_general | solution.py:23
  599.3 2.4 constant_dynamic-slice_fusion.8
  601.7 4.7 copy.67
  607.1 3.2 fusion.29
  610.3 5.8 fusion
  623.3 6.3 copy.80
  629.6 2.8 copy.79
  632.5 4.4 fusion.1
  641.5 2.8 fusion.2
  646.2 8.4 %collective-permute-done.15 = bf16[256,2816]{1,0:T(8,128)(2,1)} collective-permute-done((bf16[256,2816]{1,0:T(8,128)(2,1)}, bf16[256,2816]{1,0:T(8,128)(2,1)}, u32[]{:S(2)}, u32[]{:S(2)}) %collective-permute-start.15) | collective-permute-done | bytes 1441824 | tf_op jit(solution)/shard_map/ppermute | solution.py:727
  657.6 28.9 %collective-permute-done.17 = bf16[256,2816]{1,0:T(8,128)(2,1)} collective-permute-done((bf16[256,2816]{1,0:T(8,128)(2,1)}, bf16[256,2816]{1,0:T(8,128)(2,1)}, u32[]{:S(2)}, u32[]{:S(2)}) %collective-permute-start.17) | collective-permute-done | bytes 1441824 | tf_op jit(solution)/shard_map/ppermute | solution.py:727
  689.7 18.4 %collective-permute-done.8 = bf16[256,2048]{0,1:T(8,128)(2,1)} collective-permute-done((bf16[256,2048]{0,1:T(8,128)(2,1)S(1)}, bf16[256,2048]{0,1:T(8,128)(2,1)}, u32[]{:S(2)}, u32[]{:S(2)}) %collective-permute-start.8) | collective-permute-done | bytes 1048608 | tf_op jit(solution)/shard_map/ppermute | solution.py:727
  709.5 4.9 fusion.9
  714.4 4.7 reshape.240
  719.5 12.0 %collective-permute-done.10 = bf16[256,2048]{0,1:T(8,128)(2,1)} collective-permute-done((bf16[256,2048]{0,1:T(8,128)(2,1)}, bf16[256,2048]{0,1:T(8,128)(2,1)}, u32[]{:S(2)}, u32[]{:S(2)}) %collective-permute-start.10) | collective-permute-done | bytes 1048608 | tf_op jit(solution)/shard_map/ppermute | solution.py:727
  733.2 2.7 fusion.24
  747.4 3.1 collective-permute-start.13
  750.5 13.8 %collective-permute-done.6 = bf16[256,1536]{0,1:T(8,128)(2,1)} collective-permute-done((bf16[256,1536]{0,1:T(8,128)(2,1)}, bf16[256,1536]{0,1:T(8,128)(2,1)}, u32[]{:S(2)}, u32[]{:S(2)}) %collective-permute-start.6) | collective-permute-done | bytes 786464 | tf_op jit(solution)/shard_map/ppermute | solution.py:727
  765.6 3.1 fusion.26
  768.7 3.1 copy.78
  780.9 11.3 %shard_map.171 = f32[32,8,128]{2,1,0:T(8,128)} custom-call(f32[32,8,128]{2,1,0:T(8,128)} %pad.9.send_ref), custom_call_target="tpu_custom_call" | custom-call | tf_op jit(solution)/shard_map/pallas_call | solution.py:89
  794.4 3.8 add_add_fusion.2
  (169 shorter events, 81.2 us)
Async XLA Ops:
  7.2 6.5 copy-start.21
  7.2 296.3 %all-gather.2.cloned.1.call-start = ((), (), s32[]{:S(2)}) async-start(), calls=%async_computation.3 | async-start | bytes 5242880 | tf_op jit(solution)/shard_map/all_gather | solution.py:756
  11.1 3.9 copy-start.3
  222.6 99.7 %slice-start = ((s8[5767168]{0:T(1024)(128)(4,1)}), s8[1572864]{0:T(1024)(128)(4,1)S(1)}, s32[]{:S(2)}) async-start(s8[5767168]{0:T(1024)(128)(4,1)} %bitcast.169), calls=%async_computation.7 | async-start | bytes 3145728
  222.6 206.8 %reduce-scatter.6.cloned.1.call-start = ((), (), s32[]{:S(2)}) async-start(), calls=%async_computation.5 | async-start | bytes 5242880 | tf_op jit(solution)/shard_map/reduce_scatter | solution.py:760
  303.4 18.9 %copy-start.25 = (bf16[4,256,2048]{2,1,0:T(8,128)(2,1)S(1)}, bf16[4,256,2048]{2,1,0:T(8,128)(2,1)}, u32[]{:S(2)}) copy-start(bf16[4,256,2048]{2,1,0:T(8,128)(2,1)} %get-tuple-element.28) | copy-start | bytes 12582916
  303.4 18.9 %slice-start.1 = ((s8[5767168]{0:T(1024)(128)(4,1)}), s8[4194304]{0:T(1024)(128)(4,1)S(1)}, s32[]{:S(2)}) async-start(s8[5767168]{0:T(1024)(128)(4,1)} %bitcast.169), calls=%async_computation.8 | async-start | bytes 8388608
  354.0 1.8 copy-start.26
  354.0 155.2 %reduce-scatter.4.cloned.1.call-start = ((), (), s32[]{:S(2)}) async-start(), calls=%async_computation.4 | async-start | bytes 5242880 | tf_op jit(solution)/shard_map/reduce_scatter | solution.py:760
  366.6 2.0 copy-start.8
  366.6 408.7 %reduce-scatter.8.cloned.1.call-start = ((), (), s32[]{:S(2)}) async-start(), calls=%async_computation.6 | async-start | bytes 5242880 | tf_op jit(solution)/shard_map/reduce_scatter | solution.py:760
  387.1 29.7 %collective-permute-start.18 = (bf16[4,256,1408]{1,2,0:T(8,128)(2,1)}, bf16[4,256,1408]{1,2,0:T(8,128)(2,1)}, u32[]{:S(2)}, u32[]{:S(2)}) collective-permute-start(bf16[4,256,1408]{1,2,0:T(8,128)(2,1)} %bitcast.148), channel_id=1, source_target_pairs={{0,4},{4,0},{8,12},{12,8},{16,20},{20,16},{24,28},{28,24},{1,5},{5... | collective-permute-start | bytes 8650760 | tf_op jit(solution)/shard_map/ppermute | solution.py:727
  410.5 6.2 copy-start.17
  416.3 194.0 %collective-permute-start.14 = (bf16[4,256,2816]{2,1,0:T(8,128)(2,1)}, bf16[4,256,2816]{2,1,0:T(8,128)(2,1)}, u32[]{:S(2)}, u32[]{:S(2)}) collective-permute-start(bf16[4,256,2816]{2,1,0:T(8,128)(2,1)} %dynamic-slice_bitcast_fusion), channel_id=1, source_target_pairs={{0,4},{4,0},{8,12},{12,8},{16,20},{20,16},{24,28},{28,24},{1,5},{5... | collective-permute-start | bytes 17301512 | tf_op jit(solution)/shard_map/ppermute | solution.py:727
  419.4 1.6 copy-start.16
  422.4 184.1 %collective-permute-start.19 = (bf16[256,1408]{0,1:T(8,128)(2,1)}, bf16[256,1408]{0,1:T(8,128)(2,1)}, u32[]{:S(2)}, u32[]{:S(2)}) collective-permute-start(bf16[256,1408]{0,1:T(8,128)(2,1)} %get-tuple-element.94), channel_id=1, source_target_pairs={{0,8},{4,12},{8,0},{12,4},{16,24},{20,28},{24,16},{28,20},{1,9},{5... | collective-permute-start | bytes 2162696 | tf_op jit(solution)/shard_map/ppermute | solution.py:727
  423.9 183.2 %collective-permute-start.21 = (bf16[256,1408]{0,1:T(8,128)(2,1)}, bf16[256,1408]{0,1:T(8,128)(2,1)}, u32[]{:S(2)}, u32[]{:S(2)}) collective-permute-start(bf16[256,1408]{0,1:T(8,128)(2,1)} %get-tuple-element.95), channel_id=1, source_target_pairs={{0,24},{4,28},{8,16},{12,20},{16,8},{20,12},{24,0},{28,4},{1,25},{... | collective-permute-start | bytes 2162696 | tf_op jit(solution)/shard_map/ppermute | solution.py:727
  431.4 82.3 %copy-start.20 = (bf16[256,2048]{1,0:T(8,128)(2,1)S(1)}, bf16[256,2048]{1,0:T(8,128)(2,1)}, u32[]{:S(2)}) copy-start(bf16[256,2048]{1,0:T(8,128)(2,1)} %cot.1) | copy-start | bytes 3145732
  519.8 3.4 copy-start.22
  520.0 20.7 %collective-permute-start.1 = (bf16[256,512]{1,0:T(8,128)(2,1)S(1)}, bf16[256,512]{1,0:T(8,128)(2,1)}, u32[]{:S(2)}, u32[]{:S(2)}) collective-permute-start(bf16[256,512]{1,0:T(8,128)(2,1)S(1)} %get-tuple-element.102), channel_id=1, source_target_pairs={{0,2},{1,3},{2,0},{3,1},{4,6},{5,7},{6,4},{7,5},{8,10},{9,11},{10,... | collective-permute-start | bytes 786440 | tf_op jit(solution)/shard_map/ppermute | solution.py:727
  523.0 13.2 %collective-permute-start = (bf16[256,512]{1,0:T(8,128)(2,1)S(1)}, bf16[256,512]{1,0:T(8,128)(2,1)}, u32[]{:S(2)}, u32[]{:S(2)}) collective-permute-start(bf16[256,512]{1,0:T(8,128)(2,1)S(1)} %get-tuple-element.103), channel_id=1, source_target_pairs={{0,1},{1,2},{2,3},{3,0},{4,5},{5,6},{6,7},{7,4},{8,9},{9,10},{10,1... | collective-permute-start | bytes 786440 | tf_op jit(solution)/shard_map/ppermute | solution.py:727
  529.8 16.4 %copy-start = (f32[1024,128]{1,0:T(8,128)S(1)}, f32[1024,128]{1,0:T(8,128)}, u32[]{:S(2)}) copy-start(f32[1024,128]{1,0:T(8,128)} %get-tuple-element.108.s_high) | copy-start | bytes 1572868
  529.8 16.4 %copy-start.1 = (f32[1024,128]{1,0:T(8,128)S(1)}, f32[1024,128]{1,0:T(8,128)}, u32[]{:S(2)}) copy-start(f32[1024,128]{1,0:T(8,128)} %get-tuple-element.109.s_low) | copy-start | bytes 1572868
  529.8 16.4 %copy-start.2 = (f32[1024,128]{1,0:T(8,128)S(1)}, f32[1024,128]{1,0:T(8,128)}, u32[]{:S(2)}) copy-start(f32[1024,128]{1,0:T(8,128)} %get-tuple-element.110.cos) | copy-start | bytes 1572868
  529.8 16.4 %copy-start.4 = (s32[1024]{0:T(1024)S(1)}, s32[1024]{0:T(1024)}, u32[]{:S(2)}) copy-start(s32[1024]{0:T(1024)} %copy-done.3) | copy-start | bytes 12292
  536.1 10.1 %collective-permute-start.2 = (bf16[256,512]{1,0:T(8,128)(2,1)S(1)}, bf16[256,512]{1,0:T(8,128)(2,1)S(1)}, u32[]{:S(2)}, u32[]{:S(2)}) collective-permute-start(bf16[256,512]{1,0:T(8,128)(2,1)S(1)} %get-tuple-element.101), channel_id=1, source_target_pairs={{0,3},{1,0},{2,1},{3,2},{4,7},{5,4},{6,5},{7,6},{8,11},{9,8},{10,9... | collective-permute-start | bytes 786440 | tf_op jit(solution)/shard_map/ppermute | solution.py:727
  540.7 66.3 %collective-permute-start.20 = (bf16[256,1408]{0,1:T(8,128)(2,1)}, bf16[256,1408]{0,1:T(8,128)(2,1)}, u32[]{:S(2)}, u32[]{:S(2)}) collective-permute-start(bf16[256,1408]{0,1:T(8,128)(2,1)} %get-tuple-element.96), channel_id=1, source_target_pairs={{0,16},{4,20},{8,24},{12,28},{16,0},{20,4},{24,8},{28,12},{1,17},{... | collective-permute-start | bytes 2162696 | tf_op jit(solution)/shard_map/ppermute | solution.py:727
  546.2 86.3 %collective-permute-start.7 = (bf16[4,256,2048]{1,2,0:T(8,128)(2,1)}, bf16[4,256,2048]{1,2,0:T(8,128)(2,1)}, u32[]{:S(2)}, u32[]{:S(2)}) collective-permute-start(bf16[4,256,2048]{1,2,0:T(8,128)(2,1)} %bitcast.142), channel_id=1, source_target_pairs={{0,4},{4,0},{8,12},{12,8},{16,20},{20,16},{24,28},{28,24},{1,5},{5... | collective-permute-start | bytes 12582920 | tf_op jit(solution)/shard_map/ppermute | solution.py:727
  606.5 35.0 %collective-permute-start.3 = (bf16[4,256,1536]{1,2,0:T(8,128)(2,1)}, bf16[4,256,1536]{1,2,0:T(8,128)(2,1)}, u32[]{:S(2)}, u32[]{:S(2)}) collective-permute-start(bf16[4,256,1536]{1,2,0:T(8,128)(2,1)} %bitcast.143), channel_id=1, source_target_pairs={{0,4},{4,0},{8,12},{12,8},{16,20},{20,16},{24,28},{28,24},{1,5},{5... | collective-permute-start | bytes 9437192 | tf_op jit(solution)/shard_map/ppermute | solution.py:727
  616.0 3.8 copy-start.9
  619.9 34.8 %collective-permute-start.15 = (bf16[256,2816]{1,0:T(8,128)(2,1)}, bf16[256,2816]{1,0:T(8,128)(2,1)}, u32[]{:S(2)}, u32[]{:S(2)}) collective-permute-start(bf16[256,2816]{1,0:T(8,128)(2,1)} %get-tuple-element.85), channel_id=1, source_target_pairs={{0,8},{4,12},{8,0},{12,4},{16,24},{20,28},{24,16},{28,20},{1,9},{5... | collective-permute-start | bytes 4325384 | tf_op jit(solution)/shard_map/ppermute | solution.py:727
  621.3 65.2 %collective-permute-start.17 = (bf16[256,2816]{1,0:T(8,128)(2,1)}, bf16[256,2816]{1,0:T(8,128)(2,1)}, u32[]{:S(2)}, u32[]{:S(2)}) collective-permute-start(bf16[256,2816]{1,0:T(8,128)(2,1)} %get-tuple-element.86), channel_id=1, source_target_pairs={{0,24},{4,28},{8,16},{12,20},{16,8},{20,12},{24,0},{28,4},{1,25},{... | collective-permute-start | bytes 4325384 | tf_op jit(solution)/shard_map/ppermute | solution.py:727
  622.8 65.5 %collective-permute-start.16 = (bf16[256,2816]{1,0:T(8,128)(2,1)}, bf16[256,2816]{1,0:T(8,128)(2,1)}, u32[]{:S(2)}, u32[]{:S(2)}) collective-permute-start(bf16[256,2816]{1,0:T(8,128)(2,1)} %get-tuple-element.87), channel_id=1, source_target_pairs={{0,16},{4,20},{8,24},{12,28},{16,0},{20,4},{24,8},{28,12},{1,17},{... | collective-permute-start | bytes 4325384 | tf_op jit(solution)/shard_map/ppermute | solution.py:727
  636.9 3.1 copy-start.12
  636.9 4.6 copy-start.15
  640.0 68.0 %collective-permute-start.8 = (bf16[256,2048]{0,1:T(8,128)(2,1)S(1)}, bf16[256,2048]{0,1:T(8,128)(2,1)}, u32[]{:S(2)}, u32[]{:S(2)}) collective-permute-start(bf16[256,2048]{0,1:T(8,128)(2,1)S(1)} %get-tuple-element.88), channel_id=1, source_target_pairs={{0,8},{4,12},{8,0},{12,4},{16,24},{20,28},{24,16},{28,20},{1,9},{5... | collective-permute-start | bytes 3145736 | tf_op jit(solution)/shard_map/ppermute | solution.py:727
  644.3 87.2 %collective-permute-start.10 = (bf16[256,2048]{0,1:T(8,128)(2,1)}, bf16[256,2048]{0,1:T(8,128)(2,1)}, u32[]{:S(2)}, u32[]{:S(2)}) collective-permute-start(bf16[256,2048]{0,1:T(8,128)(2,1)} %get-tuple-element.89), channel_id=1, source_target_pairs={{0,24},{4,28},{8,16},{12,20},{16,8},{20,12},{24,0},{28,4},{1,25},{... | collective-permute-start | bytes 3145736 | tf_op jit(solution)/shard_map/ppermute | solution.py:727
  654.6 78.6 %collective-permute-start.9 = (bf16[256,2048]{0,1:T(8,128)(2,1)}, bf16[256,2048]{0,1:T(8,128)(2,1)}, u32[]{:S(2)}, u32[]{:S(2)}) collective-permute-start(bf16[256,2048]{0,1:T(8,128)(2,1)} %get-tuple-element.90), channel_id=1, source_target_pairs={{0,16},{4,20},{8,24},{12,28},{16,0},{20,4},{24,8},{28,12},{1,17},{... | collective-permute-start | bytes 3145736 | tf_op jit(solution)/shard_map/ppermute | solution.py:727
  686.5 60.9 %collective-permute-start.4 = (bf16[256,1536]{0,1:T(8,128)(2,1)}, bf16[256,1536]{0,1:T(8,128)(2,1)}, u32[]{:S(2)}, u32[]{:S(2)}) collective-permute-start(bf16[256,1536]{0,1:T(8,128)(2,1)} %get-tuple-element.91), channel_id=1, source_target_pairs={{0,8},{4,12},{8,0},{12,4},{16,24},{20,28},{24,16},{28,20},{1,9},{5... | collective-permute-start | bytes 2359304 | tf_op jit(solution)/shard_map/ppermute | solution.py:727
  688.2 76.1 %collective-permute-start.6 = (bf16[256,1536]{0,1:T(8,128)(2,1)}, bf16[256,1536]{0,1:T(8,128)(2,1)}, u32[]{:S(2)}, u32[]{:S(2)}) collective-permute-start(bf16[256,1536]{0,1:T(8,128)(2,1)} %get-tuple-element.92), channel_id=1, source_target_pairs={{0,24},{4,28},{8,16},{12,20},{16,8},{20,12},{24,0},{28,4},{1,25},{... | collective-permute-start | bytes 2359304 | tf_op jit(solution)/shard_map/ppermute | solution.py:727
  708.0 57.6 %collective-permute-start.5 = (bf16[256,1536]{0,1:T(8,128)(2,1)}, bf16[256,1536]{0,1:T(8,128)(2,1)}, u32[]{:S(2)}, u32[]{:S(2)}) collective-permute-start(bf16[256,1536]{0,1:T(8,128)(2,1)} %get-tuple-element.93), channel_id=1, source_target_pairs={{0,16},{4,20},{8,24},{12,28},{16,0},{20,4},{24,8},{28,12},{1,17},{... | collective-permute-start | bytes 2359304 | tf_op jit(solution)/shard_map/ppermute | solution.py:727
  742.1 29.7 %collective-permute-start.11 = (bf16[256,512]{1,0:T(8,128)(2,1)}, bf16[256,512]{1,0:T(8,128)(2,1)}, u32[]{:S(2)}, u32[]{:S(2)}) collective-permute-start(bf16[256,512]{1,0:T(8,128)(2,1)} %bitcast.156), channel_id=1, source_target_pairs={{0,1},{1,2},{2,3},{3,0},{4,5},{5,6},{6,7},{7,4},{8,9},{9,10},{10,1... | collective-permute-start | bytes 786440 | tf_op jit(solution)/shard_map/ppermute | solution.py:727
  744.4 28.7 %collective-permute-start.12 = (bf16[256,512]{1,0:T(8,128)(2,1)}, bf16[256,512]{1,0:T(8,128)(2,1)S(1)}, u32[]{:S(2)}, u32[]{:S(2)}) collective-permute-start(bf16[256,512]{1,0:T(8,128)(2,1)} %bitcast.154), channel_id=1, source_target_pairs={{0,2},{1,3},{2,0},{3,1},{4,6},{5,7},{6,4},{7,5},{8,10},{9,11},{10,... | collective-permute-start | bytes 786440 | tf_op jit(solution)/shard_map/ppermute | solution.py:727
  747.4 25.8 %collective-permute-start.13 = (bf16[256,512]{1,0:T(8,128)(2,1)}, bf16[256,512]{1,0:T(8,128)(2,1)}, u32[]{:S(2)}, u32[]{:S(2)}) collective-permute-start(bf16[256,512]{1,0:T(8,128)(2,1)} %bitcast.153), channel_id=1, source_target_pairs={{0,3},{1,0},{2,1},{3,2},{4,7},{5,4},{6,5},{7,6},{8,11},{9,8},{10,9... | collective-permute-start | bytes 786440 | tf_op jit(solution)/shard_map/ppermute | solution.py:727
  768.7 5.5 copy-start.19
  771.8 3.5 copy-start.14
  774.4 5.8 copy-start.24
  775.3 19.1 %copy-start.11 = (f32[256,2048]{1,0:T(8,128)S(1)}, f32[256,2048]{1,0:T(8,128)}, u32[]{:S(2)}) copy-start(f32[256,2048]{1,0:T(8,128)} %copy-done.10) | copy-start | bytes 6291460
  (7 other events, 8.5 us)
Sparse Core Ops, SparseCore 0:
  222.7 80.6 all-gather.1
  354.1 75.2 reduce-scatter.5
  431.8 77.2 reduce-scatter.3
  589.7 77.9 reduce-scatter.7

commit v3 on v2

--- a/solution.py
+++ b/solution.py
@@ -23,82 +23,6 @@
     return lax.dot_general(left, right, dims, preferred_element_type=F32)
 
 
-def layer_norm(values, gain_row, shift_row):
-    average = jnp.mean(values, axis=-1, keepdims=True)
-    centred = values - average
-    variance = jnp.mean(centred * centred, axis=-1, keepdims=True)
-    return centred * lax.rsqrt(variance + NORM_EPS) * gain_row + shift_row
-
-
-def swiglu(gate_vals, up_vals):
-    return jax.nn.silu(gate_vals) * up_vals
-
-
-def exchange_kernel(sizes, scatter, send_ref, got_ref, send_sems, recv_sems):
-    outer, inner = sizes
-    count = outer * inner
-    me = lax.axis_index("fsdp") * inner + lax.axis_index("tp")
-    barrier = pltpu.get_barrier_semaphore()
-
-    def greet(step, carry):
-        other = lax.rem(me + step, count)
-        pl.semaphore_signal(
-            barrier, inc=1, device_id=(other // inner, lax.rem(other, inner)), device_id_type=MESH
-        )
-        return carry
-
-    lax.fori_loop(1, count, greet, 0)
-    pl.semaphore_wait(barrier, count - 1)
-
-    def copy_to(step):
-        other = lax.rem(me + step, count)
-        return pltpu.make_async_remote_copy(
-            src_ref=send_ref.at[other] if scatter else send_ref.at[0],
-            dst_ref=got_ref.at[me],
-            send_sem=send_sems.at[step],
-            recv_sem=recv_sems.at[me],
-            device_id=(other // inner, lax.rem(other, inner)),
-            device_id_type=MESH,
-        )
-
-    def start(step, carry):
-        copy_to(step).start()
-        return carry
-
-    lax.fori_loop(1, count, start, 0)
-    got_ref[me] = send_ref[me] if scatter else send_ref[0]
-
-    def finish(step, carry):
-        source = lax.rem(me + step, count)
-        copy_to(step).wait_send()
-        pltpu.make_async_remote_copy(
-            src_ref=send_ref.at[0],
-            dst_ref=got_ref.at[source],
-            send_sem=send_sems.at[step],
-            recv_sem=recv_sems.at[source],
-            device_id=(source // inner, lax.rem(source, inner)),
-            device_id_type=MESH,
-        ).wait_recv()
-        return carry
-
-    lax.fori_loop(1, count, finish, 0)
-
-
-def exchange(tiles, sizes, scatter, collective_id):
-    count = sizes[0] * sizes[1]
-    return pl.pallas_call(
-        functools.partial(exchange_kernel, sizes, scatter),
-        out_shape=jax.ShapeDtypeStruct((count, 8, LANES), F32),
-        in_specs=[pl.BlockSpec(memory_space=pltpu.VMEM)],
-        out_specs=pl.BlockSpec(memory_space=pltpu.VMEM),
-        scratch_shapes=[
-            pltpu.SemaphoreType.DMA((count,)),
-            pltpu.SemaphoreType.DMA((count,)),
-        ],
-        compiler_params=pltpu.CompilerParams(collective_id=collective_id, has_side_effects=True),
-    )(tiles)
-
-
 def turn(values, cosine, sine_low, sine_high):
     return (
         values * cosine
@@ -123,85 +47,6 @@
     return weights, jnp.sum(weights, axis=0, keepdims=True)
 
 
-def attend_back_kernel(
-    rows, widest, q_in, k_in, v_in, g_in, cos, s_low, s_high, starts, g_out, b_out, kt, dk, dv
-):
-    seq_len = q_in.shape[0]
-    cosine, sine_low, sine_high = cos[...], s_low[...], s_high[...]
-    kt[...] = k_in[...].astype(F32).T.astype(BF16)
-    dk[...] = jnp.zeros_like(dk)
-    dv[...] = jnp.zeros_like(dv)
-    for block in range(seq_len // rows):
-        here = slice(block * rows, (block + 1) * rows)
-        first, last = key_range(block, rows, widest)
-        query_rows = (q_in[here, :].astype(F32) * HEAD**-0.5).astype(BF16)
-        grad_rows = g_in[here, :]
-        query_cols = query_rows.astype(F32).T.astype(BF16)
-        grad_cols = grad_rows.astype(F32).T.astype(BF16)
-        head_down = lax.broadcasted_iota(jnp.int32, query_cols.shape, 0) // HEAD
-        head_along = lax.broadcasted_iota(jnp.int32, query_rows.shape, 1) // HEAD
-        none_down, none_along = jnp.zeros_like(query_cols), jnp.zeros_like(query_rows)
-        parts = []
-        for head in range(LANES // HEAD):
-            weights, total = seen_weights(
-                k_in[first:last, :],
-                jnp.where(head_down == head, query_cols, none_down),
-                starts[:, here],
-                first,
-                block * rows,
-            )
-            probs = weights * (1.0 / total)
-            grad_probs = dot(
-                v_in[first:last, :], jnp.where(head_down == head, grad_cols, none_down), NN
-            )
-            inner = jnp.sum(probs * grad_probs, axis=0, keepdims=True)
-            grad_scores = (probs * (grad_probs - inner)).astype(BF16)
-            dk[first:last, :] += dot(
-                grad_scores, jnp.where(head_along == head, query_rows, none_along), NN
-            )
-            dv[first:last, :] += dot(
-                probs.astype(BF16), jnp.where(head_along == head, grad_rows, none_along), NN
-            )
-            parts.append(dot(kt[head * HEAD : (head + 1) * HEAD, first:last], grad_scores, NN))
-        grad_queries = jnp.concatenate(parts, axis=0).T * HEAD**-0.5
-        g_out[0, here, :] = turn(
-            grad_queries, cosine[here, :], -sine_low[here, :], -sine_high[here, :]
-        ).astype(BF16)
-    g_out[1] = turn(dk[...], cosine, -sine_low, -sine_high).astype(BF16)
-    g_out[2] = dv[...].astype(BF16)
-    b_out[...] = jnp.sum(g_out[...].astype(F32), axis=1, keepdims=True)
-
-
-def attend_backward(queries, key_vals, value_rows, grad_attended, tables, starts, widest):
-    seq_len, width = queries.shape
-    pairs = width // LANES
-    rows = min(256, seq_len)
-    column = pl.BlockSpec((seq_len, LANES), lambda i: (0, i))
-    whole = lambda shape: pl.BlockSpec(shape, lambda i: (0, 0))
-    return pl.pallas_call(
-        functools.partial(attend_back_kernel, rows, widest),
-        grid=(pairs,),
-        in_specs=[column] * 4 + [whole((seq_len, LANES))] * 3 + [whole((1, seq_len))],
-        out_specs=[
-            pl.BlockSpec((3, seq_len, LANES), lambda i: (0, 0, i)),
-            pl.BlockSpec((3, 1, LANES), lambda i: (0, 0, i)),
-        ],
-        out_shape=[
-            jax.ShapeDtypeStruct((3, seq_len, width), BF16),
-            jax.ShapeDtypeStruct((3, 1, width), F32),
-        ],
-        scratch_shapes=[
-            pltpu.VMEM((LANES, seq_len), BF16),
-            pltpu.VMEM((seq_len, LANES), F32),
-            pltpu.VMEM((seq_len, LANES), F32),
-        ],
-        compiler_params=pltpu.CompilerParams(vmem_limit_bytes=48 * 2**20),
-        cost_estimate=pl.CostEstimate(
-            flops=10 * seq_len * seq_len * width, bytes_accessed=20 * seq_len * width, transcendentals=0
-        ),
-    )(queries, key_vals, value_rows, grad_attended, *tables, starts)
-
-
 def xor(value, mask):
     bit = 1
     while bit <= mask:
@@ -303,12 +148,13 @@
 
     def slot(self, f, part=None):
         if self.by_rows:
-            rows = self.whole.shape[0] // self.at.n_fsdp
+            rows = self.whole.shape[-2] // self.at.n_fsdp
             first = f * rows
             if part is not None:
                 rows = rows // 2
                 first = first + part * rows
-            return self.whole.at[pl.ds(pl.multiple_of(first, rows), rows), :]
+            here = pl.ds(pl.multiple_of(first, rows), rows)
+            return self.whole.at[:, here, :] if len(self.whole.shape) == 3 else self.whole.at[here, :]
         width = self.whole.shape[1] // self.at.n_fsdp
         columns = pl.ds(pl.multiple_of(f * width, LANES), width)
         if part is None:
@@ -693,14 +539,14 @@
         (shape((n_tp, slab, model), BF16), hbm),
         (shape((model, 3 * width), BF16), hbm),
         (shape((model, model), BF16), hbm),
-        (shape((model, 2 * hidden), BF16), hbm),
+        (shape((2, model, hidden), BF16), hbm),
         (shape((hidden, model), BF16), hbm),
     ]
     dma = pltpu.SemaphoreType.DMA
     pairs = width // LANES
     return pl.pallas_call(
         functools.partial(front_kernel, sizes, widest),
-        in_specs=[hbm] * 6 + [vmem] * 5,
+        in_specs=[vmem] * 11,
         out_specs=[spec for _, spec in outs],
         out_shape=[out for out, _ in outs],
         scratch_shapes=[
@@ -723,37 +569,856 @@
     )(tok, cot, wq, wo, wgu, wd, tile, *tables, starts)
 
 
-def hop(values, axis, size, partner):
-    return lax.ppermute(values, axis, [(i, partner(i)) for i in range(size)])
-
-
-def scatter_fsdp(blocks, size):
-    me = lax.axis_index("fsdp")
-    core, chip = me % 2, me // 2
-    pairs = blocks.reshape((size // 2, 2) + blocks.shape[1:])
-    mine = lax.dynamic_index_in_dim(pairs, core, 1, keepdims=False)
-    other = lax.dynamic_index_in_dim(pairs, 1 - core, 1, keepdims=False)
-    got = hop(other, "fsdp", size, lambda i: i ^ 1)
-    sums = (mine.astype(F32) + got.astype(F32)).astype(BF16)
-    total = lax.dynamic_index_in_dim(sums, chip, 0, keepdims=False).astype(F32)
-    for k in range(1, size // 2):
-        block = lax.dynamic_index_in_dim(sums, chip ^ k, 0, keepdims=False)
-        total = total + hop(block, "fsdp", size, lambda i, k=k: i ^ (2 * k)).astype(F32)
+def xor_any(value, mask, bits):
+    total = 0
+    for b in range(bits):
+        both = lax.rem(value // 2**b, 2) + lax.rem(mask // 2**b, 2)
+        total = total + lax.rem(both, 2) * 2**b
     return total
 
 
-def swap_tp(blocks, size):
-    me = lax.axis_index("tp")
-    got = blocks
-    for k in range(1, size):
-        block = lax.dynamic_index_in_dim(blocks, (me + k) % size, 0, keepdims=False)
-        came = hop(block, "tp", size, lambda i, k=k: (i + k) % size)
-        got = lax.dynamic_update_index_in_dim(got, came, (me + size - k) % size, 0)
-    return got
-
-
-def gather_rows(values):
-    return lax.all_gather(values, "tp", axis=0, tiled=True)
+class Fold:
+    def __init__(self, at, total, going, came, tile, send_sems, recv_sems):
+        self.at, self.total, self.going, self.came, self.tile = at, total, going, came, tile
+        self.send_sems, self.recv_sems = send_sems, recv_sems
+        self.tiles = total.shape[1] // tile
+
+    def lanes(self, c):
+        return pl.ds(pl.multiple_of(c * self.tile, self.tile), self.tile)
+
+    def copy(self, j, c, way):
+        at = self.at
+        slot = j if way == 0 else j + (at.n_tp - j) * lax.max(0, j - at.t + 2)
+        return send(
+            self.going.at[j, :, self.lanes(c)],
+            self.came.at[slot, :, self.lanes(c)],
+            self.send_sems.at[j, c],
+            self.recv_sems.at[slot, c],
+            at.along(at.t + 1 - 2 * way),
+        )
+
+    def put(self, j, c, values):
+        at = self.at
+
+        @pl.when(j == at.t)
+        def _():
+            self.total[:, self.lanes(c)] = values
+
+        @pl.when(j != at.t)
+        def _():
+            self.going[j, :, self.lanes(c)] = values.astype(BF16)
+
+        pl.when((j > at.t) & (at.t == 0))(lambda: self.copy(j, c, 0).start())
+        pl.when((j < at.t) & (at.t == at.n_tp - 1))(lambda: self.copy(j, c, 1).start())
+
+    def arrived(self, slot, c):
+        tile = self.came.at[slot, :, self.lanes(c)]
+        send(
+            tile, tile, self.send_sems.at[0, c], self.recv_sems.at[slot, c], self.at.along(self.at.t)
+        ).wait_recv()
+
+    def forward(self, key, c):
+        at = self.at
+
+        def some(j, way):
+            self.arrived(j, c)
+            here = self.lanes(c)
+            self.going[j, :, here] = (
+                self.going[j, :, here].astype(F32) + self.came[j, :, here].astype(F32)
+            ).astype(BF16)
+            self.copy(j, c, way).start()
+
+        pl.when((key > at.t) & (at.t > 0))(lambda: some(key, 0))
+        down = at.n_tp - 1 - key
+        pl.when((down < at.t) & (at.t < at.n_tp - 1))(lambda: some(down, 1))
+
+    def end(self):
+        at = self.at
+
+        def some(c, carry):
+            here = self.lanes(c)
+
+            @pl.when(at.t > 0)
+            def _():
+                self.arrived(at.t, c)
+                self.total[:, here] = self.total[:, here] + self.came[at.t, :, here].astype(F32)
+
+            @pl.when(at.t < at.n_tp - 1)
+            def _():
+                self.arrived(at.n_tp, c)
+                self.total[:, here] = self.total[:, here] + self.came[at.n_tp, :, here].astype(F32)
+
+            return carry
+
+        lax.fori_loop(0, self.tiles, some, 0)
+
+    def finish(self):
+        at = self.at
+
+        def some(i, carry):
+            j, c = i // self.tiles, lax.rem(i, self.tiles)
+            pl.when(j > at.t)(lambda: self.copy(j, c, 0).wait_send())
+            pl.when(j < at.t)(lambda: self.copy(j, c, 1).wait_send())
+            return carry
+
+        lax.fori_loop(0, at.n_tp * self.tiles, some, 0)
+
+
+def middle_kernel(
+    sizes,
+    two, cot_all, wgu_all, wd_all,
+    gn2, hidden, sum_gu, sum_d, sib_gu, sib_d,
+    x, cots, wgu_v, wd_v, ggu, acts, came, going, stage_gu, stage_d, in_gu, in_d,
+    line_send, line_recv, fold_send, fold_recv, sib_send, sib_recv, local_sems,
+):
+    n_fsdp, n_tp = sizes
+    half = n_fsdp // 2
+    bits = half.bit_length() - 1
+    at = Places(n_fsdp, n_tp)
+    slab, model = two.shape
+    part_rows = model // n_fsdp
+    at.greet()
+    line = Line(at, two, x, line_send, line_recv)
+    line.start()
+    loads = [
+        pltpu.make_async_copy(two, x.at[at.t], local_sems.at[0]),
+        pltpu.make_async_copy(wgu_all, wgu_v, local_sems.at[1]),
+        pltpu.make_async_copy(wd_all, wd_v, local_sems.at[2]),
+        pltpu.make_async_copy(cot_all, cots, local_sems.at[3]),
+    ]
+    for load in loads:
+        load.start()
+    for load in loads:
+        load.wait()
+    fold = Fold(at, gn2, going, came, min(512, model), fold_send, fold_recv)
+
+    def unit(slot):
+        here = pl.ds(pl.multiple_of(slot * slab, slab), slab)
+        acts[0] = dot(x[slot], wgu_v[0], NN)
+        acts[1] = dot(x[slot], wgu_v[1], NN)
+        acts[2] = dot(cots[slot], wd_v[...], NT)
+        step = 16
+
+        def some(i, carry):
+            local_rows = pl.ds(pl.multiple_of(i * step, step), step)
+            rows = pl.ds(pl.multiple_of(slot * slab + i * step, step), step)
+            gate, up, grad = acts[0, local_rows, :], acts[1, local_rows, :], acts[2, local_rows, :]
+            low = jax.nn.sigmoid(gate)
+            act = gate * low
+            hidden[rows, :] = (act * up).astype(BF16)
+            ggu[0, rows, :] = (grad * up * low * (1.0 + gate * (1.0 - low))).astype(BF16)
+            ggu[1, rows, :] = (grad * act).astype(BF16)
+            return carry
+
+        lax.fori_loop(0, slab // step, some, 0)
+
+        def tiles(c, carry):
+            rows = fold.lanes(c)
+            fold.put(
+                slot,
+                c,
+                dot(ggu[0, here, :], wgu_v[0, rows, :], NT) + dot(ggu[1, here, :], wgu_v[1, rows, :], NT),
+            )
+            return carry
+
+        lax.fori_loop(0, fold.tiles, tiles, 0)
+
+    def each_from(first, last, work):
+        def some(i, carry):
+            s = (i + 1) // 2
+            slot = at.t + s * (2 * lax.rem(i, 2) - 1)
+            pl.when((slot >= 0) & (slot < n_tp))(lambda: work(slot))
+            return carry
+
+        lax.fori_loop(max(0, 2 * first - 1), 2 * last - 1, some, 0)
+
+    for s in range(n_tp):
+        if s:
+            line.step(s)
+        each_from(s, s + 1, unit)
+
+    for key in range(1, n_tp - 2):
+        for c in range(fold.tiles):
+            fold.forward(key, c)
+
+    def block(f, take):
+        columns = pl.ds(pl.multiple_of(f * part_rows, part_rows), part_rows)
+        for part in range(2):
+            rows = x[:, :, columns].reshape(n_tp * slab, part_rows)
+            take(part, dot(rows, ggu[part], TN))
+        grads = cots[:, :, columns].reshape(n_tp * slab, part_rows)
+        take(2, dot(hidden[...], grads, TN))
+
+    def sib_copies(i):
+        return [
+            send(stage_gu.at[lax.rem(i, 2)], sib_gu.at[i], sib_send.at[0, i], sib_recv.at[0, i], at.sibling()),
+            send(stage_d.at[lax.rem(i, 2)], sib_d.at[i], sib_send.at[1, i], sib_recv.at[1, i], at.sibling()),
+        ]
+
+    def keep_copies(i):
+        return [
+            pltpu.make_async_copy(stage_gu.at[lax.rem(i, 2)], sum_gu.at[i], local_sems.at[4 + lax.rem(i, 2)]),
+            pltpu.make_async_copy(stage_d.at[lax.rem(i, 2)], sum_d.at[i], local_sems.at[6 + lax.rem(i, 2)]),
+        ]
+
+    def others(i, carry):
+        pl.when(i < fold.tiles)(lambda: fold.forward(n_tp - 2, i))
+
+        @pl.when(i >= 2)
+        def _():
+            for copy in sib_copies(i - 2):
+                copy.wait_send()
+
+        def take(part, values):
+            if part < 2:
+                stage_gu[lax.rem(i, 2), part] = values.astype(BF16)
+            else:
+                stage_d[lax.rem(i, 2)] = values.astype(BF16)
+
+        block(xor_any(at.chip, i, bits) * 2 + 1 - at.core, take)
+        for copy in sib_copies(i):
+            copy.start()
+        return carry
+
+    lax.fori_loop(0, half, others, 0)
+    for i in range(half - 2, half):
+        for copy in sib_copies(jnp.int32(i)):
+            copy.wait_send()
+
+    def mine(i, carry):
+        pl.when(i < fold.tiles)(lambda: fold.forward(n_tp - 1, i))
+        for copy in sib_copies(i):
+            copy.wait_recv()
+        takes = [
+            pltpu.make_async_copy(sib_gu.at[i], in_gu, local_sems.at[8]),
+            pltpu.make_async_copy(sib_d.at[i], in_d, local_sems.at[9]),
+        ]
+        for take in takes:
+            take.start()
+
+        @pl.when(i >= 2)
+        def _():
+            for copy in keep_copies(i - 2):
+                copy.wait()
+
+        def take(part, values):
+            if part == 0:
+                for copy in takes:
+                    copy.wait()
+            if part < 2:
+                stage_gu[lax.rem(i, 2), part] = (values + in_gu[part].astype(F32)).astype(BF16)
+            else:
+                stage_d[lax.rem(i, 2)] = (values + in_d[...].astype(F32)).astype(BF16)
+
+        block(xor_any(at.chip, i, bits) * 2 + at.core, take)
+        for copy in keep_copies(i):
+            copy.start()
+        return carry
+
+    lax.fori_loop(0, half, mine, 0)
+    fold.end()
+    for i in range(half - 2, half):
+        for copy in keep_copies(jnp.int32(i)):
+            copy.wait()
+    line.finish()
+    fold.finish()
+
+
+def middle(sizes, two, cot_all, wgu_all, wd_all):
+    n_fsdp, n_tp = sizes
+    half = n_fsdp // 2
+    slab, model = two.shape
+    hidden = wd_all.shape[0]
+    part_rows = model // n_fsdp
+    tile = min(512, model)
+    hbm = pl.BlockSpec(memory_space=pl.ANY)
+    vmem = pl.BlockSpec(memory_space=pltpu.VMEM)
+    shape = jax.ShapeDtypeStruct
+    outs = [
+        (shape((slab, model), F32), vmem),
+        (shape((n_tp * slab, hidden), BF16), vmem),
+        (shape((half, 2, part_rows, hidden), BF16), hbm),
+        (shape((half, hidden, part_rows), BF16), hbm),
+        (shape((half, 2, part_rows, hidden), BF16), hbm),
+        (shape((half, hidden, part_rows), BF16), hbm),
+    ]
+    dma = pltpu.SemaphoreType.DMA
+    return pl.pallas_call(
+        functools.partial(middle_kernel, sizes),
+        in_specs=[hbm] * 4,
+        out_specs=[spec for _, spec in outs],
+        out_shape=[out for out, _ in outs],
+        scratch_shapes=[
+            pltpu.VMEM((n_tp, slab, model), BF16),
+            pltpu.VMEM((n_tp, slab, model), BF16),
+            pltpu.VMEM((2, model, hidden), BF16),
+            pltpu.VMEM((hidden, model), BF16),
+            pltpu.VMEM((2, n_tp * slab, hidden), BF16),
+            pltpu.VMEM((3, slab, hidden), F32),
+            pltpu.VMEM((n_tp + 1, slab, model), BF16),
+            pltpu.VMEM((n_tp, slab, model), BF16),
+            pltpu.VMEM((2, 2, part_rows, hidden), BF16),
+            pltpu.VMEM((2, hidden, part_rows), BF16),
+            pltpu.VMEM((2, part_rows, hidden), BF16),
+            pltpu.VMEM((hidden, part_rows), BF16),
+            dma((2, n_tp)), dma((n_tp,)), dma((n_tp, model // tile)), dma((n_tp + 1, model // tile)),
+            dma((2, half)), dma((2, half)), dma((10,)),
+        ],
+        compiler_params=pltpu.CompilerParams(
+            collective_id=3, has_side_effects=True, vmem_limit_bytes=62 * 2**20
+        ),
+        cost_estimate=pl.CostEstimate(flops=10**11, bytes_accessed=10**8, transcendentals=0),
+    )(two, cot_all, wgu_all, wd_all)
+
+
+class Spread:
+    def __init__(self, at, sums, near, relay, boxes, sems, local_sems):
+        self.at, self.sums, self.near, self.relay, self.boxes = at, sums, near, relay, boxes
+        self.sems, self.local_sems = sems, local_sems
+        self.half = at.n_fsdp // 2
+        self.by_relay = at.n_fsdp == 8
+        self.direct = [1, 2] if self.by_relay else list(range(1, self.half))
+        self.rows = sums.shape[1] // 2
+
+    def part(self, i, part):
+        return self.sums.at[i, pl.ds(part * self.rows, self.rows)]
+
+    def relay_copy(self, part):
+        return send(
+            self.part(3, part), self.relay.at[part],
+            self.sems.at[0, 3 + part], self.sems.at[1, 3 + part], self.at.near(1 + part),
+        )
+
+    def near_copy(self, i):
+        return send(
+            self.sums.at[i], self.near.at[i], self.sems.at[0, i], self.sems.at[1, i], self.at.near(i)
+        )
+
+    def start(self):
+        if self.by_relay:
+            for part in range(2):
+                self.relay_copy(part).start()
+        else:
+            for i in self.direct:
+                self.near_copy(i).start()
+
+    def add(self):
+        if not self.by_relay:
+            return
+        for part, i in ((0, 2), (1, 1)):
+            self.relay_copy(part).wait_recv()
+            takes = [
+                pltpu.make_async_copy(self.part(i, part), self.boxes.at[0], self.local_sems.at[0]),
+                pltpu.make_async_copy(self.relay.at[part], self.boxes.at[1], self.local_sems.at[1]),
+            ]
+            for take in takes:
+                take.start()
+            for take in takes:
+                take.wait()
+            self.boxes[0] = (self.boxes[0].astype(F32) + self.boxes[1].astype(F32)).astype(BF16)
+            keep = pltpu.make_async_copy(self.boxes.at[0], self.part(i, part), self.local_sems.at[0])
+            keep.start()
+            keep.wait()
+            self.near_copy(i).start()
+
+    def arrived(self):
+        for i in self.direct:
+            self.near_copy(i).wait_recv()
+
+    def finish(self):
+        if self.by_relay:
+            for part in range(2):
+                self.relay_copy(part).wait_send()
+        for i in self.direct:
+            self.near_copy(i).wait_send()
+
+
+class Pair:
+    def __init__(self, at, stage, sib, sums, inbox, sems, local_sems):
+        self.at, self.stage, self.sib, self.sums, self.inbox = at, stage, sib, sums, inbox
+        self.sems, self.local_sems = sems, local_sems
+
+    def sib_copy(self, i):
+        return send(
+            self.stage.at[lax.rem(i, 2)], self.sib.at[i], self.sems.at[0, i], self.sems.at[1, i], self.at.sibling()
+        )
+
+    def keep_copy(self, i):
+        return pltpu.make_async_copy(
+            self.stage.at[lax.rem(i, 2)], self.sums.at[i], self.local_sems.at[lax.rem(i, 2)]
+        )
+
+    def give(self, i, values):
+        pl.when(i >= 2)(lambda: self.sib_copy(i - 2).wait_send())
+        self.stage[lax.rem(i, 2)] = values().astype(BF16)
+        self.sib_copy(i).start()
+
+    def given(self, half):
+        for i in range(half - 2, half):
+            self.sib_copy(jnp.int32(i)).wait_send()
+
+    def keep(self, i, values):
+        self.sib_copy(i).wait_recv()
+        take = pltpu.make_async_copy(self.sib.at[i], self.inbox, self.local_sems.at[2])
+        take.start()
+        pl.when(i >= 2)(lambda: self.keep_copy(i - 2).wait())
+        own = values()
+        take.wait()
+        self.stage[lax.rem(i, 2)] = (own + self.inbox[...].astype(F32)).astype(BF16)
+        self.keep_copy(i).start()
+
+    def kept(self, half):
+        for i in range(half - 2, half):
+            self.keep_copy(jnp.int32(i)).wait()
+
+
+def norm_back(values, incoming, gain_row):
+    average = jnp.mean(values, axis=-1, keepdims=True)
+    centred = values - average
+    scale = lax.rsqrt(jnp.mean(centred * centred, axis=-1, keepdims=True) + NORM_EPS)
+    unit = centred * scale
+    grads = incoming * gain_row
+    inner = jnp.mean(grads * unit, axis=-1, keepdims=True)
+    back = scale * (grads - jnp.mean(grads, axis=-1, keepdims=True) - unit * inner)
+    return back, jnp.sum(incoming * unit, axis=0, keepdims=True), jnp.sum(incoming, axis=0, keepdims=True)
+
+
+def attend_back(widest, q_in, k_in, v_in, g_in, cos, s_low, s_high, starts, g_out, bias, kt, dk, dv, first_lane):
+    seq_len, width = q_in.shape
+    rows = min(256, seq_len)
+    lanes = pl.ds(pl.multiple_of(first_lane, LANES), LANES)
+    kt[...] = k_in[:, lanes].astype(F32).T.astype(BF16)
+    dk[...] = jnp.zeros_like(dk)
+    dv[...] = jnp.zeros_like(dv)
+
+    def put(part, here, values):
+        columns = pl.ds(pl.multiple_of(part * width + first_lane, LANES), LANES)
+        low = values.astype(BF16)
+        g_out[here, columns] = low
+        return jnp.sum(low.astype(F32), axis=0, keepdims=True)
+
+    total_q = jnp.zeros((1, LANES), F32)
+    for block in range(seq_len // rows):
+        here = slice(block * rows, (block + 1) * rows)
+        first, last = key_range(block, rows, widest)
+        query_rows = (q_in[here, lanes].astype(F32) * HEAD**-0.5).astype(BF16)
+        grad_rows = g_in[here, lanes]
+        query_cols = query_rows.astype(F32).T.astype(BF16)
+        grad_cols = grad_rows.astype(F32).T.astype(BF16)
+        head_down = lax.broadcasted_iota(jnp.int32, query_cols.shape, 0) // HEAD
+        head_along = lax.broadcasted_iota(jnp.int32, query_rows.shape, 1) // HEAD
+        none_down, none_along = jnp.zeros_like(query_cols), jnp.zeros_like(query_rows)
+        parts = []
+        for head in range(LANES // HEAD):
+            weights, total = seen_weights(
+                k_in[first:last, lanes],
+                jnp.where(head_down == head, query_cols, none_down),
+                starts[:, here],
+                first,
+                block * rows,
+            )
+            probs = weights * (1.0 / total)
+            grad_probs = dot(
+                v_in[first:last, lanes], jnp.where(head_down == head, grad_cols, none_down), NN
+            )
+            inner = jnp.sum(probs * grad_probs, axis=0, keepdims=True)
+            grad_scores = (probs * (grad_probs - inner)).astype(BF16)
+            dk[first:last, :] += dot(
+                grad_scores, jnp.where(head_along == head, query_rows, none_along), NN
+            )
+            dv[first:last, :] += dot(
+                probs.astype(BF16), jnp.where(head_along == head, grad_rows, none_along), NN
+            )
+            parts.append(dot(kt[head * HEAD : (head + 1) * HEAD, first:last], grad_scores, NN))
+        grad_queries = jnp.concatenate(parts, axis=0).T * HEAD**-0.5
+        total_q = total_q + put(
+            0, here, turn(grad_queries, cos[here, :], -s_low[here, :], -s_high[here, :])
+        )
+    everywhere = slice(0, seq_len)
+    bias[4:5, lanes] = total_q
+    bias[5:6, lanes] = put(1, everywhere, turn(dk[...], cos[...], -s_low[...], -s_high[...]))
+    bias[6:7, lanes] = put(2, everywhere, dv[...])
+
+
+def back_kernel(
+    sizes, widest,
+    gn2, resid, tok, cot, att_own, wo_all, wq_all, q_in, k_in, v_in, one, sum_gu_in, sum_d_in,
+    rows_in, cos, s_low, s_high, starts,
+    grad_tok, small_out, near_gu, near_d, own_gu, own_d, sum_q, near_q, sib_q, relay_q,
+    sum_o, near_o, sib_o, relay_o, zo, relay_gu, relay_d,
+    gres, res_v, tok_v, cot_v, att_v, gattn, wo_v, wq_v, q_v, k_v, v_v, gp, gatt, ghead, came, going,
+    kt, dk, dv, stage_o, inbox_o, stage_q, inbox_q, box_gu, box_d, box_o, box_q, zo_stage, zo_box,
+    norm_sums, bias, tiles, land_z, land_near, land_sib,
+    swap_send, swap_recv, fold_send, fold_recv, pair_o_sems, pair_q_sems, gu_sems, d_sems, o_sems, q_sems,
+    zo_sems, small_sems, local_sems, pair_o_local, pair_q_local,
+):
+    n_fsdp, n_tp = sizes
+    half = n_fsdp // 2
+    bits = half.bit_length() - 1
+    at = Places(n_fsdp, n_tp)
+    slab, model = tok.shape
+    seq_len, width = q_in.shape
+    part_rows = model // n_fsdp
+    pairs = width // LANES
+    loads = [
+        pltpu.make_async_copy(src, dst, local_sems.at[i])
+        for i, (src, dst) in enumerate(
+            [
+                (gn2, gres), (resid, res_v), (cot, cot_v), (wo_all, wo_v), (tok, tok_v), (att_own, att_v),
+                (q_in, q_v), (k_in, k_v), (v_in, v_v), (wq_all, wq_v),
+            ]
+        )
+    ]
+    for load in loads:
+        load.start()
+    at.greet()
+    spread_gu = Spread(at, own_gu, near_gu, relay_gu, box_gu, gu_sems, local_sems.at[pl.ds(13, 2)])
+    spread_d = Spread(at, own_d, near_d, relay_d, box_d, d_sems, local_sems.at[pl.ds(13, 2)])
+    spread_o = Spread(at, sum_o, near_o, relay_o, box_o, o_sems, local_sems.at[pl.ds(13, 2)])
+    spread_q = Spread(at, sum_q, near_q, relay_q, box_q, q_sems, local_sems.at[pl.ds(13, 2)])
+    spread_gu.start()
+    spread_d.start()
+    norm_sums[...] = jnp.zeros_like(norm_sums)
+    bias[...] = jnp.zeros_like(bias)
+    for load in loads[:4]:
+        load.wait()
+
+    step = 16
+
+    def second(i, carry):
+        here = pl.ds(pl.multiple_of(i * step, step), step)
+        back, gain, shift = norm_back(res_v[here, :], gres[here, :], rows_in[1:2, :])
+        total = cot_v[here, :].astype(F32) + back
+        gres[here, :] = total
+        gattn[here, :] = total.astype(BF16)
+        norm_sums[1:2, :] = norm_sums[1:2, :] + gain
+        norm_sums[3:4, :] = norm_sums[3:4, :] + shift
+        return carry
+
+    lax.fori_loop(0, slab // step, second, 0)
+
+    def swap_copy(i, k):
+        lanes = pl.ds(pl.multiple_of(i * LANES, LANES), LANES)
+        other = lax.rem(at.t + k, n_tp)
+        return send(
+            ghead.at[other, :, lanes],
+            gatt.at[pl.ds(pl.multiple_of(at.t * slab, slab), slab), lanes],
+            swap_send.at[i, k], swap_recv.at[i, k], at.along(other),
+        )
+
+    def give_heads(i, carry):
+        lanes = pl.ds(pl.multiple_of(i * LANES, LANES), LANES)
+
+        def to(k, carry):
+            other = lax.rem(at.t + k, n_tp)
+            rows = pl.ds(pl.multiple_of(other * width + i * LANES, LANES), LANES)
+            ghead[other, :, lanes] = dot(gattn[...], wo_v[rows, :], NT).astype(BF16)
+            pl.when(k > 0)(lambda: swap_copy(i, k).start())
+            return carry
+
+        lax.fori_loop(0, n_tp, to, 0)
+        gatt[pl.ds(pl.multiple_of(at.t * slab, slab), slab), lanes] = ghead[at.t, :, lanes]
+        return carry
+
+    lax.fori_loop(0, pairs, give_heads, 0)
+
+    loads[5].wait()
+    pair_o = Pair(at, stage_o, sib_o, sum_o, inbox_o, pair_o_sems, pair_o_local)
+    pair_q = Pair(at, stage_q, sib_q, sum_q, inbox_q, pair_q_sems, pair_q_local)
+
+    def piece(f):
+        return pl.ds(pl.multiple_of(f * part_rows, part_rows), part_rows)
+
+    def owner(i, core):
+        return xor_any(at.chip, i, bits) * 2 + core
+
+    def give_o(i, carry):
+        pair_o.give(i, lambda: dot(att_v[...], gattn[:, piece(owner(i, 1 - at.core))], TN))
+        return carry
+
+    lax.fori_loop(0, half, give_o, 0)
+    for load in loads[6:9]:
+        load.wait()
+    load_one = pltpu.make_async_copy(one, wo_v.at[pl.ds(0, seq_len), :], local_sems.at[12])
+    load_one.start()
+
+    def some_heads(i, carry):
+        for k in range(1, n_tp):
+            source = lax.rem(at.t + n_tp - k, n_tp)
+            lanes = pl.ds(pl.multiple_of(i * LANES, LANES), LANES)
+            came_rows = gatt.at[pl.ds(pl.multiple_of(source * slab, slab), slab), lanes]
+            send(came_rows, came_rows, swap_send.at[i, k], swap_recv.at[i, k], at.along(source)).wait_recv()
+        attend_back(
+            widest, q_v, k_v, v_v, gatt, cos, s_low, s_high, starts, gp, bias, kt, dk, dv, i * LANES
+        )
+        return carry
+
+    lax.fori_loop(0, pairs, some_heads, 0)
+
+    loads[9].wait()
+    fold = Fold(at, grad_tok, going, came, min(512, model), fold_send, fold_recv)
+
+    def term(slot):
+        rows = gp[pl.ds(pl.multiple_of(slot * slab, slab), slab), :]
+
+        def some(c, carry):
+            fold.put(slot, c, dot(rows, wq_v[fold.lanes(c), :], NT))
+            return carry
+
+        lax.fori_loop(0, fold.tiles, some, 0)
+
+    def far_first(i, carry):
+        s = (2 * n_tp - 1 - i) // 2
+        slot = at.t + s * (2 * lax.rem(i, 2) - 1)
+        pl.when((slot >= 0) & (slot < n_tp))(lambda: term(slot))
+        return carry
+
+    lax.fori_loop(0, 2 * n_tp - 1, far_first, 0)
+
+    spread_gu.add()
+    spread_d.add()
+    pair_o.given(half)
+
+    def forward(key, i):
+        pl.when(i < fold.tiles)(lambda: fold.forward(key, i))
+
+    def keep_o(i, carry):
+        forward(n_tp - 1, i)
+        pair_o.keep(i, lambda: dot(att_v[...], gattn[:, piece(owner(i, at.core))], TN))
+        return carry
+
+    lax.fori_loop(0, half, keep_o, 0)
+    pair_o.kept(half)
+    spread_o.start()
+    load_one.wait()
+
+    def give_q(i, carry):
+        forward(n_tp - 2, i)
+        pair_q.give(i, lambda: dot(wo_v[0:seq_len, piece(owner(i, 1 - at.core))], gp[...], TN))
+        return carry
+
+    lax.fori_loop(0, half, give_q, 0)
+    pair_q.given(half)
+
+    def keep_q(i, carry):
+        pair_q.keep(i, lambda: dot(wo_v[0:seq_len, piece(owner(i, at.core))], gp[...], TN))
+        return carry
+
+    lax.fori_loop(0, half, keep_q, 0)
+    pair_q.kept(half)
+    spread_q.start()
+    spread_o.add()
+    for key in range(n_tp - 3, 0, -1):
+        for c in range(fold.tiles):
+            fold.forward(key, c)
+    spread_q.add()
+
+    each = model // n_tp
+    spread_o.arrived()
+
+    def zo_copy(k):
+        other = lax.rem(at.t + k, n_tp)
+        return send(zo_stage.at[other], zo.at[at.t], zo_sems.at[0, k], zo_sems.at[1, k], at.along(other))
+
+    def group(k, carry):
+        other = lax.rem(at.t + k, n_tp)
+        rows = pl.ds(pl.multiple_of(other * each, each), each)
+        takes = [
+            pltpu.make_async_copy(
+                (sum_o if i == 0 else near_o).at[i, rows, :], zo_box.at[n], local_sems.at[16 + n]
+            )
+            for n, i in enumerate([0] + spread_o.direct)
+        ]
+        for take in takes:
+            take.start()
+        total = jnp.zeros(zo_box.shape[1:], F32)
+        for n, take in enumerate(takes):
+            take.wait()
+            total = total + zo_box[n].astype(F32)
+        zo_stage[other] = total.astype(BF16)
+        pl.when(k > 0)(lambda: zo_copy(k).start())
+        return carry
+
+    lax.fori_loop(0, n_tp, group, 0)
+    own_zo = pltpu.make_async_copy(zo_stage.at[at.t], zo.at[at.t], local_sems.at[15])
+    own_zo.start()
+
+    fold.end()
+    loads[4].wait()
+
+    def first(i, carry):
+        here = pl.ds(pl.multiple_of(i * step, step), step)
+        back, gain, shift = norm_back(tok_v[here, :].astype(F32), grad_tok[here, :], rows_in[0:1, :])
+        grad_tok[here, :] = gres[here, :] + back
+        norm_sums[0:1, :] = norm_sums[0:1, :] + gain
+        norm_sums[2:3, :] = norm_sums[2:3, :] + shift
+        return carry
+
+    lax.fori_loop(0, slab // step, first, 0)
+
+    lanes_each = model // (n_fsdp * n_tp)
+    kept = lax.broadcasted_iota(jnp.int32, (8, LANES), 1) < lanes_each
+
+    def tile_of(ref, index):
+        start = index * lanes_each
+        tile = ref[:, start // LANES * LANES : start // LANES * LANES + LANES]
+        return jnp.where(kept, pltpu.roll(tile, (LANES - start % LANES) % LANES, 1), 0.0)
+
+    for f in range(n_fsdp):
+        for t in range(n_tp):
+            tiles[t, f] = tile_of(norm_sums, f * n_tp + t)
+    for f in range(n_fsdp):
+        tiles[at.t, f] = tiles[at.t, f] + tile_of(bias, f)
+
+    def z_copy(k):
+        other = lax.rem(at.t + k, n_tp)
+        return send(
+            tiles.at[other], land_z.at[k], small_sems.at[0, half + k], small_sems.at[1, half + k], at.along(other)
+        )
+
+    for k in range(1, n_tp):
+        z_copy(k).start()
+    total = tiles[at.t]
+    for k in range(1, n_tp):
+        z_copy(k).wait_recv()
+        total = total + land_z[k]
+    land_z[0] = total
+
+    def chip_copy(k):
+        return send(
+            land_z.at[0, pl.ds(xor(at.chip, k) * 2, 2)], land_near.at[k],
+            small_sems.at[0, k], small_sems.at[1, k], at.near(k),
+        )
+
+    for k in range(1, half):
+        chip_copy(k).start()
+    total = land_z[0, pl.ds(at.chip * 2, 2)]
+    for k in range(1, half):
+        chip_copy(k).wait_recv()
+        total = total + land_near[k]
+    land_near[0] = total
+    to_sib = send(
+        land_near.at[0, 1 - at.core], land_sib, small_sems.at[0, 0], small_sems.at[1, 0], at.sibling()
+    )
+    to_sib.start()
+    to_sib.wait_recv()
+    small_out[...] = land_near[0, at.core] + land_sib[...]
+
+    to_sib.wait_send()
+    for k in range(1, half):
+        chip_copy(k).wait_send()
+    for k in range(1, n_tp):
+        z_copy(k).wait_send()
+        zo_copy(k).wait_send()
+        source = lax.rem(at.t + n_tp - k, n_tp)
+        send(zo.at[source], zo.at[source], zo_sems.at[0, k], zo_sems.at[1, k], at.along(source)).wait_recv()
+    own_zo.wait()
+
+    def swapped(i, carry):
+        for k in range(1, n_tp):
+            swap_copy(i, k).wait_send()
+        return carry
+
+    lax.fori_loop(0, pairs, swapped, 0)
+    fold.finish()
+    for spread in (spread_gu, spread_d, spread_q):
+        spread.arrived()
+    for spread in (spread_gu, spread_d, spread_q, spread_o):
+        spread.finish()
+
+
+def back(sizes, widest, gn2, resid, tok, cot, att_own, wo_all, wq_all, q_in, k_in, v_in, one, sum_gu, sum_d, rows_in, tables, starts):
+    n_fsdp, n_tp = sizes
+    half = n_fsdp // 2
+    slab, model = tok.shape
+    seq_len, width = q_in.shape
+    hidden = sum_d.shape[1]
+    part_rows = model // n_fsdp
+    pairs = width // LANES
+    each = model // n_tp
+    tile = min(512, model)
+    hbm = pl.BlockSpec(memory_space=pl.ANY)
+    vmem = pl.BlockSpec(memory_space=pltpu.VMEM)
+    shape = jax.ShapeDtypeStruct
+    piece_q, piece_o = (part_rows, 3 * width), (model, part_rows)
+    piece_gu, piece_d = sum_gu.shape[1:], sum_d.shape[1:]
+    halved = lambda piece: (piece[0] // 2,) + tuple(piece[1:])
+    outs = [
+        (shape((slab, model), F32), vmem),
+        (shape((8, LANES), F32), vmem),
+        (shape(sum_gu.shape, BF16), hbm),
+        (shape(sum_d.shape, BF16), hbm),
+        (shape(sum_gu.shape, BF16), hbm),
+        (shape(sum_d.shape, BF16), hbm),
+        (shape((half,) + piece_q, BF16), hbm),
+        (shape((half,) + piece_q, BF16), hbm),
+        (shape((half,) + piece_q, BF16), hbm),
+        (shape((2,) + halved(piece_q), BF16), hbm),
+        (shape((half,) + piece_o, BF16), hbm),
+        (shape((half,) + piece_o, BF16), hbm),
+        (shape((half,) + piece_o, BF16), hbm),
+        (shape((2,) + halved(piece_o), BF16), hbm),
+        (shape((n_tp, each, part_rows), BF16), hbm),
+        (shape((2,) + halved(piece_gu), BF16), hbm),
+        (shape((2,) + halved(piece_d), BF16), hbm),
+    ]
+    dma = pltpu.SemaphoreType.DMA
+    return pl.pallas_call(
+        functools.partial(back_kernel, sizes, widest),
+        in_specs=[hbm] * 13 + [vmem] * 5,
+        out_specs=[spec for _, spec in outs],
+        out_shape=[out for out, _ in outs],
+        scratch_shapes=[
+            pltpu.VMEM((slab, model), F32),
+            pltpu.VMEM((slab, model), F32),
+            pltpu.VMEM((slab, model), BF16),
+            pltpu.VMEM((slab, model), BF16),
+            pltpu.VMEM((slab, model), BF16),
+            pltpu.VMEM((slab, model), BF16),
+            pltpu.VMEM((model, model), BF16),
+            pltpu.VMEM((model, 3 * width), BF16),
+            pltpu.VMEM((seq_len, width), BF16),
+            pltpu.VMEM((seq_len, width), BF16),
+            pltpu.VMEM((seq_len, width), BF16),
+            pltpu.VMEM((seq_len, 3 * width), BF16),
+            pltpu.VMEM((seq_len, width), BF16),
+            pltpu.VMEM((n_tp, slab, width), BF16),
+            pltpu.VMEM((n_tp + 1, slab, model), BF16),
+            pltpu.VMEM((n_tp, slab, model), BF16),
+            pltpu.VMEM((LANES, seq_len), BF16),
+            pltpu.VMEM((seq_len, LANES), F32),
+            pltpu.VMEM((seq_len, LANES), F32),
+            pltpu.VMEM((2,) + piece_o, BF16),
+            pltpu.VMEM(piece_o, BF16),
+            pltpu.VMEM((2,) + piece_q, BF16),
+            pltpu.VMEM(piece_q, BF16),
+            pltpu.VMEM((2,) + halved(piece_gu), BF16),
+            pltpu.VMEM((2,) + halved(piece_d), BF16),
+            pltpu.VMEM((2,) + halved(piece_o), BF16),
+            pltpu.VMEM((2,) + halved(piece_q), BF16),
+            pltpu.VMEM((n_tp, each, part_rows), BF16),
+            pltpu.VMEM((half, each, part_rows), BF16),
+            pltpu.VMEM((8, model), F32),
+            pltpu.VMEM((8, width), F32),
+            pltpu.VMEM((n_tp, n_fsdp, 8, LANES), F32),
+            pltpu.VMEM((n_tp, n_fsdp, 8, LANES), F32),
+            pltpu.VMEM((half, 2, 8, LANES), F32),
+            pltpu.VMEM((8, LANES), F32),
+            dma((pairs, n_tp)), dma((pairs, n_tp)),
+            dma((n_tp, model // tile)), dma((n_tp + 1, model // tile)),
+            dma((2, half)), dma((2, half)),
+            dma((2, half + 1)), dma((2, half + 1)), dma((2, half + 1)), dma((2, half + 1)),
+            dma((2, n_tp)), dma((2, half + n_tp)), dma((16 + half,)), dma((3,)), dma((3,)),
+        ],
+        input_output_aliases={11: 4, 12: 5},
+        compiler_params=pltpu.CompilerParams(
+            collective_id=2, has_side_effects=True, vmem_limit_bytes=62 * 2**20
+        ),
+        cost_estimate=pl.CostEstimate(flops=10**11, bytes_accessed=10**8, transcendentals=0),
+    )(
+        gn2, resid, tok, cot, att_own, wo_all, wq_all, q_in, k_in, v_in, one, sum_gu, sum_d,
+        rows_in, *tables, starts,
+    )
 
 
 def reduce_rows(values):
@@ -790,82 +1455,43 @@
 
     tile = jnp.concatenate([ln_gains, ln_shifts, b_qkv.astype(F32), jnp.zeros((1, small), F32)], 0)
     tile = jnp.pad(tile, ((0, 0), (0, LANES - small)))
-    token_rows = tokens.astype(F32)
     (
         full_one, queries, key_vals, value_rows, residual, normed_two, norm_rows_all, attended_own,
         grad_branch, qkv_all, out_all, gu_all, down_all,
     ) = front(
         sizes, widest, tokens, cotangent, w_qkv.reshape(part_rows, 3 * local_width), w_out,
-        w_gate_up.reshape(part_rows, 2 * hidden_width), w_down, tile, tables, starts_row,
+        w_gate_up.transpose(1, 0, 2), w_down, tile, tables, starts_row,
     )
     full_one = full_one.reshape(seq_len, model_width)
-    grad_branch = grad_branch.reshape(seq_len, model_width)
-    gains_all, shifts_all = norm_rows_all[0:2], norm_rows_all[2:4]
-
-    full_two = gather_rows(normed_two)
-    gate_up = dot(full_two, gu_all, NN)
-    gate, up = gate_up[:, :hidden_width], gate_up[:, hidden_width:]
-    hidden_low = swiglu(gate, up).astype(BF16)
+
+    grad_normed_two, hidden_low, sum_gu, sum_down, _, _ = middle(
+        sizes, normed_two, grad_branch, gu_all, down_all
+    )
+    (
+        grad_tokens, shares, near_gu, near_down, own_gu, own_down, sum_qkv, near_qkv, _, _, _, _, _, _,
+        out_parts, _, _,
+    ) = back(
+        sizes, widest, grad_normed_two, residual, tokens, cotangent, attended_own, out_all, qkv_all,
+        queries, key_vals, value_rows, full_one, sum_gu, sum_down, norm_rows_all, tables, starts_row,
+    )
     branch = reduce_rows(dot(hidden_low, down_all, NN))
     result = (residual + branch).astype(BF16)
-    grad_out = cotangent.astype(F32)
-    grad_hidden = dot(grad_branch, down_all, NT)
-    _, swiglu_pull = jax.vjp(swiglu, gate, up)
-    grad_gate, grad_up = swiglu_pull(grad_hidden)
-    grad_gate_up = jnp.concatenate([grad_gate, grad_up], axis=1).astype(BF16)
-    grad_normed_two = reduce_rows(dot(grad_gate_up, gu_all, NT))
-    grad_gu = dot(full_two, grad_gate_up, TN).astype(BF16)
-    grad_down = dot(grad_branch, hidden_low, TN).astype(BF16)
-    gu_share = scatter_fsdp(grad_gu.reshape(n_fsdp, part_rows, 2 * hidden_width), n_fsdp)
-    down_share = scatter_fsdp(grad_down.reshape(n_fsdp, part_rows, hidden_width), n_fsdp)
-    _, second_pull = jax.vjp(layer_norm, residual, gains_all[1], shifts_all[1])
-    grad_resid_norm, grad_gain_two, grad_shift_two = second_pull(grad_normed_two)
-    grad_residual = grad_out + grad_resid_norm
-
-    grad_attn = grad_residual.astype(BF16)
-    grad_o = dot(grad_attn, attended_own, TN).astype(BF16)
-    grad_attended_own = dot(grad_attn, out_all, NT).astype(BF16)
-    grad_attended = swap_tp(
-        grad_attended_own.reshape(slab_rows, n_tp, local_width).transpose(1, 0, 2), n_tp
-    ).reshape(seq_len, local_width)
-    grad_projected, grad_bias = attend_backward(
-        queries, key_vals, value_rows, grad_attended, tables, starts_row, widest
-    )
-    grad_projected = grad_projected.transpose(1, 0, 2).reshape(seq_len, 3 * local_width)
-    grad_qkv = dot(full_one, grad_projected, TN).astype(BF16)
-    grad_normed_one = reduce_rows(dot(grad_projected, qkv_all, NT))
-    _, first_pull = jax.vjp(layer_norm, token_rows, gains_all[0], shifts_all[0])
-    grad_token_norm, grad_gain_one, grad_shift_one = first_pull(grad_normed_one)
-    grad_tokens = grad_residual + grad_token_norm
-
-    out_share = scatter_fsdp(grad_o.reshape(n_fsdp, part_rows, model_width), n_fsdp).astype(BF16)
-    out_share = jnp.sum(
-        swap_tp(out_share.reshape(part_rows, n_tp, local_width).transpose(1, 0, 2), n_tp).astype(F32),
-        axis=0,
-    ).T
-    qkv_share = scatter_fsdp(grad_qkv.reshape(n_fsdp, part_rows, 3 * local_width), n_fsdp)
-
-    count = n_fsdp * n_tp
-    norm_grads = jnp.stack([grad_gain_one, grad_gain_two, grad_shift_one, grad_shift_two])
-    norm_grads = norm_grads.reshape(4, count, small).transpose(1, 0, 2)
-    bias_grads = grad_bias.reshape(3, n_fsdp, small).transpose(1, 0, 2)
-    bias_grads = jnp.where(
-        (jnp.arange(n_tp) == at_tp)[None, :, None, None], bias_grads[:, None], 0.0
-    ).reshape(count, 3, small)
-    tiles = jnp.concatenate([norm_grads, bias_grads, jnp.zeros((count, 1, small), F32)], axis=1)
-    tiles = jnp.pad(tiles, ((0, 0), (0, 0), (0, LANES - small)))
-    shares = jnp.sum(exchange(tiles, sizes, True, 2), axis=0)[:, :small]
-
+    direct = [1, 2] if n_fsdp == 8 else list(range(1, n_fsdp // 2))
+
+    def total(sums, near):
+        return sum([near[i].astype(F32) for i in direct], sums[0].astype(F32))
+
+    shares = shares[:, :small]
     return (
         result,
         grad_tokens,
         shares[0:2],
         shares[2:4],
-        qkv_share.reshape(part_rows, 3, local_width),
+        total(sum_qkv, near_qkv).reshape(part_rows, 3, local_width),
         shares[4:7],
-        out_share,
-        gu_share.reshape(part_rows, 2, hidden_width),
-        down_share.T,
+        jnp.sum(out_parts.astype(F32), axis=0),
+        total(own_gu, near_gu).transpose(1, 0, 2),
+        total(own_down, near_down),
     )
 
 

time: 814 us -> 651 us (0.80)
  Pallas kernels: 241 us -> 587 us
  waiting for transfers between devices: 252 us -> 0.02 us
  matrix products: 119 us -> 11 us
  local copies, waits for them, and re-layouts: 93.8 us -> 13.5 us
  other arithmetic: 52.8 us -> 17 us
  starting transfers between devices: 32 us -> 0.04 us
    pallas_call x2, Pallas kernels: 36.6 us -> 382 us  [the longest x1 218 us: back(): pl.pallas_call(functools.partial(back_kernel, sizes, widest), in_specs=[h...]
    dot_general x10 -> x1, matrix products: 119 us -> 11 us  [dot(): return lax.dot_general(left, right, dims, preferred_element_type=F32)]
    ppermute x22 -> x0, waiting for transfers between devices: 89.7 us -> none  [hop(): return lax.ppermute(values, axis, [(i, partner(i)) for i in range(size)])]
    reduce_scatter x3 -> x1, waiting for transfers between devices: 81.8 us -> 0.01 us  [reduce_rows(): lax.psum_scatter(values.astype(BF16), 'tp', scatter_dimension=0, tiled=True)]
    all_gather x1 -> x0, waiting for transfers between devices: 80.6 us -> none  [gather_rows(): return lax.all_gather(values, 'tp', axis=0, tiled=True)]
    ppermute x22 -> x0, starting transfers between devices: 31.5 us -> none  [hop(): return lax.ppermute(values, axis, [(i, partner(i)) for i in range(size)])]
    dynamic_slice x6 -> x0, local copies, waits for them, and re-layouts: 25.2 us -> none  [the longest x3 15.6 us: scatter_fsdp(): other = lax.dynamic_index_in_dim(pairs, 1 - core, 1, keepdims=False)]
    unnamed x64 -> x19, local copies, waits for them, and re-layouts: 33.3 us -> 9.42 us
  transfers between devices with their start and end apart: 26 -> 1, of which waited for: 13 -> 0; matrix products, arithmetic and copies ran while one was open for 22% -> 2% of each run, Pallas kernels for 3% -> 34%
where the time goes in v3:
time: 651 us; the launch traced here: 643 us
  Pallas kernels  587 us (90%)
  other arithmetic  17 us (3%)
  between operations  14.6 us (2%)
  local copies, waits for them, and re-layouts  13.5 us (2%)
  matrix products  11 us (2%)
    pallas_call x1, Pallas kernels, back(): pl.pallas_call(functools.partial(back_kernel, sizes, widest), in_specs=[h...  218 us
    pallas_call x1, Pallas kernels, front(): pl.pallas_call(functools.partial(front_kernel, sizes, widest), in_specs=[...  206 us
    pallas_call x1, Pallas kernels, middle(): pl.pallas_call(functools.partial(middle_kernel, sizes), in_specs=[hbm] *...  164 us
  transfers between devices with their start and end apart: 1, of which 0 were waited for; matrix products, arithmetic and copies ran while one was open for 2% of the time, Pallas kernels for 34%

profile of v3, /device:TPU:0, one launch (start us, length us, event | category | flops | bytes accessed | tf_op | source)
XLA Modules:
  0.0 643.4 jit_solution(1422813626394314794)
XLA Ops:
  7.2 0.0 copy-start.2
  7.2 0.0 reduce-scatter.2.cloned.1.call-start
  7.3 0.8 convert_element_type.71
  8.1 0.1 pad.8.clone
  8.1 0.8 maximum_maximum_fusion
  8.9 0.6 pad.4.tile
  9.5 0.8 reduce-window.8
  10.3 0.7 select_reduce_fusion
  11.1 0.0 copy-start.5
  11.1 1.4 copy.31
  12.5 1.2 copy.33.wq
  13.6 0.0 copy-done.2
  13.6 1.2 copy.38
  14.9 0.0 copy-done.5
  14.9 3.2 fusion
  18.1 205.6 %shard_map.169 = (bf16[4,256,2048]{2,1,0:T(8,128)(2,1)}, bf16[1024,512]{1,0:T(8,128)(2,1)}, bf16[1024,512]{1,0:T(8,128)(2,1)}, bf16[1024,512]{1,0:T(8,128)(2,1)}...) custom-call(bf16[256,2048]{1,0:T(8,128)(2,1)} %tok.3, ...), custom_call_target="tpu_custom_call" | custom-call | flops 99999997952 | bytes 100000000 | tf_op jit(solution)/shard_map/pallas_call | solution.py:547
  223.6 164.1 %shard_map.170 = (f32[256,2048]{1,0:T(8,128)}, bf16[1024,1408]{1,0:T(8,128)(2,1)}, bf16[4,2,256,1408]{3,2,1,0:T(8,128)(2,1)}, bf16[4,1408,256]{2,1,0:T(8,128)(2,...) custom-call(bf16[256,2048]{1,0:T(8,128)(2,1)} %get-tuple-element.36.two, ...), custom_call_target="tpu_custom_call" | custom-call | flops 99999997952 | bytes 100000000 | tf_op jit(solution)/shard_map/pallas_call | solution.py:846
  387.8 11.0 %convolution_convert_fusion = bf16[1024,2048]{1,0:T(8,128)(2,1)} fusion(bf16[1024,1408]{1,0:T(8,128)(2,1)} %get-tuple-element.40, bf16[1408,2048]{1,0:T(8,128)(2,1)} %get-tuple-element.39.wd_all), kind=kOutput, calls=%fused_computation | convolution fusion | flops 5907677184 | bytes 12845056 | tf_op jit(solution)/shard_map/dot_general | solution.py:23
  398.7 0.0 reduce-scatter.2.cloned.1.call-update
  398.7 217.5 %shard_map.171 = (f32[256,2048]{1,0:T(8,128)}, f32[8,128]{1,0:T(8,128)}, bf16[4,2,256,1408]{3,2,1,0:T(8,128)(2,1)}, bf16[4,1408,256]{2,1,0:T(8,128)(2,1)}, bf16[...) custom-call(f32[256,2048]{1,0:T(8,128)} %get-tuple-element.41.gn2, ...), custom_call_target="tpu_custom_call", output_to_operand_aliasing={{4}: (11, {}), {5}: (12, {})} | custom-call | flops 99999997952 | bytes 100000000 | tf_op jit(solution)/shard_map/pallas_call | solution.py:1366
  616.3 1.3 slice.45
  617.6 1.9 convert_add_fusion
  619.4 0.5 copy.34
  619.9 1.6 copy.35
  621.5 2.7 add_bitcast_fusion
  624.2 0.0 copy-start.3
  624.2 0.0 copy-start.6
  624.2 0.0 copy-start.4
  624.3 3.8 copy.36
  628.1 0.0 copy-start
  628.1 0.0 copy-done.3
  628.1 0.9 convert_reduce_fusion
  629.0 0.0 copy-done.6
  629.0 0.6 fusion.8
  629.6 0.0 copy-done.4
  629.6 2.5 add_bitcast_fusion.1
  632.1 0.0 reduce-scatter.2.cloned.1.call-done
  632.1 0.0 copy-done
  632.1 0.0 copy-start.1
  632.1 2.6 add_convert_fusion
  634.7 0.0 copy-done.1
  634.8 1.3 copy.42
  (4 shorter events, 0.0 us)
Async XLA Ops:
  7.2 6.5 %copy-start.2 = (bf16[256,2,1408]{2,1,0:T(2,128)(2,1)S(1)}, bf16[256,2,1408]{2,1,0:T(2,128)(2,1)}, u32[]{:S(2)}) copy-start(bf16[256,2,1408]{2,1,0:T(2,128)(2,1)} %param.17) | copy-start | bytes 4325380
  7.2 624.9 %reduce-scatter.2.cloned.1.call-start = ((), (), s32[]{:S(2)}) async-start(), calls=%async_computation.1 | async-start | bytes 5242880 | tf_op jit(solution)/shard_map/reduce_scatter | solution.py:1425
  11.1 3.8 copy-start.5
  624.2 3.8 copy-start.3
  624.2 4.8 copy-start.6
  624.2 5.3 copy-start.4
  628.1 4.1 copy-start
  632.1 2.6 copy-start.1
Sparse Core Ops, SparseCore 0:
  398.9 119.1 reduce-scatter.1

commit v4 on v3

--- a/solution.py
+++ b/solution.py
@@ -114,22 +114,34 @@
         pl.when(at.t < at.n_tp - 1)(lambda: self.copy(at.t, 0, True).start())
         pl.when(at.t > 0)(lambda: self.copy(at.t, 1, True).start())
 
-    def step(self, s):
+    def start_inner(self):
+        at = self.at
+        pl.when(at.t < at.n_tp - 2)(lambda: self.copy(at.t, 0, True).start())
+        pl.when(at.t > 1)(lambda: self.copy(at.t, 1, True).start())
+
+    def start_outer(self):
+        at = self.at
+        pl.when(at.t == at.n_tp - 2)(lambda: self.copy(at.t, 0, True).start())
+        pl.when(at.t == 1)(lambda: self.copy(at.t, 1, True).start())
+
+    def step(self, s, on=True):
         at = self.at
 
         @pl.when(at.t >= s)
         def _():
             self.copy(at.t - s, 0, False).wait_recv()
-            pl.when(at.t < at.n_tp - 1)(lambda: self.copy(at.t - s, 0, False).start())
+            if on:
+                pl.when(at.t < at.n_tp - 1)(lambda: self.copy(at.t - s, 0, False).start())
 
         @pl.when(at.t + s < at.n_tp)
         def _():
             self.copy(at.t + s, 1, False).wait_recv()
-            pl.when(at.t > 0)(lambda: self.copy(at.t + s, 1, False).start())
-
-    def finish(self):
+            if on:
+                pl.when(at.t > 0)(lambda: self.copy(at.t + s, 1, False).start())
+
+    def finish(self, last=None):
         at = self.at
-        for s in range(at.n_tp):
+        for s in range(at.n_tp if last is None else last):
             pl.when((at.t >= s) & (at.t < at.n_tp - 1))(
                 lambda s=s: self.copy(at.t - s, 0, s == 0).wait_send()
             )
@@ -406,8 +418,11 @@
                 came = wo_rows(lax.rem(at.t + n_tp - k, n_tp))
                 send(came, came, wz_sems.at[0, k], wz_sems.at[1, k], at.along(at.t)).wait_recv()
             weights[1].start()
+        if s == 2:
+            weights[0].pass_last()
+            weights[2].start()
+            grads.start_inner()
         each_from(s, s + 1, normalise)
-    weights[0].pass_last()
     own_copies[1].wait()
     weights[0].complete()
     load = pltpu.make_async_copy(wq_all, wq_v, local_sems.at[6])
@@ -415,10 +430,9 @@
     load.wait()
     each_from(0, n_tp - 1, project)
     weights[1].pass_on()
-    weights[2].start()
     weights[3].start()
     line.step(n_tp - 1)
-    grads.start()
+    grads.start_outer()
     each_from(n_tp - 1, n_tp, normalise)
     each_from(n_tp - 1, n_tp, project)
 
@@ -438,10 +452,11 @@
             swap_copy(i, k).start()
         columns = pl.ds(pl.multiple_of(at.t * width + i * LANES, LANES), LANES)
         att[:, columns] = heads[at.t, :, lanes]
+        pl.when(i == width // LANES // 2 - 1)(weights[1].pass_last)
         return carry
 
     lax.fori_loop(0, width // LANES, some_heads, 0)
-    weights[1].pass_last()
+    weights[2].pass_on()
     weights[1].complete()
     load = pltpu.make_async_copy(wo_all, wo_v, local_sems.at[7])
     load.start()
@@ -466,6 +481,7 @@
         return carry
 
     lax.fori_loop(0, model // wide, out_columns, 0)
+    weights[3].pass_on()
 
     def second_norm(i, carry):
         here = pl.ds(pl.multiple_of(i * 32, 32), 32)
@@ -474,19 +490,17 @@
 
     lax.fori_loop(0, slab // 32, second_norm, 0)
 
-    weights[2].pass_on()
-    weights[3].pass_on()
-    for s in range(2, n_tp):
-        grads.step(s)
     weights[2].pass_last()
     weights[3].pass_last()
+    for s in range(2, n_tp - 1):
+        grads.step(s, on=s < n_tp - 2)
     for copy in own_copies[3:]:
         copy.wait()
     weights[2].complete()
     weights[3].complete()
     keep.wait()
     line.finish()
-    grads.finish()
+    grads.finish(n_tp - 2)
     for weight in weights:
         weight.finish()
 
@@ -664,12 +678,80 @@
         lax.fori_loop(0, at.n_tp * self.tiles, some, 0)
 
 
+class Spread:
+    def __init__(self, at, sums, near, relay, boxes, sems, local_sems):
+        self.at, self.sums, self.near, self.relay, self.boxes = at, sums, near, relay, boxes
+        self.sems, self.local_sems = sems, local_sems
+        self.half = at.n_fsdp // 2
+        self.by_relay = at.n_fsdp == 8
+        self.direct = [1, 2] if self.by_relay else list(range(1, self.half))
+        self.rows = sums.shape[1] // 2
+
+    def part(self, i, part):
+        return self.sums.at[i, pl.ds(part * self.rows, self.rows)]
+
+    def relay_copy(self, part):
+        return send(
+            self.part(3, part), self.relay.at[part],
+            self.sems.at[0, 3 + part], self.sems.at[1, 3 + part], self.at.near(1 + part),
+        )
+
+    def near_copy(self, i):
+        return send(
+            self.sums.at[i], self.near.at[i], self.sems.at[0, i], self.sems.at[1, i], self.at.near(i)
+        )
+
+    def start(self):
+        if self.by_relay:
+            for part in range(2):
+                self.relay_copy(part).start()
+        else:
+            for i in self.direct:
+                self.near_copy(i).start()
+
+    def relayed(self):
+        for part in range(2):
+            self.relay_copy(part).wait_send()
+            self.relay_copy(part).wait_recv()
+
+    def add(self, here=False):
+        if not self.by_relay:
+            return
+        for part, i in ((0, 2), (1, 1)):
+            if not here:
+                self.relay_copy(part).wait_recv()
+            takes = [
+                pltpu.make_async_copy(self.part(i, part), self.boxes.at[0], self.local_sems.at[0]),
+                pltpu.make_async_copy(self.relay.at[part], self.boxes.at[1], self.local_sems.at[1]),
+            ]
+            for take in takes:
+                take.start()
+            for take in takes:
+                take.wait()
+            self.boxes[0] = (self.boxes[0].astype(F32) + self.boxes[1].astype(F32)).astype(BF16)
+            keep = pltpu.make_async_copy(self.boxes.at[0], self.part(i, part), self.local_sems.at[0])
+            keep.start()
+            keep.wait()
+            self.near_copy(i).start()
+
+    def arrived(self):
+        for i in self.direct:
+            self.near_copy(i).wait_recv()
+
+    def finish(self, relays=True):
+        if self.by_relay and relays:
+            for part in range(2):
+                self.relay_copy(part).wait_send()
+        for i in self.direct:
+            self.near_copy(i).wait_send()
+
+
 def middle_kernel(
     sizes,
     two, cot_all, wgu_all, wd_all,
-    gn2, hidden, sum_gu, sum_d, sib_gu, sib_d,
-    x, cots, wgu_v, wd_v, ggu, acts, came, going, stage_gu, stage_d, in_gu, in_d,
-    line_send, line_recv, fold_send, fold_recv, sib_send, sib_recv, local_sems,
+    gn2, branch, sum_gu, sum_d, sib_gu, sib_d, relay_gu, relay_d,
+    hidden, x, cots, wgu_v, wd_v, ggu, acts, came, going, stage_gu, stage_d, in_gu, in_d,
+    line_send, line_recv, fold_send, fold_recv, sib_send, sib_recv, cot_sems, relay_sems, local_sems,
 ):
     n_fsdp, n_tp = sizes
     half = n_fsdp // 2
@@ -684,12 +766,24 @@
         pltpu.make_async_copy(two, x.at[at.t], local_sems.at[0]),
         pltpu.make_async_copy(wgu_all, wgu_v, local_sems.at[1]),
         pltpu.make_async_copy(wd_all, wd_v, local_sems.at[2]),
-        pltpu.make_async_copy(cot_all, cots, local_sems.at[3]),
     ]
     for load in loads:
         load.start()
+
+    def cot_copy(j):
+        return pltpu.make_async_copy(cot_all.at[j], cots.at[j], cot_sems.at[0, j])
+
+    def cot_last(slot, way):
+        return send(
+            cot_all.at[slot], cots.at[slot], cot_sems.at[1, slot], cot_sems.at[2, slot], at.along(at.t + 1 - 2 * way)
+        )
+
+    for j in range(n_tp):
+        pl.when((at.t - j < n_tp - 1) & (j - at.t < n_tp - 1))(cot_copy(j).start)
     for load in loads:
         load.wait()
+    for j in range(n_tp):
+        pl.when((at.t - j < n_tp - 1) & (j - at.t < n_tp - 1))(cot_copy(j).wait)
     fold = Fold(at, gn2, going, came, min(512, model), fold_send, fold_recv)
 
     def unit(slot):
@@ -723,6 +817,23 @@
 
         lax.fori_loop(0, fold.tiles, tiles, 0)
 
+        def branch_copy(c):
+            return pltpu.make_async_copy(
+                stage_gu.at[c // 2 % 2, c % 2, pl.ds(0, slab), pl.ds(0, fold.tile)],
+                branch.at[slot, :, fold.lanes(c)],
+                local_sems.at[4 + c % 4],
+            )
+
+        for c in range(fold.tiles):
+            if c >= 4:
+                branch_copy(c - 4).wait()
+            stage_gu[c // 2 % 2, c % 2, 0:slab, 0 : fold.tile] = dot(
+                hidden[here, :], wd_v[:, c * fold.tile : (c + 1) * fold.tile], NN
+            ).astype(BF16)
+            branch_copy(c).start()
+        for c in range(max(0, fold.tiles - 4), fold.tiles):
+            branch_copy(c).wait()
+
     def each_from(first, last, work):
         def some(i, carry):
             s = (i + 1) // 2
@@ -735,6 +846,12 @@
     for s in range(n_tp):
         if s:
             line.step(s)
+        if s == 1:
+            pl.when(at.t == n_tp - 2)(lambda: cot_last(0, 0).start())
+            pl.when(at.t == 1)(lambda: cot_last(n_tp - 1, 1).start())
+        if s == n_tp - 1:
+            pl.when(at.t == n_tp - 1)(lambda: cot_last(0, 0).wait_recv())
+            pl.when(at.t == 0)(lambda: cot_last(n_tp - 1, 1).wait_recv())
         each_from(s, s + 1, unit)
 
     for key in range(1, n_tp - 2):
@@ -749,79 +866,103 @@
         grads = cots[:, :, columns].reshape(n_tp * slab, part_rows)
         take(2, dot(hidden[...], grads, TN))
 
-    def sib_copies(i):
+    spreads = [
+        Spread(at, sum_gu, None, relay_gu, None, relay_sems.at[0], None),
+        Spread(at, sum_d, None, relay_d, None, relay_sems.at[1], None),
+    ]
+    by_relay = spreads[0].by_relay
+
+    def order(n):
+        return lax.rem(n + half - 1, half) if by_relay else n
+
+    def sib_copies(n):
+        i, slot = order(n), lax.rem(n, 2)
         return [
-            send(stage_gu.at[lax.rem(i, 2)], sib_gu.at[i], sib_send.at[0, i], sib_recv.at[0, i], at.sibling()),
-            send(stage_d.at[lax.rem(i, 2)], sib_d.at[i], sib_send.at[1, i], sib_recv.at[1, i], at.sibling()),
+            send(stage_gu.at[slot], sib_gu.at[i], sib_send.at[0, i], sib_recv.at[0, i], at.sibling()),
+            send(stage_d.at[slot], sib_d.at[i], sib_send.at[1, i], sib_recv.at[1, i], at.sibling()),
         ]
 
-    def keep_copies(i):
+    def keep_copies(n):
+        i, slot = order(n), lax.rem(n, 2)
         return [
-            pltpu.make_async_copy(stage_gu.at[lax.rem(i, 2)], sum_gu.at[i], local_sems.at[4 + lax.rem(i, 2)]),
-            pltpu.make_async_copy(stage_d.at[lax.rem(i, 2)], sum_d.at[i], local_sems.at[6 + lax.rem(i, 2)]),
+            pltpu.make_async_copy(stage_gu.at[slot], sum_gu.at[i], local_sems.at[4 + slot]),
+            pltpu.make_async_copy(stage_d.at[slot], sum_d.at[i], local_sems.at[6 + slot]),
         ]
 
-    def others(i, carry):
-        pl.when(i < fold.tiles)(lambda: fold.forward(n_tp - 2, i))
-
-        @pl.when(i >= 2)
+    def others(n, carry):
+        pl.when(n < fold.tiles)(lambda: fold.forward(n_tp - 2, n))
+
+        @pl.when(n >= 2)
         def _():
-            for copy in sib_copies(i - 2):
+            for copy in sib_copies(n - 2):
                 copy.wait_send()
 
         def take(part, values):
             if part < 2:
-                stage_gu[lax.rem(i, 2), part] = values.astype(BF16)
+                stage_gu[lax.rem(n, 2), part] = values.astype(BF16)
             else:
-                stage_d[lax.rem(i, 2)] = values.astype(BF16)
-
-        block(xor_any(at.chip, i, bits) * 2 + 1 - at.core, take)
-        for copy in sib_copies(i):
+                stage_d[lax.rem(n, 2)] = values.astype(BF16)
+
+        block(xor_any(at.chip, order(n), bits) * 2 + 1 - at.core, take)
+        for copy in sib_copies(n):
             copy.start()
         return carry
 
     lax.fori_loop(0, half, others, 0)
-    for i in range(half - 2, half):
-        for copy in sib_copies(jnp.int32(i)):
+    for n in range(half - 2, half):
+        for copy in sib_copies(jnp.int32(n)):
             copy.wait_send()
 
-    def mine(i, carry):
-        pl.when(i < fold.tiles)(lambda: fold.forward(n_tp - 1, i))
-        for copy in sib_copies(i):
+    def mine(n, carry):
+        for copy in sib_copies(n):
             copy.wait_recv()
         takes = [
-            pltpu.make_async_copy(sib_gu.at[i], in_gu, local_sems.at[8]),
-            pltpu.make_async_copy(sib_d.at[i], in_d, local_sems.at[9]),
+            pltpu.make_async_copy(sib_gu.at[order(n)], in_gu, local_sems.at[8]),
+            pltpu.make_async_copy(sib_d.at[order(n)], in_d, local_sems.at[9]),
         ]
         for take in takes:
             take.start()
 
-        @pl.when(i >= 2)
+        @pl.when(n >= 2)
         def _():
-            for copy in keep_copies(i - 2):
+            for copy in keep_copies(n - 2):
                 copy.wait()
+
+        if by_relay:
+
+            @pl.when(n == 2)
+            def _():
+                for spread in spreads:
+                    spread.start()
 
         def take(part, values):
             if part == 0:
                 for copy in takes:
                     copy.wait()
             if part < 2:
-                stage_gu[lax.rem(i, 2), part] = (values + in_gu[part].astype(F32)).astype(BF16)
+                stage_gu[lax.rem(n, 2), part] = (values + in_gu[part].astype(F32)).astype(BF16)
             else:
-                stage_d[lax.rem(i, 2)] = (values + in_d[...].astype(F32)).astype(BF16)
-
-        block(xor_any(at.chip, i, bits) * 2 + at.core, take)
-        for copy in keep_copies(i):
+                stage_d[lax.rem(n, 2)] = (values + in_d[...].astype(F32)).astype(BF16)
+
+        block(xor_any(at.chip, order(n), bits) * 2 + at.core, take)
+        for copy in keep_copies(n):
             copy.start()
         return carry
 
     lax.fori_loop(0, half, mine, 0)
+    for c in range(fold.tiles):
+        fold.forward(n_tp - 1, c)
     fold.end()
     for i in range(half - 2, half):
         for copy in keep_copies(jnp.int32(i)):
             copy.wait()
     line.finish()
+    pl.when(at.t == n_tp - 2)(lambda: cot_last(0, 0).wait_send())
+    pl.when(at.t == 1)(lambda: cot_last(n_tp - 1, 1).wait_send())
     fold.finish()
+    if by_relay:
+        for spread in spreads:
+            spread.relayed()
 
 
 def middle(sizes, two, cot_all, wgu_all, wd_all):
@@ -836,11 +977,13 @@
     shape = jax.ShapeDtypeStruct
     outs = [
         (shape((slab, model), F32), vmem),
-        (shape((n_tp * slab, hidden), BF16), vmem),
+        (shape((n_tp, slab, model), BF16), hbm),
         (shape((half, 2, part_rows, hidden), BF16), hbm),
         (shape((half, hidden, part_rows), BF16), hbm),
         (shape((half, 2, part_rows, hidden), BF16), hbm),
         (shape((half, hidden, part_rows), BF16), hbm),
+        (shape((2, 1, part_rows, hidden), BF16), hbm),
+        (shape((2, hidden // 2, part_rows), BF16), hbm),
     ]
     dma = pltpu.SemaphoreType.DMA
     return pl.pallas_call(
@@ -849,6 +992,7 @@
         out_specs=[spec for _, spec in outs],
         out_shape=[out for out, _ in outs],
         scratch_shapes=[
+            pltpu.VMEM((n_tp * slab, hidden), BF16),
             pltpu.VMEM((n_tp, slab, model), BF16),
             pltpu.VMEM((n_tp, slab, model), BF16),
             pltpu.VMEM((2, model, hidden), BF16),
@@ -862,75 +1006,13 @@
             pltpu.VMEM((2, part_rows, hidden), BF16),
             pltpu.VMEM((hidden, part_rows), BF16),
             dma((2, n_tp)), dma((n_tp,)), dma((n_tp, model // tile)), dma((n_tp + 1, model // tile)),
-            dma((2, half)), dma((2, half)), dma((10,)),
+            dma((2, half)), dma((2, half)), dma((3, n_tp)), dma((2, 2, half + 1)), dma((10,)),
         ],
         compiler_params=pltpu.CompilerParams(
             collective_id=3, has_side_effects=True, vmem_limit_bytes=62 * 2**20
         ),
         cost_estimate=pl.CostEstimate(flops=10**11, bytes_accessed=10**8, transcendentals=0),
     )(two, cot_all, wgu_all, wd_all)
-
-
-class Spread:
-    def __init__(self, at, sums, near, relay, boxes, sems, local_sems):
-        self.at, self.sums, self.near, self.relay, self.boxes = at, sums, near, relay, boxes
-        self.sems, self.local_sems = sems, local_sems
-        self.half = at.n_fsdp // 2
-        self.by_relay = at.n_fsdp == 8
-        self.direct = [1, 2] if self.by_relay else list(range(1, self.half))
-        self.rows = sums.shape[1] // 2
-
-    def part(self, i, part):
-        return self.sums.at[i, pl.ds(part * self.rows, self.rows)]
-
-    def relay_copy(self, part):
-        return send(
-            self.part(3, part), self.relay.at[part],
-            self.sems.at[0, 3 + part], self.sems.at[1, 3 + part], self.at.near(1 + part),
-        )
-
-    def near_copy(self, i):
-        return send(
-            self.sums.at[i], self.near.at[i], self.sems.at[0, i], self.sems.at[1, i], self.at.near(i)
-        )
-
-    def start(self):
-        if self.by_relay:
-            for part in range(2):
-                self.relay_copy(part).start()
-        else:
-            for i in self.direct:
-                self.near_copy(i).start()
-
-    def add(self):
-        if not self.by_relay:
-            return
-        for part, i in ((0, 2), (1, 1)):
-            self.relay_copy(part).wait_recv()
-            takes = [
-                pltpu.make_async_copy(self.part(i, part), self.boxes.at[0], self.local_sems.at[0]),
-                pltpu.make_async_copy(self.relay.at[part], self.boxes.at[1], self.local_sems.at[1]),
-            ]
-            for take in takes:
-                take.start()
-            for take in takes:
-                take.wait()
-            self.boxes[0] = (self.boxes[0].astype(F32) + self.boxes[1].astype(F32)).astype(BF16)
-            keep = pltpu.make_async_copy(self.boxes.at[0], self.part(i, part), self.local_sems.at[0])
-            keep.start()
-            keep.wait()
-            self.near_copy(i).start()
-
-    def arrived(self):
-        for i in self.direct:
-            self.near_copy(i).wait_recv()
-
-    def finish(self):
-        if self.by_relay:
-            for part in range(2):
-                self.relay_copy(part).wait_send()
-        for i in self.direct:
-            self.near_copy(i).wait_send()
 
 
 class Pair:
@@ -1043,9 +1125,9 @@
 def back_kernel(
     sizes, widest,
     gn2, resid, tok, cot, att_own, wo_all, wq_all, q_in, k_in, v_in, one, sum_gu_in, sum_d_in,
-    rows_in, cos, s_low, s_high, starts,
+    relay_gu, relay_d, rows_in, cos, s_low, s_high, starts,
     grad_tok, small_out, near_gu, near_d, own_gu, own_d, sum_q, near_q, sib_q, relay_q,
-    sum_o, near_o, sib_o, relay_o, zo, relay_gu, relay_d,
+    sum_o, near_o, sib_o, relay_o, zo,
     gres, res_v, tok_v, cot_v, att_v, gattn, wo_v, wq_v, q_v, k_v, v_v, gp, gatt, ghead, came, going,
     kt, dk, dv, stage_o, inbox_o, stage_q, inbox_q, box_gu, box_d, box_o, box_q, zo_stage, zo_box,
     norm_sums, bias, tiles, land_z, land_near, land_sib,
@@ -1076,8 +1158,9 @@
     spread_d = Spread(at, own_d, near_d, relay_d, box_d, d_sems, local_sems.at[pl.ds(13, 2)])
     spread_o = Spread(at, sum_o, near_o, relay_o, box_o, o_sems, local_sems.at[pl.ds(13, 2)])
     spread_q = Spread(at, sum_q, near_q, relay_q, box_q, q_sems, local_sems.at[pl.ds(13, 2)])
-    spread_gu.start()
-    spread_d.start()
+    if not spread_gu.by_relay:
+        spread_gu.start()
+        spread_d.start()
     norm_sums[...] = jnp.zeros_like(norm_sums)
     bias[...] = jnp.zeros_like(bias)
     for load in loads[:4]:
@@ -1122,6 +1205,9 @@
 
     lax.fori_loop(0, pairs, give_heads, 0)
 
+    spread_gu.add(here=True)
+    spread_d.add(here=True)
+
     loads[5].wait()
     pair_o = Pair(at, stage_o, sib_o, sum_o, inbox_o, pair_o_sems, pair_o_local)
     pair_q = Pair(at, stage_q, sib_q, sum_q, inbox_q, pair_q_sems, pair_q_local)
@@ -1151,9 +1237,18 @@
         attend_back(
             widest, q_v, k_v, v_v, gatt, cos, s_low, s_high, starts, gp, bias, kt, dk, dv, i * LANES
         )
+
+        def keep_o(n, carry):
+            pair_o.keep(n, lambda: dot(att_v[...], gattn[:, piece(owner(n, at.core))], TN))
+            return carry
+
+        lax.fori_loop(i * half // pairs, (i + 1) * half // pairs, keep_o, 0)
         return carry
 
+    pair_o.given(half)
     lax.fori_loop(0, pairs, some_heads, 0)
+    pair_o.kept(half)
+    spread_o.start()
 
     loads[9].wait()
     fold = Fold(at, grad_tok, going, came, min(512, model), fold_send, fold_recv)
@@ -1175,25 +1270,10 @@
 
     lax.fori_loop(0, 2 * n_tp - 1, far_first, 0)
 
-    spread_gu.add()
-    spread_d.add()
-    pair_o.given(half)
-
-    def forward(key, i):
-        pl.when(i < fold.tiles)(lambda: fold.forward(key, i))
-
-    def keep_o(i, carry):
-        forward(n_tp - 1, i)
-        pair_o.keep(i, lambda: dot(att_v[...], gattn[:, piece(owner(i, at.core))], TN))
-        return carry
-
-    lax.fori_loop(0, half, keep_o, 0)
-    pair_o.kept(half)
-    spread_o.start()
+    spread_o.add()
     load_one.wait()
 
     def give_q(i, carry):
-        forward(n_tp - 2, i)
         pair_q.give(i, lambda: dot(wo_v[0:seq_len, piece(owner(i, 1 - at.core))], gp[...], TN))
         return carry
 
@@ -1207,11 +1287,12 @@
     lax.fori_loop(0, half, keep_q, 0)
     pair_q.kept(half)
     spread_q.start()
-    spread_o.add()
-    for key in range(n_tp - 3, 0, -1):
+    for c in range(fold.tiles):
+        fold.forward(n_tp - 1, c)
+    spread_q.add()
+    for key in range(n_tp - 2, 0, -1):
         for c in range(fold.tiles):
             fold.forward(key, c)
-    spread_q.add()
 
     each = model // n_tp
     spread_o.arrived()
@@ -1236,7 +1317,6 @@
             take.wait()
             total = total + zo_box[n].astype(F32)
         zo_stage[other] = total.astype(BF16)
-        pl.when(k > 0)(lambda: zo_copy(k).start())
         return carry
 
     lax.fori_loop(0, n_tp, group, 0)
@@ -1244,6 +1324,8 @@
     own_zo.start()
 
     fold.end()
+    for k in range(1, n_tp):
+        zo_copy(k).start()
     loads[4].wait()
 
     def first(i, carry):
@@ -1323,11 +1405,13 @@
     fold.finish()
     for spread in (spread_gu, spread_d, spread_q):
         spread.arrived()
-    for spread in (spread_gu, spread_d, spread_q, spread_o):
+    for spread in (spread_gu, spread_d):
+        spread.finish(relays=False)
+    for spread in (spread_q, spread_o):
         spread.finish()
 
 
-def back(sizes, widest, gn2, resid, tok, cot, att_own, wo_all, wq_all, q_in, k_in, v_in, one, sum_gu, sum_d, rows_in, tables, starts):
+def back(sizes, widest, gn2, resid, tok, cot, att_own, wo_all, wq_all, q_in, k_in, v_in, one, sum_gu, sum_d, relay_gu, relay_d, rows_in, tables, starts):
     n_fsdp, n_tp = sizes
     half = n_fsdp // 2
     slab, model = tok.shape
@@ -1359,13 +1443,11 @@
         (shape((half,) + piece_o, BF16), hbm),
         (shape((2,) + halved(piece_o), BF16), hbm),
         (shape((n_tp, each, part_rows), BF16), hbm),
-        (shape((2,) + halved(piece_gu), BF16), hbm),
-        (shape((2,) + halved(piece_d), BF16), hbm),
     ]
     dma = pltpu.SemaphoreType.DMA
     return pl.pallas_call(
         functools.partial(back_kernel, sizes, widest),
-        in_specs=[hbm] * 13 + [vmem] * 5,
+        in_specs=[hbm] * 15 + [vmem] * 5,
         out_specs=[spec for _, spec in outs],
         out_shape=[out for out, _ in outs],
         scratch_shapes=[
@@ -1417,7 +1499,7 @@
         cost_estimate=pl.CostEstimate(flops=10**11, bytes_accessed=10**8, transcendentals=0),
     )(
         gn2, resid, tok, cot, att_own, wo_all, wq_all, q_in, k_in, v_in, one, sum_gu, sum_d,
-        rows_in, *tables, starts,
+        relay_gu, relay_d, rows_in, *tables, starts,
     )
 
 
@@ -1464,17 +1546,18 @@
     )
     full_one = full_one.reshape(seq_len, model_width)
 
-    grad_normed_two, hidden_low, sum_gu, sum_down, _, _ = middle(
+    grad_normed_two, branch_terms, sum_gu, sum_down, _, _, relay_gu, relay_down = middle(
         sizes, normed_two, grad_branch, gu_all, down_all
     )
     (
         grad_tokens, shares, near_gu, near_down, own_gu, own_down, sum_qkv, near_qkv, _, _, _, _, _, _,
-        out_parts, _, _,
+        out_parts,
     ) = back(
         sizes, widest, grad_normed_two, residual, tokens, cotangent, attended_own, out_all, qkv_all,
-        queries, key_vals, value_rows, full_one, sum_gu, sum_down, norm_rows_all, tables, starts_row,
+        queries, key_vals, value_rows, full_one, sum_gu, sum_down, relay_gu, relay_down,
+        norm_rows_all, tables, starts_row,
     )
-    branch = reduce_rows(dot(hidden_low, down_all, NN))
+    branch = reduce_rows(branch_terms.reshape(seq_len, model_width))
     result = (residual + branch).astype(BF16)
     direct = [1, 2] if n_fsdp == 8 else list(range(1, n_fsdp // 2))
 

time: 651 us -> 608 us (0.934)
  Pallas kernels: 587 us -> 555 us
  matrix products: 11 us -> 0 us
    pallas_call x1, Pallas kernels: 206 us -> 179 us  [front(): pl.pallas_call(functools.partial(front_kernel, sizes, widest), in_specs=[...]
    pallas_call x1, Pallas kernels: 218 us -> 203 us  [back(): pl.pallas_call(functools.partial(back_kernel, sizes, widest), in_specs=[h...]
    dot_general x1 -> x0, matrix products: 11 us -> none  [dot(): return lax.dot_general(left, right, dims, preferred_element_type=F32)]
    pallas_call x1, Pallas kernels: 164 us -> 173 us  [middle(): pl.pallas_call(functools.partial(middle_kernel, sizes), in_specs=[hbm] *...]
  transfers between devices with their start and end apart: 1 -> 1, of which waited for: 0 -> 0; matrix products, arithmetic and copies ran while one was open for 2% -> 3% of each run, Pallas kernels for 34% -> 34%
where the time goes in v4:
time: 608 us; the launch traced here: 600 us
  Pallas kernels  555 us (91%)
  other arithmetic  17 us (3%)
  between operations  14.6 us (2%)
  local copies, waits for them, and re-layouts  13.5 us (2%)
    pallas_call x1, Pallas kernels, back(): pl.pallas_call(functools.partial(back_kernel, sizes, widest), in_specs=[h...  203 us
    pallas_call x1, Pallas kernels, front(): pl.pallas_call(functools.partial(front_kernel, sizes, widest), in_specs=[...  179 us
    pallas_call x1, Pallas kernels, middle(): pl.pallas_call(functools.partial(middle_kernel, sizes), in_specs=[hbm] *...  173 us
  transfers between devices with their start and end apart: 1, of which 0 were waited for; matrix products, arithmetic and copies ran while one was open for 3% of the time, Pallas kernels for 34%

profile of v4, /device:TPU:0, one launch (start us, length us, event | category | flops | bytes accessed | tf_op | source)
XLA Modules:
  0.0 600.1 jit_solution(8565692889269504608)
XLA Ops:
  7.2 0.0 copy-start.2
  7.2 0.0 reduce-scatter.2.cloned.1.call-start
  7.3 0.8 convert_element_type.68
  8.1 0.1 pad.8.clone
  8.1 0.8 maximum_maximum_fusion
  8.9 0.6 pad.4.tile
  9.5 0.8 reduce-window.8
  10.3 0.7 select_reduce_fusion
  11.1 0.0 copy-start.5
  11.1 1.4 copy.31
  12.5 1.2 copy.33.wq
  13.6 0.0 copy-done.2
  13.6 1.2 copy.38
  14.9 0.0 copy-done.5
  14.9 3.2 fusion
  18.1 178.7 %shard_map.169 = (bf16[4,256,2048]{2,1,0:T(8,128)(2,1)}, bf16[1024,512]{1,0:T(8,128)(2,1)}, bf16[1024,512]{1,0:T(8,128)(2,1)}, bf16[1024,512]{1,0:T(8,128)(2,1)}...) custom-call(bf16[256,2048]{1,0:T(8,128)(2,1)} %tok.3, ...), custom_call_target="tpu_custom_call" | custom-call | flops 99999997952 | bytes 100000000 | tf_op jit(solution)/shard_map/pallas_call | solution.py:561
  196.7 173.0 %shard_map.170 = (f32[256,2048]{1,0:T(8,128)}, bf16[4,256,2048]{2,1,0:T(8,128)(2,1)}, bf16[4,2,256,1408]{3,2,1,0:T(8,128)(2,1)}, bf16[4,1408,256]{2,1,0:T(8,128)...) custom-call(bf16[256,2048]{1,0:T(8,128)(2,1)} %get-tuple-element.38., ...), custom_call_target="tpu_custom_call" | custom-call | flops 99999997952 | bytes 100000000 | tf_op jit(solution)/shard_map/pallas_call | solution.py:989
  369.7 0.0 reduce-scatter.2.cloned.1.call-update
  369.8 203.3 %shard_map.171 = (f32[256,2048]{1,0:T(8,128)}, f32[8,128]{1,0:T(8,128)}, bf16[4,2,256,1408]{3,2,1,0:T(8,128)(2,1)}, bf16[4,1408,256]{2,1,0:T(8,128)(2,1)}, bf16[...) custom-call(f32[256,2048]{1,0:T(8,128)} %get-tuple-element.43.gn2, ...), custom_call_target="tpu_custom_call", output_to_operand_aliasing={{4}: (11, {}), {5}: (12, {})} | custom-call | flops 99999997952 | bytes 100000000 | tf_op jit(solution)/shard_map/pallas_call | solution.py:1448
  573.0 1.3 slice.45
  574.3 1.9 convert_add_fusion
  576.2 0.5 copy.34
  576.7 1.6 copy.35
  578.3 2.7 add_bitcast_fusion
  581.0 0.0 copy-start.3
  581.0 0.0 copy-start.6
  581.0 0.0 copy-start.4
  581.0 3.8 copy.36
  584.8 0.0 copy-start
  584.8 0.0 copy-done.3
  584.8 0.9 convert_reduce_fusion
  585.8 0.0 copy-done.6
  585.8 0.6 fusion.8
  586.3 0.0 copy-done.4
  586.3 2.5 add_bitcast_fusion.1
  588.9 0.0 reduce-scatter.2.cloned.1.call-done
  588.9 0.0 copy-done
  588.9 0.0 copy-start.1
  588.9 2.6 add_convert_fusion
  591.5 0.0 copy-done.1
  591.5 1.3 copy.42
  (4 shorter events, 0.0 us)
Async XLA Ops:
  7.2 6.5 %copy-start.2 = (bf16[256,2,1408]{2,1,0:T(2,128)(2,1)S(1)}, bf16[256,2,1408]{2,1,0:T(2,128)(2,1)}, u32[]{:S(2)}) copy-start(bf16[256,2,1408]{2,1,0:T(2,128)(2,1)} %param.17) | copy-start | bytes 4325380
  7.2 581.7 %reduce-scatter.2.cloned.1.call-start = ((), (), s32[]{:S(2)}) async-start(), calls=%async_computation.1 | async-start | bytes 5242880 | tf_op jit(solution)/shard_map/reduce_scatter | solution.py:1507
  11.1 3.8 copy-start.5
  581.0 3.8 copy-start.3
  581.0 4.8 copy-start.6
  581.0 5.3 copy-start.4
  584.8 4.1 copy-start
  588.9 2.6 copy-start.1
Sparse Core Ops, SparseCore 0:
  369.9 111.9 reduce-scatter.1

commit v5 on v4

--- a/solution.py
+++ b/solution.py
@@ -271,8 +271,9 @@
 
 def front_kernel(
     sizes, widest,
-    tok, cot, wq, wo, wgu, wd, tile, cos, s_low, s_high, starts,
+    tok, cot, wq, wo, wgu, wd, tile, turns, starts,
     one, q_out, k_out, v_out, resid, two, rows_out, att_out, cot_all, wq_all, wo_all, wgu_all, wd_all,
+    cos, s_low, s_high,
     toks, wq_v, wo_v, att, heads, vt, small, bias,
     tok_send, tok_recv, cot_send, cot_recv, near_sems, sib_sems, wz_sems, small_sems,
     swap_send, swap_recv, local_sems,
@@ -318,6 +319,14 @@
     ]
     for copy in own_copies:
         copy.start()
+
+    eight = ROT // 2
+    cosine, sine = turns[0:eight, :], turns[eight : 2 * eight, :]
+    none = jnp.zeros_like(sine)
+    flat = jnp.zeros((HEAD - ROT, turns.shape[1]), F32)
+    cos[...] = jnp.concatenate([cosine, cosine, flat + 1.0] * 2, axis=0).T
+    s_low[...] = jnp.concatenate([-sine, none, flat] * 2, axis=0).T
+    s_high[...] = jnp.concatenate([none, sine, flat] * 2, axis=0).T
 
     small[at.t, at.f] = tile[...]
     mine = small.at[at.t, at.f]
@@ -531,7 +540,7 @@
             ]
 
 
-def front(sizes, widest, tok, cot, wq, wo, wgu, wd, tile, tables, starts):
+def front(sizes, widest, tok, cot, wq, wo, wgu, wd, tile, turns, starts):
     n_fsdp, n_tp = sizes
     half = n_fsdp // 2
     slab, model = tok.shape
@@ -555,12 +564,12 @@
         (shape((model, model), BF16), hbm),
         (shape((2, model, hidden), BF16), hbm),
         (shape((hidden, model), BF16), hbm),
-    ]
+    ] + [(shape((seq_len, LANES), F32), vmem)] * 3
     dma = pltpu.SemaphoreType.DMA
     pairs = width // LANES
     return pl.pallas_call(
         functools.partial(front_kernel, sizes, widest),
-        in_specs=[vmem] * 11,
+        in_specs=[vmem] * 9,
         out_specs=[spec for _, spec in outs],
         out_shape=[out for out, _ in outs],
         scratch_shapes=[
@@ -580,7 +589,7 @@
             collective_id=1, has_side_effects=True, vmem_limit_bytes=60 * 2**20
         ),
         cost_estimate=pl.CostEstimate(flops=10**11, bytes_accessed=10**8, transcendentals=0),
-    )(tok, cot, wq, wo, wgu, wd, tile, *tables, starts)
+    )(tok, cot, wq, wo, wgu, wd, tile, turns, starts)
 
 
 def xor_any(value, mask, bits):
@@ -1270,27 +1279,28 @@
 
     lax.fori_loop(0, 2 * n_tp - 1, far_first, 0)
 
-    spread_o.add()
     load_one.wait()
 
     def give_q(i, carry):
         pair_q.give(i, lambda: dot(wo_v[0:seq_len, piece(owner(i, 1 - at.core))], gp[...], TN))
         return carry
 
-    lax.fori_loop(0, half, give_q, 0)
-    pair_q.given(half)
-
     def keep_q(i, carry):
         pair_q.keep(i, lambda: dot(wo_v[0:seq_len, piece(owner(i, at.core))], gp[...], TN))
         return carry
 
-    lax.fori_loop(0, half, keep_q, 0)
+    for c in range(fold.tiles):
+        fold.forward(n_tp - 1, c)
+        lax.fori_loop(half * c // fold.tiles, half * (c + 1) // fold.tiles, give_q, 0)
+        if c == 1:
+            spread_o.add()
+    pair_q.given(half)
+    for c in range(fold.tiles):
+        fold.forward(n_tp - 2, c)
+        lax.fori_loop(half * c // fold.tiles, half * (c + 1) // fold.tiles, keep_q, 0)
     pair_q.kept(half)
     spread_q.start()
-    for c in range(fold.tiles):
-        fold.forward(n_tp - 1, c)
-    spread_q.add()
-    for key in range(n_tp - 2, 0, -1):
+    for key in range(n_tp - 3, 0, -1):
         for c in range(fold.tiles):
             fold.forward(key, c)
 
@@ -1323,9 +1333,11 @@
     own_zo = pltpu.make_async_copy(zo_stage.at[at.t], zo.at[at.t], local_sems.at[15])
     own_zo.start()
 
-    fold.end()
     for k in range(1, n_tp):
         zo_copy(k).start()
+    spread_q.add()
+
+    fold.end()
     loads[4].wait()
 
     def first(i, carry):
@@ -1524,14 +1536,9 @@
     passed = (doc_ends[None, :] <= ids[:, None]).astype(jnp.int32)
     starts = jnp.sum(passed * length_row[None, :], axis=1)
     places = (ids - starts).astype(F32)
-    lane = jnp.arange(LANES, dtype=jnp.int32) % HEAD
-    frequency = 10000.0 ** (-2.0 * (lane % (ROT // 2)).astype(F32) / ROT)
-    angles = places[:, None] * frequency[None, :]
-    cosine = jnp.where(lane[None] < ROT, jnp.cos(angles), 1.0)
-    sine = jnp.sin(angles)
-    sine_low = jnp.where(lane[None] < ROT // 2, -sine, 0.0)
-    sine_high = jnp.where((lane[None] >= ROT // 2) & (lane[None] < ROT), sine, 0.0)
-    tables = (cosine, sine_low, sine_high)
+    frequency = 10000.0 ** (-2.0 * jnp.arange(ROT // 2, dtype=F32) / ROT)
+    angles = frequency[:, None] * places[None, :]
+    turns = jnp.concatenate([jnp.cos(angles), jnp.sin(angles)], axis=0)
     starts_row = starts.reshape(1, seq_len).astype(jnp.int32)
     widest = seq_len // 2
 
@@ -1539,10 +1546,10 @@
     tile = jnp.pad(tile, ((0, 0), (0, LANES - small)))
     (
         full_one, queries, key_vals, value_rows, residual, normed_two, norm_rows_all, attended_own,
-        grad_branch, qkv_all, out_all, gu_all, down_all,
+        grad_branch, qkv_all, out_all, gu_all, down_all, *tables,
     ) = front(
         sizes, widest, tokens, cotangent, w_qkv.reshape(part_rows, 3 * local_width), w_out,
-        w_gate_up.transpose(1, 0, 2), w_down, tile, tables, starts_row,
+        w_gate_up.transpose(1, 0, 2), w_down, tile, turns, starts_row,
     )
     full_one = full_one.reshape(seq_len, model_width)
 
@@ -1573,7 +1580,7 @@
         total(sum_qkv, near_qkv).reshape(part_rows, 3, local_width),
         shares[4:7],
         jnp.sum(out_parts.astype(F32), axis=0),
-        total(own_gu, near_gu).transpose(1, 0, 2),
+        jnp.stack([total(own_gu[:, part], near_gu[:, part]) for part in range(2)], axis=1),
         total(own_down, near_down),
     )
 

time: 608 us -> 599 us (0.985)
    pallas_call x1, Pallas kernels: 203 us -> 197 us  [back(): pl.pallas_call(functools.partial(back_kernel, sizes, widest), in_specs=[h...]
  transfers between devices with their start and end apart: 1 -> 1, of which waited for: 0 -> 0; matrix products, arithmetic and copies ran while one was open for 3% -> 3% of each run, Pallas kernels for 34% -> 33%
where the time goes in v5:
time: 599 us; the launch traced here: 592 us
  Pallas kernels  549 us (92%)
  other arithmetic  14.8 us (2%)
  between operations  14.6 us (2%)
  local copies, waits for them, and re-layouts  13.5 us (2%)
    pallas_call x1, Pallas kernels, back(): pl.pallas_call(functools.partial(back_kernel, sizes, widest), in_specs=[h...  197 us
    pallas_call x1, Pallas kernels, front(): pl.pallas_call(functools.partial(front_kernel, sizes, widest), in_specs=[...  179 us
    pallas_call x1, Pallas kernels, middle(): pl.pallas_call(functools.partial(middle_kernel, sizes), in_specs=[hbm] *...  173 us
  transfers between devices with their start and end apart: 1, of which 0 were waited for; matrix products, arithmetic and copies ran while one was open for 3% of the time, Pallas kernels for 33%

profile of v5, /device:TPU:0, one launch (start us, length us, event | category | flops | bytes accessed | tf_op | source)
XLA Modules:
  0.0 591.7 jit_solution(18154099827833849042)
XLA Ops:
  7.2 0.0 copy-start.2
  7.2 0.0 reduce-scatter.2.cloned.1.call-start
  7.2 0.8 convert_element_type.115
  8.0 0.1 pad.12.clone
  8.1 0.8 maximum_maximum_fusion
  8.9 0.6 pad.4.tile
  9.5 0.8 reduce-window.8
  10.3 0.7 select_reduce_fusion
  11.0 0.0 copy-start.5
  11.1 1.4 copy.31
  12.5 1.2 copy.33.wq
  13.6 0.0 copy-done.2
  13.6 1.2 copy.38
  14.9 0.0 copy-done.5
  14.9 0.2 multiply_cosine_fusion
  15.1 0.6 pad_maximum_fusion.1.turns
  15.7 178.6 %shard_map.169 = (bf16[4,256,2048]{2,1,0:T(8,128)(2,1)}, bf16[1024,512]{1,0:T(8,128)(2,1)}, bf16[1024,512]{1,0:T(8,128)(2,1)}, bf16[1024,512]{1,0:T(8,128)(2,1)}...) custom-call(bf16[256,2048]{1,0:T(8,128)(2,1)} %tok.3, ...), custom_call_target="tpu_custom_call" | custom-call | flops 99999997952 | bytes 100000000 | tf_op jit(solution)/shard_map/pallas_call | solution.py:570
  194.3 173.1 %shard_map.170 = (f32[256,2048]{1,0:T(8,128)}, bf16[4,256,2048]{2,1,0:T(8,128)(2,1)}, bf16[4,2,256,1408]{3,2,1,0:T(8,128)(2,1)}, bf16[4,1408,256]{2,1,0:T(8,128)...) custom-call(bf16[256,2048]{1,0:T(8,128)(2,1)} %get-tuple-element.41., ...), custom_call_target="tpu_custom_call" | custom-call | flops 99999997952 | bytes 100000000 | tf_op jit(solution)/shard_map/pallas_call | solution.py:998
  367.4 0.0 reduce-scatter.2.cloned.1.call-update
  367.4 197.0 %shard_map.171 = (f32[256,2048]{1,0:T(8,128)}, f32[8,128]{1,0:T(8,128)}, bf16[4,2,256,1408]{3,2,1,0:T(8,128)(2,1)}, bf16[4,1408,256]{2,1,0:T(8,128)(2,1)}, bf16[...) custom-call(f32[256,2048]{1,0:T(8,128)} %get-tuple-element.46.gn2, ...), custom_call_target="tpu_custom_call", output_to_operand_aliasing={{4}: (11, {}), {5}: (12, {})} | custom-call | flops 99999997952 | bytes 100000000 | tf_op jit(solution)/shard_map/pallas_call | solution.py:1460
  564.4 1.3 slice.70
  565.7 1.9 convert_add_fusion
  567.5 0.5 copy.34
  568.0 1.6 copy.35
  569.6 2.7 add_bitcast_fusion.2
  572.3 0.2 pad_maximum_fusion
  572.5 0.0 copy-start.3
  572.5 0.0 copy-start.6
  572.5 0.0 copy-start.4
  572.5 3.8 copy.36
  576.3 0.0 copy-done.3
  576.3 0.9 convert_reduce_fusion
  577.3 0.0 copy-done.6
  577.3 0.0 copy-start
  577.3 0.6 fusion
  577.8 0.0 copy-done.4
  577.8 2.6 add_bitcast_fusion
  580.4 0.0 reduce-scatter.2.cloned.1.call-done
  580.4 0.0 copy-done
  580.4 0.0 copy-start.1
  580.4 2.6 add_convert_fusion
  583.1 0.0 copy-done.1
  583.1 1.3 copy.42
  (2 shorter events, 0.0 us)
Async XLA Ops:
  7.2 6.4 %copy-start.2 = (bf16[256,2,1408]{2,1,0:T(2,128)(2,1)S(1)}, bf16[256,2,1408]{2,1,0:T(2,128)(2,1)}, u32[]{:S(2)}) copy-start(bf16[256,2,1408]{2,1,0:T(2,128)(2,1)} %param.17) | copy-start | bytes 4325380
  7.2 573.2 %reduce-scatter.2.cloned.1.call-start = ((), (), s32[]{:S(2)}) async-start(), calls=%async_computation.1 | async-start | bytes 5242880 | tf_op jit(solution)/shard_map/reduce_scatter | solution.py:1519
  11.0 3.8 copy-start.5
  572.5 3.8 copy-start.3
  572.5 4.8 copy-start.6
  572.5 5.3 copy-start.4
  577.3 3.2 copy-start
  580.4 2.6 copy-start.1
Sparse Core Ops, SparseCore 0:
  367.5 111.9 reduce-scatter.1

commit v6 on v5

--- a/solution.py
+++ b/solution.py
@@ -1515,6 +1515,50 @@
     )
 
 
+def last_kernel(count, *refs):
+    gu, down, qkv = refs[:count], refs[count : 2 * count], refs[2 * count : 3 * count]
+    gu_out, down_out, qkv_out = refs[3 * count :]
+    width = qkv_out.shape[2]
+    for part in range(2):
+        gu_out[:, part, :] = sum([ref[0, part].astype(F32) for ref in gu[1:]], gu[0][0, part].astype(F32))
+    down_out[...] = sum([ref[0].astype(F32) for ref in down[1:]], down[0][0].astype(F32))
+    for part in range(3):
+        lanes = slice(part * width, (part + 1) * width)
+        qkv_out[:, part, :] = sum(
+            [ref[0, :, lanes].astype(F32) for ref in qkv[1:]], qkv[0][0, :, lanes].astype(F32)
+        )
+
+
+def last_sums(own_gu, near_gu, own_down, near_down, own_qkv, near_qkv, direct):
+    rows, hidden, part_rows = own_gu.shape[2], own_gu.shape[3], own_down.shape[2]
+    width = own_qkv.shape[2] // 3
+    steps = 4
+    gu = lambda k: pl.BlockSpec((1, 2, rows // steps, hidden), lambda i, k=k: (k, 0, i, 0))
+    down = lambda k: pl.BlockSpec((1, hidden // steps, part_rows), lambda i, k=k: (k, i, 0))
+    qkv = lambda k: pl.BlockSpec((1, rows // steps, 3 * width), lambda i, k=k: (k, i, 0))
+    places = [0] + direct
+    return pl.pallas_call(
+        functools.partial(last_kernel, len(places)),
+        grid=(steps,),
+        in_specs=[make(k) for make in (gu, down, qkv) for k in places],
+        out_specs=[
+            pl.BlockSpec((rows // steps, 2, hidden), lambda i: (i, 0, 0)),
+            pl.BlockSpec((hidden // steps, part_rows), lambda i: (i, 0)),
+            pl.BlockSpec((rows // steps, 3, width), lambda i: (i, 0, 0)),
+        ],
+        out_shape=[
+            jax.ShapeDtypeStruct((rows, 2, hidden), F32),
+            jax.ShapeDtypeStruct((hidden, part_rows), F32),
+            jax.ShapeDtypeStruct((rows, 3, width), F32),
+        ],
+        compiler_params=pltpu.CompilerParams(vmem_limit_bytes=62 * 2**20),
+    )(
+        *[own_gu] + [near_gu] * len(direct),
+        *[own_down] + [near_down] * len(direct),
+        *[own_qkv] + [near_qkv] * len(direct),
+    )
+
+
 def reduce_rows(values):
     return lax.psum_scatter(values.astype(BF16), "tp", scatter_dimension=0, tiled=True).astype(F32)
 
@@ -1568,20 +1612,20 @@
     result = (residual + branch).astype(BF16)
     direct = [1, 2] if n_fsdp == 8 else list(range(1, n_fsdp // 2))
 
-    def total(sums, near):
-        return sum([near[i].astype(F32) for i in direct], sums[0].astype(F32))
-
+    gu_share, down_share, qkv_share = last_sums(
+        own_gu, near_gu, own_down, near_down, sum_qkv, near_qkv, direct
+    )
     shares = shares[:, :small]
     return (
         result,
         grad_tokens,
         shares[0:2],
         shares[2:4],
-        total(sum_qkv, near_qkv).reshape(part_rows, 3, local_width),
+        qkv_share,
         shares[4:7],
         jnp.sum(out_parts.astype(F32), axis=0),
-        jnp.stack([total(own_gu[:, part], near_gu[:, part]) for part in range(2)], axis=1),
-        total(own_down, near_down),
+        gu_share,
+        down_share,
     )
 
 

time: 599 us -> 597 us (level)
  other arithmetic: 14.8 us -> 7.53 us
  Pallas kernels: 549 us -> 556 us
    add x3 -> x0, other arithmetic: 7.12 us -> none  [total(): return sum([near[i].astype(F32) for i in direct], sums[0].astype(F32))]
    pallas_call x0 -> x1, Pallas kernels: none -> 6.69 us  [last_sums(): pl.pallas_call(functools.partial(last_kernel, len(places)), grid=(steps,)...]
  transfers between devices with their start and end apart: 1 -> 1, of which waited for: 0 -> 0; matrix products, arithmetic and copies ran while one was open for 3% -> 1% of each run, Pallas kernels for 33% -> 35%
where the time goes in v6:
time: 597 us; the launch traced here: 589 us
  Pallas kernels  556 us (93%)
  between operations  14.6 us (2%)
  local copies, waits for them, and re-layouts  11.1 us (2%)
  other arithmetic  7.53 us (1%)
    pallas_call x1, Pallas kernels, back(): pl.pallas_call(functools.partial(back_kernel, sizes, widest), in_specs=[h...  197 us
    pallas_call x1, Pallas kernels, front(): pl.pallas_call(functools.partial(front_kernel, sizes, widest), in_specs=[...  179 us
    pallas_call x1, Pallas kernels, middle(): pl.pallas_call(functools.partial(middle_kernel, sizes), in_specs=[hbm] *...  173 us
  transfers between devices with their start and end apart: 1, of which 0 were waited for; matrix products, arithmetic and copies ran while one was open for 1% of the time, Pallas kernels for 35%

profile of v6, /device:TPU:0, one launch (start us, length us, event | category | flops | bytes accessed | tf_op | source)
XLA Modules:
  0.0 588.9 jit_solution(8353054210227395611)
XLA Ops:
  7.2 0.0 copy-start.2
  7.2 0.0 reduce-scatter.2.cloned.1.call-start
  7.2 0.8 convert_element_type.22
  8.0 0.1 pad.10.clone
  8.1 0.8 maximum_maximum_fusion
  8.9 0.6 pad.4.tile
  9.5 0.8 reduce-window.8
  10.3 0.7 select_reduce_fusion
  11.0 0.0 copy-start.4
  11.1 1.4 copy.28
  12.5 1.2 copy.30.wq
  13.6 0.0 copy-done.2
  13.6 1.2 copy.33
  14.9 0.0 copy-done.4
  14.9 0.2 multiply_cosine_fusion
  15.1 0.6 pad_maximum_fusion.turns
  15.7 178.6 %shard_map.169 = (bf16[4,256,2048]{2,1,0:T(8,128)(2,1)}, bf16[1024,512]{1,0:T(8,128)(2,1)}, bf16[1024,512]{1,0:T(8,128)(2,1)}, bf16[1024,512]{1,0:T(8,128)(2,1)}...) custom-call(bf16[256,2048]{1,0:T(8,128)(2,1)} %tok.3, ...), custom_call_target="tpu_custom_call" | custom-call | flops 99999997952 | bytes 100000000 | tf_op jit(solution)/shard_map/pallas_call | solution.py:570
  194.3 173.1 %shard_map.170 = (f32[256,2048]{1,0:T(8,128)}, bf16[4,256,2048]{2,1,0:T(8,128)(2,1)}, bf16[4,2,256,1408]{3,2,1,0:T(8,128)(2,1)}, bf16[4,1408,256]{2,1,0:T(8,128)...) custom-call(bf16[256,2048]{1,0:T(8,128)(2,1)} %get-tuple-element.44., ...), custom_call_target="tpu_custom_call" | custom-call | flops 99999997952 | bytes 100000000 | tf_op jit(solution)/shard_map/pallas_call | solution.py:998
  367.4 0.0 reduce-scatter.2.cloned.1.call-update
  367.4 197.3 %shard_map.171 = (f32[256,2048]{1,0:T(8,128)}, f32[8,128]{1,0:T(8,128)}, bf16[4,2,256,1408]{3,2,1,0:T(8,128)(2,1)}, bf16[4,1408,256]{2,1,0:T(8,128)(2,1)}, bf16[...) custom-call(f32[256,2048]{1,0:T(8,128)} %get-tuple-element.49.gn2, ...), custom_call_target="tpu_custom_call", output_to_operand_aliasing={{4}: (11, {}), {5}: (12, {})} | custom-call | flops 99999997952 | bytes 100000000 | tf_op jit(solution)/shard_map/pallas_call | solution.py:1460
  564.7 1.3 slice.15
  566.0 6.7 %shard_map.172 = (f32[256,2,1408]{2,1,0:T(2,128)}, f32[1408,256]{1,0:T(8,128)}, f32[256,3,512]{2,1,0:T(4,128)}) custom-call(bf16[4,2,256,1408]{3,2,1,0:T(8,128)(2,1)} %get-tuple-element.67.refs_0_, bf16[4,2,256,1408]{3,2,1,0:T(8,128)(2,1)} %get-tuple-element.68.refs_1_.refs_2_, bf16[4,2,256,1408]{3,2,1,0:T(8,128)(2,1)} %get-tuple-element.68.refs_1_.refs_2_, ...), custom_call_target="tpu_custom_call" | custom-call | tf_op jit(solution)/shard_map/pallas_call | solution.py:1540
  572.7 0.0 copy-start.3
  572.7 0.0 copy-start.5
  572.7 0.0 copy-start
  572.7 3.4 copy.31
  576.1 0.0 copy-done.3
  576.1 0.9 convert_reduce_fusion
  577.0 0.0 copy-done.5
  577.1 0.6 fusion
  577.6 0.0 reduce-scatter.2.cloned.1.call-done
  577.6 0.0 copy-done
  577.6 0.0 copy-start.1
  577.6 2.6 add_convert_fusion
  580.3 0.0 copy-done.1
  580.3 1.3 copy.37
  (2 shorter events, 0.0 us)
Async XLA Ops:
  7.2 6.4 %copy-start.2 = (bf16[256,2,1408]{2,1,0:T(2,128)(2,1)S(1)}, bf16[256,2,1408]{2,1,0:T(2,128)(2,1)}, u32[]{:S(2)}) copy-start(bf16[256,2,1408]{2,1,0:T(2,128)(2,1)} %param.17) | copy-start | bytes 4325380
  7.2 570.4 %reduce-scatter.2.cloned.1.call-start = ((), (), s32[]{:S(2)}) async-start(), calls=%async_computation.1 | async-start | bytes 5242880 | tf_op jit(solution)/shard_map/reduce_scatter | solution.py:1563
  11.0 3.8 copy-start.4
  572.7 3.4 copy-start.3
  572.7 4.4 copy-start.5
  572.7 4.9 copy-start
  577.6 2.6 copy-start.1
Sparse Core Ops, SparseCore 0:
  367.6 111.6 reduce-scatter.1

commit v7 on v6

--- a/solution.py
+++ b/solution.py
@@ -1189,8 +1189,11 @@
 
     lax.fori_loop(0, slab // step, second, 0)
 
+    per = 2 if pairs % 2 == 0 else 1
+    wide = per * LANES
+
     def swap_copy(i, k):
-        lanes = pl.ds(pl.multiple_of(i * LANES, LANES), LANES)
+        lanes = pl.ds(pl.multiple_of(i * wide, wide), wide)
         other = lax.rem(at.t + k, n_tp)
         return send(
             ghead.at[other, :, lanes],
@@ -1199,11 +1202,11 @@
         )
 
     def give_heads(i, carry):
-        lanes = pl.ds(pl.multiple_of(i * LANES, LANES), LANES)
+        lanes = pl.ds(pl.multiple_of(i * wide, wide), wide)
 
         def to(k, carry):
             other = lax.rem(at.t + k, n_tp)
-            rows = pl.ds(pl.multiple_of(other * width + i * LANES, LANES), LANES)
+            rows = pl.ds(pl.multiple_of(other * width + i * wide, wide), wide)
             ghead[other, :, lanes] = dot(gattn[...], wo_v[rows, :], NT).astype(BF16)
             pl.when(k > 0)(lambda: swap_copy(i, k).start())
             return carry
@@ -1212,8 +1215,7 @@
         gatt[pl.ds(pl.multiple_of(at.t * slab, slab), slab), lanes] = ghead[at.t, :, lanes]
         return carry
 
-    lax.fori_loop(0, pairs, give_heads, 0)
-
+    lax.fori_loop(0, pairs // per, give_heads, 0)
     spread_gu.add(here=True)
     spread_d.add(here=True)
 
@@ -1238,11 +1240,17 @@
     load_one.start()
 
     def some_heads(i, carry):
-        for k in range(1, n_tp):
-            source = lax.rem(at.t + n_tp - k, n_tp)
-            lanes = pl.ds(pl.multiple_of(i * LANES, LANES), LANES)
-            came_rows = gatt.at[pl.ds(pl.multiple_of(source * slab, slab), slab), lanes]
-            send(came_rows, came_rows, swap_send.at[i, k], swap_recv.at[i, k], at.along(source)).wait_recv()
+        def heads_came():
+            block = i // per
+            lanes = pl.ds(pl.multiple_of(block * wide, wide), wide)
+            for k in range(1, n_tp):
+                source = lax.rem(at.t + n_tp - k, n_tp)
+                came_rows = gatt.at[pl.ds(pl.multiple_of(source * slab, slab), slab), lanes]
+                send(
+                    came_rows, came_rows, swap_send.at[block, k], swap_recv.at[block, k], at.along(source)
+                ).wait_recv()
+
+        pl.when(lax.rem(i, per) == 0)(heads_came)
         attend_back(
             widest, q_v, k_v, v_v, gatt, cos, s_low, s_high, starts, gp, bias, kt, dk, dv, i * LANES
         )
@@ -1413,7 +1421,7 @@
             swap_copy(i, k).wait_send()
         return carry
 
-    lax.fori_loop(0, pairs, swapped, 0)
+    lax.fori_loop(0, pairs // per, swapped, 0)
     fold.finish()
     for spread in (spread_gu, spread_d, spread_q):
         spread.arrived()

time: 597 us -> 605 us (1.013)
  Pallas kernels: 556 us -> 564 us
    pallas_call x1, Pallas kernels: 197 us -> 206 us  [back(): pl.pallas_call(functools.partial(back_kernel, sizes, widest), in_specs=[h...]
  transfers between devices with their start and end apart: 1 -> 1, of which waited for: 0 -> 0; matrix products, arithmetic and copies ran while one was open for 1% -> 1% of each run, Pallas kernels for 35% -> 36%
where the time goes in v7:
time: 605 us; the launch traced here: 597 us
  Pallas kernels  564 us (93%)
  between operations  14.6 us (2%)
  local copies, waits for them, and re-layouts  11.1 us (2%)
  other arithmetic  7.53 us (1%)
    pallas_call x1, Pallas kernels, back(): pl.pallas_call(functools.partial(back_kernel, sizes, widest), in_specs=[h...  206 us
    pallas_call x1, Pallas kernels, front(): pl.pallas_call(functools.partial(front_kernel, sizes, widest), in_specs=[...  179 us
    pallas_call x1, Pallas kernels, middle(): pl.pallas_call(functools.partial(middle_kernel, sizes), in_specs=[hbm] *...  173 us
  transfers between devices with their start and end apart: 1, of which 0 were waited for; matrix products, arithmetic and copies ran while one was open for 1% of the time, Pallas kernels for 36%

profile of v7, /device:TPU:0, one launch (start us, length us, event | category | flops | bytes accessed | tf_op | source)
XLA Modules:
  0.0 597.2 jit_solution(12830868134741090732)
XLA Ops:
  7.2 0.0 copy-start.2
  7.2 0.0 reduce-scatter.2.cloned.1.call-start
  7.2 0.8 convert_element_type.22
  8.0 0.1 pad.10.clone
  8.1 0.8 maximum_maximum_fusion
  8.9 0.6 pad.4.tile
  9.5 0.8 reduce-window.8
  10.3 0.7 select_reduce_fusion
  11.0 0.0 copy-start.4
  11.1 1.4 copy.28
  12.5 1.2 copy.30.wq
  13.6 0.0 copy-done.2
  13.6 1.2 copy.33
  14.9 0.0 copy-done.4
  14.9 0.2 multiply_cosine_fusion
  15.1 0.6 pad_maximum_fusion.turns
  15.7 178.6 %shard_map.169 = (bf16[4,256,2048]{2,1,0:T(8,128)(2,1)}, bf16[1024,512]{1,0:T(8,128)(2,1)}, bf16[1024,512]{1,0:T(8,128)(2,1)}, bf16[1024,512]{1,0:T(8,128)(2,1)}...) custom-call(bf16[256,2048]{1,0:T(8,128)(2,1)} %tok.3, ...), custom_call_target="tpu_custom_call" | custom-call | flops 99999997952 | bytes 100000000 | tf_op jit(solution)/shard_map/pallas_call | solution.py:570
  194.3 173.1 %shard_map.170 = (f32[256,2048]{1,0:T(8,128)}, bf16[4,256,2048]{2,1,0:T(8,128)(2,1)}, bf16[4,2,256,1408]{3,2,1,0:T(8,128)(2,1)}, bf16[4,1408,256]{2,1,0:T(8,128)...) custom-call(bf16[256,2048]{1,0:T(8,128)(2,1)} %get-tuple-element.44., ...), custom_call_target="tpu_custom_call" | custom-call | flops 99999997952 | bytes 100000000 | tf_op jit(solution)/shard_map/pallas_call | solution.py:998
  367.4 0.0 reduce-scatter.2.cloned.1.call-update
  367.4 205.6 %shard_map.171 = (f32[256,2048]{1,0:T(8,128)}, f32[8,128]{1,0:T(8,128)}, bf16[4,2,256,1408]{3,2,1,0:T(8,128)(2,1)}, bf16[4,1408,256]{2,1,0:T(8,128)(2,1)}, bf16[...) custom-call(f32[256,2048]{1,0:T(8,128)} %get-tuple-element.49.gn2, ...), custom_call_target="tpu_custom_call", output_to_operand_aliasing={{4}: (11, {}), {5}: (12, {})} | custom-call | flops 99999997952 | bytes 100000000 | tf_op jit(solution)/shard_map/pallas_call | solution.py:1468
  573.1 1.3 slice.15
  574.3 6.7 %shard_map.172 = (f32[256,2,1408]{2,1,0:T(2,128)}, f32[1408,256]{1,0:T(8,128)}, f32[256,3,512]{2,1,0:T(4,128)}) custom-call(bf16[4,2,256,1408]{3,2,1,0:T(8,128)(2,1)} %get-tuple-element.67.refs_0_, bf16[4,2,256,1408]{3,2,1,0:T(8,128)(2,1)} %get-tuple-element.68.refs_1_.refs_2_, bf16[4,2,256,1408]{3,2,1,0:T(8,128)(2,1)} %get-tuple-element.68.refs_1_.refs_2_, ...), custom_call_target="tpu_custom_call" | custom-call | tf_op jit(solution)/shard_map/pallas_call | solution.py:1548
  581.0 0.0 copy-start.3
  581.0 0.0 copy-start.5
  581.0 0.0 copy-start
  581.1 3.4 copy.31
  584.4 0.0 copy-done.3
  584.4 0.9 convert_reduce_fusion
  585.4 0.0 copy-done.5
  585.4 0.6 fusion
  586.0 0.0 reduce-scatter.2.cloned.1.call-done
  586.0 0.0 copy-done
  586.0 0.0 copy-start.1
  586.0 2.6 add_convert_fusion
  588.6 0.0 copy-done.1
  588.6 1.3 copy.37
  (2 shorter events, 0.0 us)
Async XLA Ops:
  7.2 6.4 %copy-start.2 = (bf16[256,2,1408]{2,1,0:T(2,128)(2,1)S(1)}, bf16[256,2,1408]{2,1,0:T(2,128)(2,1)}, u32[]{:S(2)}) copy-start(bf16[256,2,1408]{2,1,0:T(2,128)(2,1)} %param.17) | copy-start | bytes 4325380
  7.2 578.8 %reduce-scatter.2.cloned.1.call-start = ((), (), s32[]{:S(2)}) async-start(), calls=%async_computation.1 | async-start | bytes 5242880 | tf_op jit(solution)/shard_map/reduce_scatter | solution.py:1571
  11.0 3.8 copy-start.4
  581.0 3.4 copy-start.3
  581.0 4.4 copy-start.5
  581.0 4.9 copy-start
  586.0 2.6 copy-start.1
Sparse Core Ops, SparseCore 0:
  367.6 111.6 reduce-scatter.1
